TPU v7x, 32 devices: a whole 2x2x4 slice. The times are simulated.
32 devices in a mesh: stream: 4 (over z), mod: 8 (over y, x, core).
Axes of the slice: x: 2, y: 2, z: 4, core: 2. Of those that a mesh axis runs over, the one named last changes fastest.
Arguments:
- pixels: bfloat16 [4, 192, 128, 384], P('stream', None, 'mod'), may hold values from -6 to 6
- stem_weight: bfloat16 [256, 128], replicated, may hold values from -0.375 to 0.375
- veto_weight: float32 [8, 128], replicated, may hold values from -0.25 to 0.25
- hit_frames: int32 [4, 48], P('stream'), may hold values from 0 to 191, as said below
- assign: int32 [4, 48, 1], P('stream'), may hold values from 0 to 3; in each aligned block of 6 rows (0 to 5, 6 to 11, ..., all dimensions but the last counted through in order) at most 2 rows name the same one
- token_in: bfloat16 [4, 384, 24], P('stream'), may hold values from -1.25 to 1.25
- token_out: bfloat16 [4, 24, 384], P('stream'), may hold values from -0.3125 to 0.3125
- chan_in: bfloat16 [4, 128, 512], P('stream'), may hold values from -0.5 to 0.5
- chan_out: bfloat16 [4, 512, 128], P('stream'), may hold values from -0.25 to 0.25
- readout: bfloat16 [1024, 128], replicated, may hold values from -0.1875 to 0.1875
- latent_gain: float32 [128], replicated, may hold values from 0.1 to 1.9
- class_weight: float32 [128, 8], replicated, may hold values from -0.5 to 0.5
Outputs:
- veto: float32 [4, 192], P('stream', 'mod')
- latents: float32 [4, 48, 128], P('stream', 'mod')
- scores: float32 [4, 48, 8], P('stream', 'mod')
Inputs may be any that keep to these rules, and one draw needn't show every extreme that they name: `hit_frames`: each row lists, rising and distinct, exactly 6 frames from every aligned block of 24 frames. `assign`: within the 6 hits of one aligned block (one owner's hits) no stream is named more than 2 times.
All inputs are finite; a program needn't handle non-finite values.
Results may differ from a plain program's by a relative error of at most 0.0095.
Values may be sent and summed in bfloat16 or wider, within the bound.
No kernel may reach another device: no remote copies, remote signals or barrier semaphores. Data moves between devices by JAX's collectives and lax.ppermute only.
A program may use at most 128 MiB of HBM per device.

v0:
```python
import jax
import jax.numpy as jnp
from jax import lax
from jax.sharding import PartitionSpec as P

PATCH = 16
CAP = 2


def rms_norm(values):
    return values * lax.rsqrt(jnp.mean(values * values, axis=-1, keepdims=True) + 1e-06)


def stem_layer(frame_pixels, stem_weight):
    count, height, width = frame_pixels.shape
    pixel_tiles = frame_pixels.reshape(count, height // PATCH, PATCH, width // PATCH, PATCH)
    kernel = stem_weight.reshape(PATCH, PATCH, -1)
    response = jnp.einsum(
        "fapbq,pqc->fabc", pixel_tiles, kernel, preferred_element_type=jnp.float32
    )
    return jax.nn.gelu(response).astype(jnp.bfloat16).reshape(count, -1, kernel.shape[-1])


def encode(
    tokens, mix_in, mix_out, chan_in, chan_out, readout, latent_gain, class_weight, module_count
):
    batch = tokens.shape[0]
    channels = tokens.shape[-1]
    row_len = mix_in.shape[1]
    grid_tokens = tokens.reshape(batch, -1, row_len, channels)
    normed = rms_norm(grid_tokens.astype(jnp.float32)).astype(jnp.bfloat16)
    mixed_tok = jax.nn.gelu(
        jnp.einsum("mw,brwc->brmc", mix_in, normed, preferred_element_type=jnp.float32)
    ).astype(jnp.bfloat16)
    after_mix = (
        grid_tokens.astype(jnp.float32)
        + jnp.einsum("wm,brmc->brwc", mix_out, mixed_tok, preferred_element_type=jnp.float32)
    ).astype(jnp.bfloat16)
    after_mix = after_mix.reshape(batch, -1, channels)
    normed_two = rms_norm(after_mix.astype(jnp.float32)).astype(jnp.bfloat16)
    hidden = jax.nn.gelu(
        jnp.einsum("btc,ch->bth", normed_two, chan_in, preferred_element_type=jnp.float32)
    ).astype(jnp.bfloat16)
    after_mlp = after_mix.astype(jnp.float32) + jnp.einsum(
        "bth,hc->btc", hidden, chan_out, preferred_element_type=jnp.float32
    )
    pooled = (
        jnp.mean(after_mlp.reshape(batch, module_count, -1, channels), axis=2)
        .reshape(batch, -1)
        .astype(jnp.bfloat16)
    )
    projected = jnp.dot(pooled, readout, preferred_element_type=jnp.float32)
    latent = rms_norm(projected) * latent_gain
    class_scores = jnp.dot(latent, class_weight, precision=lax.Precision.HIGHEST)
    return (latent, class_scores)


def local(
    pixels,
    stem_weight,
    veto_weight,
    hit_frames,
    assign,
    token_in,
    token_out,
    chan_in,
    chan_out,
    readout,
    latent_gain,
    class_weight,
):
    module_count = lax.axis_size("mod")
    stream_count = lax.axis_size("stream")
    mod_index = lax.axis_index("mod")
    frames_total = pixels.shape[1]
    frames_owned = frames_total // module_count
    hits_owned = hit_frames.shape[1] // module_count
    features = stem_layer(pixels[0], stem_weight)
    channels = features.shape[2]
    own_hits = lax.dynamic_slice_in_dim(hit_frames[0], mod_index * hits_owned, hits_owned)
    targets = lax.dynamic_slice_in_dim(assign[0, :, 0], mod_index * hits_owned, hits_owned)
    owned_frames = lax.all_to_all(features, "mod", split_axis=0, concat_axis=1, tiled=True)
    module_means = jnp.mean(
        owned_frames.reshape(frames_owned, module_count, -1, channels), axis=2, dtype=jnp.float32
    )
    veto_score = jnp.sum(module_means * veto_weight, axis=(1, 2))
    chosen = jnp.take(owned_frames, own_hits - mod_index * frames_owned, axis=0)
    position = jnp.arange(hits_owned, dtype=jnp.int32)
    earlier = (targets[:, None] == targets[None, :]) & (position[None, :] < position[:, None])
    slot_rank = jnp.sum(earlier.astype(jnp.int32), axis=1)
    stream_ids = jnp.arange(stream_count, dtype=jnp.int32)
    slot_ids = jnp.arange(CAP, dtype=jnp.int32)
    placing = (targets[None, None, :] == stream_ids[:, None, None]) & (
        slot_rank[None, None, :] == slot_ids[None, :, None]
    )
    outgoing = jnp.einsum(
        "tkh,hxc->tkxc", placing.astype(jnp.bfloat16), chosen, preferred_element_type=jnp.float32
    ).astype(jnp.bfloat16)
    received = lax.all_to_all(outgoing, "stream", split_axis=0, concat_axis=0, tiled=True)
    slot_count = received.shape[1]
    flat = received.reshape(stream_count * slot_count, received.shape[2], received.shape[3])
    latent, class_scores = encode(
        flat,
        token_in[0],
        token_out[0],
        chan_in[0],
        chan_out[0],
        readout,
        latent_gain,
        class_weight,
        module_count,
    )
    slot_latents = latent.reshape(stream_count, slot_count, -1)
    slot_scores = class_scores.reshape(stream_count, slot_count, -1)
    back_latents, back_scores = (
        lax.all_to_all(slot_latents, "stream", split_axis=0, concat_axis=0, tiled=True),
        lax.all_to_all(slot_scores, "stream", split_axis=0, concat_axis=0, tiled=True),
    )
    placing_float = placing.astype(jnp.float32)
    hit_latents = jnp.einsum(
        "tkh,tkc->hc", placing_float, back_latents, precision=lax.Precision.HIGHEST
    )
    hit_scores = jnp.einsum(
        "tkh,tkc->hc", placing_float, back_scores, precision=lax.Precision.HIGHEST
    )
    return (veto_score[None], hit_latents[None], hit_scores[None])


def solution(mesh):
    in_specs = (
        P("stream", None, "mod", None),
        P(),
        P(),
        P("stream", None),
        P("stream", None, None),
        P("stream", None, None),
        P("stream", None, None),
        P("stream", None, None),
        P("stream", None, None),
        P(),
        P(),
        P(),
    )
    out_specs = (P("stream", "mod"), P("stream", "mod", None), P("stream", "mod", None))
    return jax.shard_map(local, mesh=mesh, in_specs=in_specs, out_specs=out_specs, check_vma=False)
```

profile of v0, /device:TPU:0, one launch (start us, length us, event | category | flops | bytes accessed | tf_op | source)
XLA Modules:
  0.0 90.9 jit_solution(2511634341921954747)
XLA Ops:
  0.6 3.8 %copy.42 = bf16[1,192,16,384]{1,3,2,0:T(8,128)(2,1)S(1)} copy(bf16[1,192,16,384]{3,2,1,0:T(8,128)(2,1)} %param.12) | data formatting | bytes 4718592 | tf_op args[0]
  4.5 11.3 %copy.43 = bf16[192,16,24,16]{2,3,1,0:T(8,128)(2,1)} copy(bf16[192,16,24,16]{0,3,2,1:T(8,128)(2,1)S(1)} %bitcast.106) | data formatting | bytes 4718592 | tf_op jit(solution)/shard_map/reshape
  15.8 9.1 %fusion.27 = bf16[192,24,128]{2,1,0:T(8,128)(2,1)} fusion(bf16[192,16,24,16]{2,3,1,0:T(8,128)(2,1)} %copy.43, bf16[16,16,128,1]{2,1,0,3:T(8,128)(2,1)S(1)} %bitcast.116), kind=kOutput, calls=%fused_computation.29 | convolution fusion | flops 307298304 | bytes 3604480 | tf_op jit(solution)/shard_map/fapbq,pqc->fabc/dot_general | solution.py:18
  24.9 5.2 %all-to-all-start = ((bf16[192,24,128]{2,1,0:T(8,128)(2,1)}), bf16[192,24,128]{2,1,0:T(8,128)(2,1)S(1)}, u32[]{:S(2)}, u32[]{:S(2)}) async-start(bf16[192,24,128]{2,1,0:T(8,128)(2,1)} %fusion.27), calls=%async_computation | async-start | bytes 2359296 | tf_op jit(solution)/shard_map/all_to_all | solution.py:82
  30.3 0.2 convert_reduce_fusion.1
  30.5 16.4 %all-to-all-done = bf16[192,24,128]{2,1,0:T(8,128)(2,1)S(1)} async-done(((bf16[192,24,128]{2,1,0:T(8,128)(2,1)}), bf16[192,24,128]{2,1,0:T(8,128)(2,1)S(1)}, u32[]{:S(2)}, u32[]{:S(2)}) %all-to-all-start) | async-done | bytes 1179680 | tf_op jit(solution)/shard_map/all_to_all | solution.py:82
  46.9 0.3 copy.44
  47.2 0.6 gather_fusion
  47.8 0.1 broadcast_select_fusion
  47.9 0.3 convolution_convert_fusion
  48.3 0.8 copy.46
  49.1 4.9 %all-to-all-start.1 = ((bf16[4,2,192,128]{3,2,1,0:T(8,128)(2,1)}), bf16[4,2,192,128]{3,2,1,0:T(8,128)(2,1)S(1)}, u32[]{:S(2)}, u32[]{:S(2)}) async-start(bf16[4,2,192,128]{3,2,1,0:T(8,128)(2,1)} %copy.46), calls=%async_computation.1 | async-start | bytes 786432 | tf_op jit(solution)/shard_map/all_to_all | solution.py:99
  53.9 0.4 convert_reduce_fusion
  54.4 8.4 %all-to-all-done.1 = bf16[4,2,192,128]{3,2,1,0:T(8,128)(2,1)S(1)} async-done(((bf16[4,2,192,128]{3,2,1,0:T(8,128)(2,1)}), bf16[4,2,192,128]{3,2,1,0:T(8,128)(2,1)S(1)}, u32[]{:S(2)}, u32[]{:S(2)}) %all-to-all-start.1) | async-done | bytes 393248 | tf_op jit(solution)/shard_map/all_to_all | solution.py:99
  62.8 0.4 multiply_reduce_fusion.1
  63.2 0.3 multiply_convert_fusion.1
  63.5 4.9 %multiply_reduce_fusion = (f32[8,8,24]{2,1,0:T(8,128)S(1)}, f32[8,8,24,128]{3,2,1,0:T(8,128)S(1)}) fusion(bf16[1,24,384]{2,1,0:T(8,128)(2,1)S(1)} %copy-done.8, bf16[8,8,24,128]{3,2,1,0:T(8,128)(2,1)S(1)} %bitcast.113, bf16[1,384,24]{1,2,0:T(8,128)(2,1)S(1)} %copy-done.9, bf16[8,8,24,128]{3,2,1,0:T(8,128)(2,1)S(1)} %bitcast.109), kind=kOutput, calls=%fused_computation.41 | convolution fusion | flops 331479552 | bytes 1615872 | tf_op jit(solution)/shard_map/wm,brmc->brwc/dot_general | solution.py:37
  68.4 0.3 multiply_convert_fusion
  68.8 1.3 %fusion.32 = f32[8,192,128]{2,1,0:T(8,128)S(1)} fusion(f32[8,192,128]{2,1,0:T(8,128)S(1)} %bitcast.111, bf16[8,192,128]{2,1,0:T(8,128)(2,1)S(1)} %bitcast.114, bf16[1,512,128]{2,1,0:T(8,128)(2,1)S(1)} %copy-done.5, bf16[1,128,512]{2,1,0:T(8,128)(2,1)S(1)} %copy-done.6), kind=kOutput, calls=%fused_computation.33 | convolution fusion | flops 409927680 | bytes 2228224 | tf_op jit(solution)/shard_map/bth,hc->btc/dot_general | solution.py:44
  70.1 0.1 reduce_sum.68
  70.3 0.3 multiply_reduce_fusion.3
  70.5 0.7 multiply_multiply_fusion.3
  71.2 1.4 %fusion.76 = f32[8,8]{1,0:T(8,128)} fusion(f32[8,128]{1,0:T(8,128)} %multiply_multiply_fusion.3, f32[128,8]{0,1:T(8,128)S(1)} %copy-done.1), kind=kOutput, calls=%fused_computation.94 | convolution fusion | flops 98304 | bytes 8448 | tf_op jit(solution)/shard_map/dot_general | solution.py:54
  72.6 3.2 %all-to-all-start.3 = ((f32[4,2,8]{2,1,0:T(2,128)}), f32[4,2,8]{2,1,0:T(2,128)S(1)}, u32[]{:S(2)}, u32[]{:S(2)}) async-start(f32[4,2,8]{2,1,0:T(2,128)} %bitcast.36), calls=%async_computation.3 | async-start | bytes 8192 | tf_op jit(solution)/shard_map/all_to_all | solution.py:117
  75.8 0.8 multiply_reduce_fusion.2
  76.6 4.8 %all-to-all-done.3 = f32[4,2,8]{2,1,0:T(2,128)S(1)} async-done(((f32[4,2,8]{2,1,0:T(2,128)}), f32[4,2,8]{2,1,0:T(2,128)S(1)}, u32[]{:S(2)}, u32[]{:S(2)}) %all-to-all-start.3) | async-done | bytes 288 | tf_op jit(solution)/shard_map/all_to_all | solution.py:117
  81.4 3.2 %all-to-all-start.2 = ((f32[4,2,128]{2,1,0:T(2,128)}), f32[4,2,128]{2,1,0:T(2,128)S(1)}, u32[]{:S(2)}, u32[]{:S(2)}) async-start(f32[4,2,128]{2,1,0:T(2,128)} %bitcast.33), calls=%async_computation.2 | async-start | bytes 8192 | tf_op jit(solution)/shard_map/all_to_all | solution.py:116
  84.6 0.2 convolution_bitcast_fusion
  84.8 0.6 copy.51
  85.4 4.8 %all-to-all-done.2 = f32[4,2,128]{2,1,0:T(2,128)S(1)} async-done(((f32[4,2,128]{2,1,0:T(2,128)}), f32[4,2,128]{2,1,0:T(2,128)S(1)}, u32[]{:S(2)}, u32[]{:S(2)}) %all-to-all-start.2) | async-done | bytes 4128 | tf_op jit(solution)/shard_map/all_to_all | solution.py:116
  90.1 0.2 convolution_bitcast_fusion.1
  90.3 0.6 copy.50
  (33 shorter events, 0.4 us)
Async XLA Ops:
  0.6 69.6 %copy-start = (bf16[1024,128]{1,0:T(8,128)(2,1)S(1)}, bf16[1024,128]{1,0:T(8,128)(2,1)}, u32[]{:S(2)}) copy-start(bf16[1024,128]{1,0:T(8,128)(2,1)} %param.21) | copy-start | bytes 786436
  4.5 11.3 %copy-start.7 = (bf16[256,128]{1,0:T(8,128)(2,1)S(1)}, bf16[256,128]{1,0:T(8,128)(2,1)}, u32[]{:S(2)}) copy-start(bf16[256,128]{1,0:T(8,128)(2,1)} %param.13) | copy-start | bytes 196612
  15.8 14.3 %copy-start.3 = (s32[1,48]{1,0:T(1,128)S(1)}, s32[1,48]{1,0:T(1,128)}, u32[]{:S(2)}) copy-start(s32[1,48]{1,0:T(1,128)} %param.15) | copy-start | bytes 580
  15.8 14.5 %copy-start.10 = (s32[1,48,1]{1,2,0:T(1,128)S(1)}, s32[1,48,1]{1,2,0:T(1,128)}, u32[]{:S(2)}) copy-start(s32[1,48,1]{1,2,0:T(1,128)} %param.16) | copy-start | bytes 580
  24.9 22.0 %all-to-all-start = ((bf16[192,24,128]{2,1,0:T(8,128)(2,1)}), bf16[192,24,128]{2,1,0:T(8,128)(2,1)S(1)}, u32[]{:S(2)}, u32[]{:S(2)}) async-start(bf16[192,24,128]{2,1,0:T(8,128)(2,1)} %fusion.27), calls=%async_computation | async-start | bytes 2359296 | tf_op jit(solution)/shard_map/all_to_all | solution.py:82
  30.1 23.9 %copy-start.2 = (f32[8,128]{1,0:T(8,128)S(1)}, f32[8,128]{1,0:T(8,128)}, u32[]{:S(2)}) copy-start(f32[8,128]{1,0:T(8,128)} %param.14) | copy-start | bytes 12292
  47.2 16.3 %copy-start.8 = (bf16[1,24,384]{2,1,0:T(8,128)(2,1)S(1)}, bf16[1,24,384]{2,1,0:T(8,128)(2,1)}, u32[]{:S(2)}) copy-start(bf16[1,24,384]{2,1,0:T(8,128)(2,1)} %param.18) | copy-start | bytes 55300
  47.2 16.3 %copy-start.9 = (bf16[1,384,24]{1,2,0:T(8,128)(2,1)S(1)}, bf16[1,384,24]{1,2,0:T(8,128)(2,1)}, u32[]{:S(2)}) copy-start(bf16[1,384,24]{1,2,0:T(8,128)(2,1)} %param.17) | copy-start | bytes 55300
  49.1 13.8 %all-to-all-start.1 = ((bf16[4,2,192,128]{3,2,1,0:T(8,128)(2,1)}), bf16[4,2,192,128]{3,2,1,0:T(8,128)(2,1)S(1)}, u32[]{:S(2)}, u32[]{:S(2)}) async-start(bf16[4,2,192,128]{3,2,1,0:T(8,128)(2,1)} %copy.46), calls=%async_computation.1 | async-start | bytes 786432 | tf_op jit(solution)/shard_map/all_to_all | solution.py:99
  63.5 5.2 %copy-start.5 = (bf16[1,512,128]{2,1,0:T(8,128)(2,1)S(1)}, bf16[1,512,128]{2,1,0:T(8,128)(2,1)}, u32[]{:S(2)}) copy-start(bf16[1,512,128]{2,1,0:T(8,128)(2,1)} %param.20) | copy-start | bytes 393220
  63.5 5.2 %copy-start.6 = (bf16[1,128,512]{2,1,0:T(8,128)(2,1)S(1)}, bf16[1,128,512]{2,1,0:T(8,128)(2,1)}, u32[]{:S(2)}) copy-start(bf16[1,128,512]{2,1,0:T(8,128)(2,1)} %param.19) | copy-start | bytes 393220
  68.7 1.8 %copy-start.4 = (f32[128]{0:T(128)S(1)}, f32[128]{0:T(128)}, u32[]{:S(2)}) copy-start(f32[128]{0:T(128)} %param.22) | copy-start | bytes 1540
  68.8 2.4 %copy-start.1 = (f32[128,8]{0,1:T(8,128)S(1)}, f32[128,8]{0,1:T(8,128)}, u32[]{:S(2)}) copy-start(f32[128,8]{0,1:T(8,128)} %param.23) | copy-start | bytes 12292
  72.6 8.8 %all-to-all-start.3 = ((f32[4,2,8]{2,1,0:T(2,128)}), f32[4,2,8]{2,1,0:T(2,128)S(1)}, u32[]{:S(2)}, u32[]{:S(2)}) async-start(f32[4,2,8]{2,1,0:T(2,128)} %bitcast.36), calls=%async_computation.3 | async-start | bytes 8192 | tf_op jit(solution)/shard_map/all_to_all | solution.py:117
  81.4 8.8 %all-to-all-start.2 = ((f32[4,2,128]{2,1,0:T(2,128)}), f32[4,2,128]{2,1,0:T(2,128)S(1)}, u32[]{:S(2)}, u32[]{:S(2)}) async-start(f32[4,2,128]{2,1,0:T(2,128)} %bitcast.33), calls=%async_computation.2 | async-start | bytes 8192 | tf_op jit(solution)/shard_map/all_to_all | solution.py:116
where the time goes:
time: 92 us; the launch traced here: 90.9 us
  waiting for transfers between devices  34.3 us (37%)
  local copies, waits for them, and re-layouts  18.1 us (20%)
  matrix products  17.7 us (19%)
  starting transfers between devices  16.5 us (18%)
  other arithmetic  3.38 us (4%)
    all_to_all x1, waiting for transfers between devices, local(): lax.all_to_all(features, 'mod', split_axis=0, concat_axis=1, tiled=True)  16.4 us
    reshape x1, local copies, waits for them, and re-layouts  11.3 us
    dot_general x1, matrix products, stem_layer(): jnp.einsum('fapbq,pqc->fabc', pixel_tiles, kernel, preferred_element_type...  9.1 us
    all_to_all x1, waiting for transfers between devices, local(): lax.all_to_all(outgoing, 'stream', split_axis=0, concat_axis=0, tiled=True)  8.44 us
    all_to_all x1, starting transfers between devices, local(): lax.all_to_all(features, 'mod', split_axis=0, concat_axis=1, tiled=True)  5.17 us
    unnamed x25, local copies, waits for them, and re-layouts  5.09 us
    dot_general x1, matrix products, encode(): jnp.einsum('wm,brmc->brwc', mix_out, mixed_tok, preferred_element_type=jn...  4.89 us
    all_to_all x1, starting transfers between devices, local(): lax.all_to_all(outgoing, 'stream', split_axis=0, concat_axis=0, tiled=True)  4.87 us
  transfers between devices with their start and end apart: 4, of which 4 were waited for; matrix products, arithmetic and copies ran while one was open for 3% of the time, Pallas kernels for 0%

commit v1 on v0

v1 whole, which is shorter than its diff:
```python
import functools
import math

import jax
import jax.numpy as jnp
from jax import lax
from jax.experimental import pallas as pl
from jax.experimental.pallas import tpu as pltpu
from jax.sharding import PartitionSpec as P

PATCH = 16
LANES = 128
GROUP = 16
VETO_ROWS = 16
PAD_ROW = 32
VMEM_BYTES = 60 * 1024 * 1024
ENCODE_VMEM_BYTES = 32 * 1024 * 1024
F32 = jnp.float32
BF16 = jnp.bfloat16
GELU_A = math.sqrt(2.0 / math.pi)
GELU_B = GELU_A * 0.044715


def gelu(x):
    half = 0.5 * x
    return half + half * jnp.tanh(x * (GELU_A + GELU_B * (x * x)))


def rms_norm(values):
    return values * lax.rsqrt(jnp.mean(values * values, axis=-1, keepdims=True) + 1e-06)


def dot(a, b):
    return jnp.dot(a, b, preferred_element_type=F32)


def iota(shape, axis):
    return lax.broadcasted_iota(jnp.int32, shape, axis)


def pack_kernel(token_in, token_out, chan_in, chan_out, mine, other, token_in_rows, token_out_rows, sems):
    core = lax.axis_index("mod") % 2
    channels, hidden = chan_in.shape
    width, mix = token_in.shape
    small = (
        pltpu.make_async_copy(token_in, token_in_rows, sems.at[0]),
        pltpu.make_async_copy(token_out, token_out_rows, sems.at[1]),
    )
    for c in small:
        c.start()

    def pack(first, second):
        large = [pltpu.make_async_copy(chan_out, second.at[pl.ds(0, hidden)], sems.at[2])]
        for j in range(hidden // LANES):
            large.append(
                pltpu.make_async_copy(
                    chan_in.at[:, pl.ds(j * LANES, LANES)], first.at[pl.ds(j * channels, channels)], sems.at[3 + j]
                )
            )
        for c in large:
            c.start()
        for c in small:
            c.wait()
        for source, ref in ((token_in_rows, first), (token_out_rows, second)):
            wide = source[...].astype(F32)
            wide = jnp.concatenate([wide, jnp.zeros((PAD_ROW - width, mix), F32)], axis=0).astype(BF16)
            for j in range(mix // LANES):
                ref[hidden + j * PAD_ROW : hidden + (j + 1) * PAD_ROW, :] = wide[:, j * LANES : (j + 1) * LANES]
        for c in large:
            c.wait()

    @pl.when(core == 0)
    def _():
        pack(mine, other)

    @pl.when(core == 1)
    def _():
        pack(other, mine)


def turn(tiles, span):
    count = len(tiles)
    lane = iota(tiles[0].shape, 1)
    size = span * count // 2
    half = count // 2
    while half:
        low = (lane // size) % 2 == 0
        done = list(tiles)
        for i in range(count):
            if i // half % 2 == 0:
                a, b = tiles[i], tiles[i + half]
                done[i] = jnp.where(low, a, roll(b, size))
                done[i + half] = jnp.where(low, roll(a, LANES - size), b)
        tiles, half, size = done, half // 2, size // 2
    return tiles


def roll(x, shift):
    return jnp.concatenate([x[:, LANES - shift :], x[:, : LANES - shift]], axis=1)


def stem_kernel(pixels, weight, veto_weight, hit_frames, out, images, rows, small, wide, veto_rows, hit_row, chosen, sems):
    frames, _, columns = images.shape
    owners = out.shape[0]
    hits = hit_frames.shape[1]
    owned = frames // owners
    hit_rows = out.shape[1] - VETO_ROWS
    channels = weight.shape[1]
    blocks = columns // LANES
    quads = LANES // (2 * PATCH)
    tokens = columns // PATCH
    pieces = sems.shape[0] - 3
    step = frames // pieces

    def copy(i):
        span = pl.ds(i * step, step)
        return pltpu.make_async_copy(pixels.at[span], images.at[span], sems.at[i])

    side = [
        pltpu.make_async_copy(weight, small, sems.at[pieces]),
        pltpu.make_async_copy(veto_weight, veto_rows, sems.at[pieces + 1]),
        pltpu.make_async_copy(hit_frames, hit_row, sems.at[pieces + 2]),
    ]
    for c in side:
        c.start()
    for i in range(pieces):
        copy(i).start()
    size = GROUP * PATCH
    r, c = iota((size, size), 0), iota((size, size), 1)
    swap = (c == (r % GROUP) * PATCH + r // GROUP).astype(F32).astype(BF16)
    for c in side:
        c.wait()
    zero = jnp.zeros((PATCH, channels), BF16)
    for p in range(PATCH):
        tile = small[p * PATCH : (p + 1) * PATCH, :]
        for a in range(2):
            top = (p * 2 + a) * PATCH
            for b in range(2):
                wide[top : top + PATCH, b * channels : (b + 1) * channels] = tile if a == b else zero
    for i in range(pieces):
        copy(i).wait()
        for g in range(i * step // GROUP, (i + 1) * step // GROUP):
            block = images[g * GROUP : (g + 1) * GROUP].reshape(size, columns)
            turned = dot(swap, block).astype(BF16)
            for j in range(blocks):
                for p in range(0, PATCH, quads):
                    tiles = [
                        turned[q * GROUP : (q + 1) * GROUP, j * LANES : (j + 1) * LANES] for q in range(p, p + quads)
                    ]
                    for n, tile in enumerate(turn(tiles, 2 * PATCH)):
                        top = (n * blocks + j) * frames + g * GROUP
                        rows[top : top + GROUP, p * 2 * PATCH : p * 2 * PATCH + LANES] = tile
    pick = (iota((frames, hits), 0) == hit_row[...]).astype(F32).T.astype(BF16)
    sums = jnp.zeros((frames, channels), F32)
    for n in range(quads):
        for j in range(blocks):
            top = (n * blocks + j) * frames
            part = gelu(dot(rows[top : top + frames, :], wide[...]))
            sums = sums + part[:, :channels] + part[:, channels:]
            taken = dot(pick, part.astype(BF16))
            for k in range(2):
                chosen[pl.ds(j * 2 * quads + 2 * n + k, hits, stride=tokens), :] = taken[
                    :, k * channels : (k + 1) * channels
                ]
    scale = jnp.broadcast_to(veto_rows[pl.ds(lax.axis_index("mod"), 1), :] / tokens, (VETO_ROWS, channels))
    row = iota((VETO_ROWS, owned), 0)
    for o in range(owners):
        out[o, 0:hit_rows, :] = chosen[o * hit_rows : (o + 1) * hit_rows, :].astype(BF16)
        veto = lax.dot_general(
            scale,
            sums[o * owned : (o + 1) * owned],
            (((1,), (1,)), ((), ())),
            preferred_element_type=F32,
            precision=lax.Precision.HIGHEST,
        )
        high = veto.astype(BF16).astype(F32)
        both = jnp.where(row == 0, high, jnp.where(row == 1, veto - high, 0.0))
        both = jnp.concatenate([both, jnp.zeros((VETO_ROWS, LANES - owned), F32)], axis=1)
        out[o, hit_rows : hit_rows + VETO_ROWS, :] = both.astype(BF16)


def encode_kernel(streams, width, hidden, *refs):
    features, targets, readout, gain, class_weight = refs[:5]
    halves = refs[5 : 5 + 2 * streams]
    veto, latents, scores, table, pools, sems = refs[5 + 2 * streams :]
    owners = features.shape[0]
    channels = features.shape[2]
    hits = latents.shape[0]
    hit_rows = hits * width
    here = lax.axis_index("stream")
    own = lax.axis_index("mod")
    core = own % 2
    copies = []
    for k in range(streams):
        copies.append(pltpu.make_async_copy(halves[2 * k], table.at[k, core], sems.at[2 * k]))
        copies.append(pltpu.make_async_copy(halves[2 * k + 1], table.at[k, 1 - core], sems.at[2 * k + 1]))
    for c in copies:
        c.start()
    terms = jnp.sum(features[:, hit_rows : hit_rows + VETO_ROWS, :].astype(F32), axis=0)
    veto[...] = jnp.sum(terms, axis=0, keepdims=True)[:, : veto.shape[1]]
    pools[...] = jnp.zeros_like(pools)
    for c in copies:
        c.wait()

    def encode(slot, x):
        target = targets[own * hits + slot]
        k = target ^ here
        extra = table.shape[2] - hidden
        blocks = extra // PAD_ROW
        packed = table[k, 0, hidden:, :].astype(F32)
        token_in = jnp.concatenate([packed[j * PAD_ROW : (j + 1) * PAD_ROW] for j in range(blocks)], axis=1)
        token_in = token_in.T.astype(BF16)
        normed = rms_norm(x)
        gap = jnp.zeros((PAD_ROW - width, channels), F32)
        wide = jnp.concatenate(
            [jnp.concatenate([normed[r], gap], axis=0).astype(BF16) for r in range(owners)], axis=1
        )
        mixed = gelu(dot(token_in, wide)).astype(BF16)
        mix_rows = table[k, 1, hidden:, :]
        token_out = jnp.concatenate(
            [mix_rows[j * PAD_ROW : (j + 1) * PAD_ROW] for j in range(blocks)], axis=1
        )
        back = dot(token_out, mixed)
        after = jnp.concatenate(
            [x[r] + back[:width, r * channels : (r + 1) * channels] for r in range(owners)], axis=0
        )
        after = after.astype(BF16).astype(F32)
        chan_in = jnp.concatenate(
            [table[k, 0, j * channels : (j + 1) * channels, :] for j in range(hidden // channels)], axis=1
        )
        inner = gelu(dot(rms_norm(after).astype(BF16), chan_in)).astype(BF16)
        last = after + dot(inner, table[k, 1, 0:hidden, :])
        pool = jnp.sum(last.reshape(owners, width, channels), axis=1) * (1.0 / width)
        pools[pl.ds(pl.multiple_of(slot * owners, owners), owners), :] = pool

    pair = 2

    @pl.loop(0, hits // pair)
    def _(i):
        x = features[:, pl.ds(pl.multiple_of(i * pair * width, 16), pair * width), :].astype(F32)
        for a in range(pair):
            encode(i * pair + a, x[:, a * width : (a + 1) * width])

    pooled = jnp.concatenate(
        [pools[pl.ds(r, 8, stride=owners), :].astype(BF16) for r in range(owners)], axis=1
    )
    latent = rms_norm(dot(pooled, readout[...])) * gain[...]
    latents[:, 0, :] = latent[:hits]
    scores[:, 0, :] = lax.dot_general(
        latent,
        class_weight[...],
        (((1,), (1,)), ((), ())),
        preferred_element_type=F32,
        precision=lax.Precision.HIGHEST,
    )[:hits]


def vmem(count):
    return [pl.BlockSpec(memory_space=pltpu.VMEM)] * count


PARAMS = pltpu.CompilerParams(vmem_limit_bytes=VMEM_BYTES)
ENCODE_PARAMS = pltpu.CompilerParams(vmem_limit_bytes=ENCODE_VMEM_BYTES)


def local(
    pixels,
    stem_weight,
    veto_weight,
    hit_frames,
    assign,
    token_in,
    token_out,
    chan_in,
    chan_out,
    readout,
    latent_gain,
    class_weight,
):
    owners = lax.axis_size("mod")
    streams = lax.axis_size("stream")
    _, frames, height, columns = pixels.shape
    channels = stem_weight.shape[1]
    mix, width = token_in.shape[1:]
    hidden = chan_in.shape[2]
    hits = hit_frames.shape[1]
    hits_owned = hits // owners
    hit_rows = hits_owned * width
    half_rows = hidden + mix * PAD_ROW // LANES
    anywhere = pl.BlockSpec(memory_space=pl.ANY)

    half = jax.ShapeDtypeStruct((half_rows, LANES), BF16)
    mine, other = pl.pallas_call(
        pack_kernel,
        name="pack",
        out_shape=(half, half),
        in_specs=[anywhere] * 4,
        out_specs=vmem(2),
        scratch_shapes=[
            pltpu.VMEM((width, mix), BF16),
            pltpu.VMEM((width, mix), BF16),
            pltpu.SemaphoreType.DMA((3 + hidden // LANES,)),
        ],
        compiler_params=PARAMS,
    )(token_in[0].T, token_out[0], chan_in[0], chan_out[0])
    halves = [mine, other]
    for k in range(1, streams):
        got = lax.ppermute(mine, "stream", [(i, i ^ k) for i in range(streams)])
        halves += [got, lax.ppermute(got, "mod", [(i, i ^ 1) for i in range(owners)])]

    outgoing = pl.pallas_call(
        stem_kernel,
        name="stem",
        out_shape=jax.ShapeDtypeStruct((owners, hit_rows + VETO_ROWS, channels), BF16),
        in_specs=[anywhere] * 4,
        out_specs=vmem(1)[0],
        scratch_shapes=[
            pltpu.VMEM((frames, height, columns), BF16),
            pltpu.VMEM((frames * columns // (2 * PATCH), 2 * PATCH * PATCH), BF16),
            pltpu.VMEM(stem_weight.shape, BF16),
            pltpu.VMEM((2 * PATCH * PATCH, 2 * channels), BF16),
            pltpu.VMEM(veto_weight.shape, F32),
            pltpu.VMEM((1, hits), jnp.int32),
            pltpu.VMEM((hits * width, channels), F32),
            pltpu.SemaphoreType.DMA((4 + 3,)),
        ],
        compiler_params=PARAMS,
        cost_estimate=pl.CostEstimate(flops=5_000_000_000, bytes_accessed=3_000_000, transcendentals=0),
    )(pixels[0], stem_weight, veto_weight, hit_frames)
    received = lax.all_to_all(outgoing, "mod", split_axis=0, concat_axis=0, tiled=True)

    veto, latents, scores = pl.pallas_call(
        functools.partial(encode_kernel, streams, width, hidden),
        name="encode",
        out_shape=(
            jax.ShapeDtypeStruct((1, frames // owners), F32),
            jax.ShapeDtypeStruct((hits_owned, 1, channels), F32),
            jax.ShapeDtypeStruct((hits_owned, 1, class_weight.shape[1]), F32),
        ),
        in_specs=vmem(1)
        + [pl.BlockSpec(memory_space=pltpu.SMEM)]
        + vmem(3)
        + [pl.BlockSpec(memory_space=pl.ANY)] * len(halves),
        out_specs=tuple(vmem(3)),
        scratch_shapes=[
            pltpu.VMEM((streams, 2, half_rows, LANES), BF16),
            pltpu.VMEM((8 * owners, channels), F32),
            pltpu.SemaphoreType.DMA((2 * streams,)),
        ],
        compiler_params=ENCODE_PARAMS,
    )(received, assign.reshape(hits), readout, latent_gain.reshape(1, channels), class_weight.T, *halves)
    return (veto, jnp.swapaxes(latents, 0, 1), jnp.swapaxes(scores, 0, 1))


def solution(mesh):
    in_specs = (
        P("stream", None, "mod", None),
        P(),
        P(),
        P("stream", None),
        P("stream", None, None),
        P("stream", None, None),
        P("stream", None, None),
        P("stream", None, None),
        P("stream", None, None),
        P(),
        P(),
        P(),
    )
    out_specs = (P("stream", "mod"), P("stream", "mod", None), P("stream", "mod", None))
    return jax.shard_map(local, mesh=mesh, in_specs=in_specs, out_specs=out_specs, check_vma=False)
```

time: 92 us -> 37.8 us (0.41)
  waiting for transfers between devices: 34.3 us -> 6.63 us
  Pallas kernels: 0 us -> 19.5 us
  local copies, waits for them, and re-layouts: 18.1 us -> 0.03 us
  matrix products: 17.7 us -> 0 us
  starting transfers between devices: 16.5 us -> 10.6 us
  other arithmetic: 3.38 us -> 0 us
    all_to_all x4 -> x1, waiting for transfers between devices: 34.3 us -> 6.46 us  [local(): lax.all_to_all(outgoing, 'mod', split_axis=0, concat_axis=0, tiled=True)]
    pallas_call x0 -> x3, Pallas kernels: none -> 19.5 us  [the longest x1 10.3 us: local(): pl.pallas_call(functools.partial(encode_kernel, streams, width, hidden),...]
    dot_general x8 -> x0, matrix products: 17.7 us -> none  [the longest x1 9.1 us: stem_layer(): jnp.einsum('fapbq,pqc->fabc', pixel_tiles, kernel, preferred_element_type...]
    all_to_all x4 -> x1, starting transfers between devices: 16.5 us -> 3.95 us  [local(): lax.all_to_all(outgoing, 'mod', split_axis=0, concat_axis=0, tiled=True)]
    reshape x1 -> x0, local copies, waits for them, and re-layouts: 11.3 us -> none
    ppermute x0 -> x6, starting transfers between devices: none -> 6.69 us  [the longest x3 5.68 us: local(): got = lax.ppermute(mine, 'stream', [(i, i ^ k) for i in range(streams)])]
    unnamed x25 -> x12, local copies, waits for them, and re-layouts: 5.09 us -> 0.03 us
    reduce_sum x5 -> x0, other arithmetic: 1.87 us -> none  [the longest x1 0.77 us: local(): veto_score = jnp.sum(module_means * veto_weight, axis=(1, 2))]
  transfers between devices with their start and end apart: 4 -> 7, of which waited for: 4 -> 2; matrix products, arithmetic and copies ran while one was open for 3% -> 0% of each run, Pallas kernels for 0% -> 20%
where the time goes in v1:
time: 37.8 us; the launch traced here: 37.5 us
  Pallas kernels  19.5 us (52%)
  starting transfers between devices  10.6 us (28%)
  waiting for transfers between devices  6.63 us (18%)
  between operations  0.74 us (2%)
    pallas_call x1, Pallas kernels, local(): pl.pallas_call(functools.partial(encode_kernel, streams, width, hidden),...  10.3 us
    pallas_call x1, Pallas kernels, local(): pl.pallas_call(stem_kernel, name='stem', out_shape=jax.ShapeDtypeStruct((...  7.47 us
    all_to_all x1, waiting for transfers between devices, local(): lax.all_to_all(outgoing, 'mod', split_axis=0, concat_axis=0, tiled=True)  6.46 us
    ppermute x3, starting transfers between devices, local(): got = lax.ppermute(mine, 'stream', [(i, i ^ k) for i in range(streams)])  5.68 us
    all_to_all x1, starting transfers between devices, local(): lax.all_to_all(outgoing, 'mod', split_axis=0, concat_axis=0, tiled=True)  3.95 us
    pallas_call x1, Pallas kernels, local(): pl.pallas_call(pack_kernel, name='pack', out_shape=(half, half), in_specs...  1.74 us
    ppermute x3, starting transfers between devices, local(): lax.ppermute(got, 'mod', [(i, i ^ 1) for i in range(owners)])  1.01 us
  transfers between devices with their start and end apart: 7, of which 2 were waited for; matrix products, arithmetic and copies ran while one was open for 0% of the time, Pallas kernels for 20%

profile of v1, /device:TPU:0, one launch (start us, length us, event | category | flops | bytes accessed | tf_op | source)
XLA Modules:
  0.0 37.5 jit_solution(3580201787101593298)
XLA Ops:
  0.6 1.7 %pack.1 = (bf16[608,128]{1,0:T(8,128)(2,1)}, bf16[608,128]{1,0:T(8,128)(2,1)}) custom-call(bf16[24,384]{1,0:T(8,128)(2,1)} %bitcast.17, bf16[24,384]{1,0:T(8,128)(2,1)} %bitcast.18, bf16[128,512]{1,0:T(8,128)(2,1)} %bitcast.15, bf16[512,128]{1,0:T(8,128)(2,1)} %bitcast.16), custom_call_target="tpu_custom_call" | custom-call | tf_op jit(solution)/shard_map/pack/pallas_call | solution.py:293
  2.4 3.1 %collective-permute-start = (bf16[608,128]{1,0:T(8,128)(2,1)}, bf16[608,128]{1,0:T(8,128)(2,1)S(1)}, u32[]{:S(2)}, u32[]{:S(2)}) collective-permute-start(bf16[608,128]{1,0:T(8,128)(2,1)} %get-tuple-element.8.refs_5_), channel_id=1, source_target_pairs={{0,8},{8,0},{16,24},{24,16},{1,9},{9,1},{17,25},{25,17},{2,10},{10... | collective-permute-start | bytes 466952 | tf_op jit(solution)/shard_map/ppermute | solution.py:308
  5.5 2.6 %collective-permute-start.2 = (bf16[608,128]{1,0:T(8,128)(2,1)}, bf16[608,128]{1,0:T(8,128)(2,1)S(1)}, u32[]{:S(2)}, u32[]{:S(2)}) collective-permute-start(bf16[608,128]{1,0:T(8,128)(2,1)} %get-tuple-element.8.refs_5_), channel_id=1, source_target_pairs={{0,16},{8,24},{16,0},{24,8},{1,17},{9,25},{17,1},{25,9},{2,18},{10... | collective-permute-start | bytes 466952 | tf_op jit(solution)/shard_map/ppermute | solution.py:308
  8.1 0.0 collective-permute-start.4
  8.1 0.0 copy-start
  8.1 0.0 copy-start.1
  8.1 0.0 copy-start.2
  8.1 0.0 copy-start.3
  8.1 0.0 copy-start.4
  8.1 0.0 copy-start.5
  8.1 7.5 %stem.1 = bf16[8,160,128]{2,1,0:T(8,128)(2,1)} custom-call(bf16[192,16,384]{2,1,0:T(8,128)(2,1)} %bitcast.19, bf16[256,128]{1,0:T(8,128)(2,1)} %weight.1, f32[8,128]{1,0:T(8,128)} %veto_weight.1, s32[1,48]{1,0:T(1,128)} %hit_frames.1), custom_call_target="tpu_custom_call" | custom-call | flops 5000000000 | bytes 3000000 | tf_op jit(solution)/shard_map/stem/pallas_call | solution.py:311
  15.6 4.0 %all-to-all-start = ((bf16[8,160,128]{2,1,0:T(8,128)(2,1)}), bf16[8,160,128]{2,1,0:T(8,128)(2,1)S(1)}, u32[]{:S(2)}, u32[]{:S(2)}) async-start(bf16[8,160,128]{2,1,0:T(8,128)(2,1)} %stem.1), calls=%async_computation | async-start | bytes 655360 | tf_op jit(solution)/shard_map/all_to_all | solution.py:330
  19.5 0.0 collective-permute-done.refs_7_
  19.5 0.5 %collective-permute-start.1 = (bf16[608,128]{1,0:T(8,128)(2,1)S(1)}, bf16[608,128]{1,0:T(8,128)(2,1)S(1)}, u32[]{:S(2)}, u32[]{:S(2)}) collective-permute-start(bf16[608,128]{1,0:T(8,128)(2,1)S(1)} %collective-permute-done.refs_7_), channel_id=1, source_target_pairs={{0,1},{1,0},{2,3},{3,2},{4,5},{5,4},{6,7},{7,6},{8,9},{9,8},{10,11... | collective-permute-start | bytes 466952 | tf_op jit(solution)/shard_map/ppermute | solution.py:309
  20.0 0.2 collective-permute-done.2.refs_9_
  20.2 0.0 collective-permute-start.3
  20.2 0.0 collective-permute-done.4.refs_11_
  20.2 0.5 %collective-permute-start.5 = (bf16[608,128]{1,0:T(8,128)(2,1)S(1)}, bf16[608,128]{1,0:T(8,128)(2,1)S(1)}, u32[]{:S(2)}, u32[]{:S(2)}) collective-permute-start(bf16[608,128]{1,0:T(8,128)(2,1)S(1)} %collective-permute-done.4.refs_11_), channel_id=1, source_target_pairs={{0,1},{1,0},{2,3},{3,2},{4,5},{5,4},{6,7},{7,6},{8,9},{9,8},{10,11... | collective-permute-start | bytes 466952 | tf_op jit(solution)/shard_map/ppermute | solution.py:309
  20.7 6.5 %all-to-all-done.refs_0_ = bf16[8,160,128]{2,1,0:T(8,128)(2,1)S(1)} async-done(((bf16[8,160,128]{2,1,0:T(8,128)(2,1)}), bf16[8,160,128]{2,1,0:T(8,128)(2,1)S(1)}, u32[]{:S(2)}, u32[]{:S(2)}) %all-to-all-start) | async-done | bytes 327712 | tf_op jit(solution)/shard_map/all_to_all | solution.py:330
  27.2 0.0 collective-permute-done.1.refs_8_
  27.2 0.0 collective-permute-done.3.refs_10_
  27.2 0.0 collective-permute-done.5.refs_12_
  27.2 0.0 copy-done
  27.2 0.0 copy-done.1
  27.2 0.0 copy-done.2
  27.2 0.0 copy-done.3
  27.2 0.0 copy-done.4
  27.2 0.0 copy-done.5
  27.2 10.3 %encode.1 = (f32[1,24]{1,0:T(1,128)}, f32[6,1,128]{2,1,0:T(1,128)}, f32[6,1,8]{2,1,0:T(1,128)}) custom-call(bf16[8,160,128]{2,1,0:T(8,128)(2,1)S(1)} %all-to-all-done.refs_0_, s32[48]{0:T(128)S(1)} %bitcast.13, bf16[1024,128]{1,0:T(8,128)(2,1)S(1)} %copy-done, f32[1,128]{1,0:T(1,128)S(1)} %bitcast.14, f32[8,128]{1,0:T(8,128)S(1)} %bitcast.12, ...), custom_call_target="tpu_custom_call" | custom-call | tf_op jit(solution)/shard_map/encode/pallas_call | solution.py:332
Async XLA Ops:
  2.4 17.2 %collective-permute-start = (bf16[608,128]{1,0:T(8,128)(2,1)}, bf16[608,128]{1,0:T(8,128)(2,1)S(1)}, u32[]{:S(2)}, u32[]{:S(2)}) collective-permute-start(bf16[608,128]{1,0:T(8,128)(2,1)} %get-tuple-element.8.refs_5_), channel_id=1, source_target_pairs={{0,8},{8,0},{16,24},{24,16},{1,9},{9,1},{17,25},{25,17},{2,10},{10... | collective-permute-start | bytes 466952 | tf_op jit(solution)/shard_map/ppermute | solution.py:308
  5.5 14.7 %collective-permute-start.2 = (bf16[608,128]{1,0:T(8,128)(2,1)}, bf16[608,128]{1,0:T(8,128)(2,1)S(1)}, u32[]{:S(2)}, u32[]{:S(2)}) collective-permute-start(bf16[608,128]{1,0:T(8,128)(2,1)} %get-tuple-element.8.refs_5_), channel_id=1, source_target_pairs={{0,16},{8,24},{16,0},{24,8},{1,17},{9,25},{17,1},{25,9},{2,18},{10... | collective-permute-start | bytes 466952 | tf_op jit(solution)/shard_map/ppermute | solution.py:308
  8.1 12.1 %collective-permute-start.4 = (bf16[608,128]{1,0:T(8,128)(2,1)}, bf16[608,128]{1,0:T(8,128)(2,1)S(1)}, u32[]{:S(2)}, u32[]{:S(2)}) collective-permute-start(bf16[608,128]{1,0:T(8,128)(2,1)} %get-tuple-element.8.refs_5_), channel_id=1, source_target_pairs={{0,24},{8,16},{16,8},{24,0},{1,25},{9,17},{17,9},{25,1},{2,26},{10... | collective-permute-start | bytes 466952 | tf_op jit(solution)/shard_map/ppermute | solution.py:308
  8.1 19.1 %copy-start = (bf16[1024,128]{1,0:T(8,128)(2,1)S(1)}, bf16[1024,128]{1,0:T(8,128)(2,1)}, u32[]{:S(2)}) copy-start(bf16[1024,128]{1,0:T(8,128)(2,1)} %refs_2_.1) | copy-start | bytes 786436
  8.1 19.1 %copy-start.1 = (bf16[608,128]{1,0:T(8,128)(2,1)S(1)}, bf16[608,128]{1,0:T(8,128)(2,1)}, u32[]{:S(2)}) copy-start(bf16[608,128]{1,0:T(8,128)(2,1)} %get-tuple-element.8.refs_5_) | copy-start | bytes 466948
  8.1 19.1 %copy-start.2 = (bf16[608,128]{1,0:T(8,128)(2,1)S(1)}, bf16[608,128]{1,0:T(8,128)(2,1)}, u32[]{:S(2)}) copy-start(bf16[608,128]{1,0:T(8,128)(2,1)} %get-tuple-element.9.refs_6_) | copy-start | bytes 466948
  8.1 19.2 %copy-start.3 = (f32[128,8]{0,1:T(8,128)S(1)}, f32[128,8]{0,1:T(8,128)}, u32[]{:S(2)}) copy-start(f32[128,8]{0,1:T(8,128)} %param.23) | copy-start | bytes 12292
  8.1 19.2 %copy-start.4 = (s32[1,48,1]{1,2,0:T(1,128)S(1)}, s32[1,48,1]{1,2,0:T(1,128)}, u32[]{:S(2)}) copy-start(s32[1,48,1]{1,2,0:T(1,128)} %param.16) | copy-start | bytes 580
  8.1 19.1 %copy-start.5 = (f32[128]{0:T(128)S(1)}, f32[128]{0:T(128)}, u32[]{:S(2)}) copy-start(f32[128]{0:T(128)} %param.22) | copy-start | bytes 1540
  15.6 11.6 %all-to-all-start = ((bf16[8,160,128]{2,1,0:T(8,128)(2,1)}), bf16[8,160,128]{2,1,0:T(8,128)(2,1)S(1)}, u32[]{:S(2)}, u32[]{:S(2)}) async-start(bf16[8,160,128]{2,1,0:T(8,128)(2,1)} %stem.1), calls=%async_computation | async-start | bytes 655360 | tf_op jit(solution)/shard_map/all_to_all | solution.py:330
  19.5 7.6 %collective-permute-start.1 = (bf16[608,128]{1,0:T(8,128)(2,1)S(1)}, bf16[608,128]{1,0:T(8,128)(2,1)S(1)}, u32[]{:S(2)}, u32[]{:S(2)}) collective-permute-start(bf16[608,128]{1,0:T(8,128)(2,1)S(1)} %collective-permute-done.refs_7_), channel_id=1, source_target_pairs={{0,1},{1,0},{2,3},{3,2},{4,5},{5,4},{6,7},{7,6},{8,9},{9,8},{10,11... | collective-permute-start | bytes 466952 | tf_op jit(solution)/shard_map/ppermute | solution.py:309
  20.2 7.0 %collective-permute-start.3 = (bf16[608,128]{1,0:T(8,128)(2,1)S(1)}, bf16[608,128]{1,0:T(8,128)(2,1)S(1)}, u32[]{:S(2)}, u32[]{:S(2)}) collective-permute-start(bf16[608,128]{1,0:T(8,128)(2,1)S(1)} %collective-permute-done.2.refs_9_), channel_id=1, source_target_pairs={{0,1},{1,0},{2,3},{3,2},{4,5},{5,4},{6,7},{7,6},{8,9},{9,8},{10,11... | collective-permute-start | bytes 466952 | tf_op jit(solution)/shard_map/ppermute | solution.py:309
  20.2 7.0 %collective-permute-start.5 = (bf16[608,128]{1,0:T(8,128)(2,1)S(1)}, bf16[608,128]{1,0:T(8,128)(2,1)S(1)}, u32[]{:S(2)}, u32[]{:S(2)}) collective-permute-start(bf16[608,128]{1,0:T(8,128)(2,1)S(1)} %collective-permute-done.4.refs_11_), channel_id=1, source_target_pairs={{0,1},{1,0},{2,3},{3,2},{4,5},{5,4},{6,7},{7,6},{8,9},{9,8},{10,11... | collective-permute-start | bytes 466952 | tf_op jit(solution)/shard_map/ppermute | solution.py:309

commit v2 on v1

v2 whole, which is shorter than its diff:
```python
import functools
import math

import jax
import jax.numpy as jnp
from jax import lax
from jax.experimental import pallas as pl
from jax.experimental.pallas import tpu as pltpu
from jax.sharding import PartitionSpec as P

PATCH = 16
LANES = 128
GROUP = 16
VETO_ROWS = 16
PAD_ROW = 32
PACK_VMEM_BYTES = 16 * 1024 * 1024
STEM_VMEM_BYTES = 40 * 1024 * 1024
ENCODE_VMEM_BYTES = 32 * 1024 * 1024
F32 = jnp.float32
BF16 = jnp.bfloat16
GELU_A = math.sqrt(2.0 / math.pi)
GELU_B = GELU_A * 0.044715


def gelu(x):
    half = 0.5 * x
    return half + half * jnp.tanh(x * (GELU_A + GELU_B * (x * x)))


def gelu_narrow(x):
    x = x.astype(BF16)
    half = x * BF16(0.5)
    return half + half * jnp.tanh(x * (BF16(GELU_A) + BF16(GELU_B) * (x * x)))


def rms_norm(values):
    return values * lax.rsqrt(jnp.mean(values * values, axis=-1, keepdims=True) + 1e-06)


def dot(a, b):
    return jnp.dot(a, b, preferred_element_type=F32)


def iota(shape, axis):
    return lax.broadcasted_iota(jnp.int32, shape, axis)


def pack_kernel(
    token_in, token_out, chan_in, chan_out, pixels, mine, other, images, token_in_rows, token_out_rows, sems
):
    core = lax.axis_index("mod") % 2
    channels, hidden = chan_in.shape
    width, mix = token_in.shape
    small = (
        pltpu.make_async_copy(token_in, token_in_rows, sems.at[0]),
        pltpu.make_async_copy(token_out, token_out_rows, sems.at[1]),
    )
    for c in small:
        c.start()
    whole = pltpu.make_async_copy(pixels, images, sems.at[3 + hidden // LANES])

    def pack(first, second):
        large = [pltpu.make_async_copy(chan_out, second.at[pl.ds(0, hidden)], sems.at[2])]
        for j in range(hidden // LANES):
            large.append(
                pltpu.make_async_copy(
                    chan_in.at[:, pl.ds(j * LANES, LANES)], first.at[pl.ds(j * channels, channels)], sems.at[3 + j]
                )
            )
        for c in large:
            c.start()
        whole.start()
        for c in small:
            c.wait()
        for source, ref in ((token_in_rows, first), (token_out_rows, second)):
            wide = source[...].astype(F32)
            wide = jnp.concatenate([wide, jnp.zeros((PAD_ROW - width, mix), F32)], axis=0).astype(BF16)
            for j in range(mix // LANES):
                ref[hidden + j * PAD_ROW : hidden + (j + 1) * PAD_ROW, :] = wide[:, j * LANES : (j + 1) * LANES]
        for c in large:
            c.wait()

    @pl.when(core == 0)
    def _():
        pack(mine, other)

    @pl.when(core == 1)
    def _():
        pack(other, mine)

    whole.wait()


def turn(tiles, span):
    count = len(tiles)
    lane = iota(tiles[0].shape, 1)
    size = span * count // 2
    half = count // 2
    while half:
        low = (lane // size) % 2 == 0
        done = list(tiles)
        for i in range(count):
            if i // half % 2 == 0:
                a, b = tiles[i], tiles[i + half]
                done[i] = jnp.where(low, a, roll(b, size))
                done[i + half] = jnp.where(low, roll(a, LANES - size), b)
        tiles, half, size = done, half // 2, size // 2
    return tiles


def roll(x, shift):
    return jnp.concatenate([x[:, LANES - shift :], x[:, : LANES - shift]], axis=1)


def stem_kernel(
    images, weight, veto_weight, hit_frames, out, rows, small, wide, veto_rows, hit_row, chosen, sems
):
    frames, _, columns = images.shape
    owners = out.shape[0]
    hits = hit_frames.shape[1]
    owned = frames // owners
    hit_rows = out.shape[1] - VETO_ROWS
    channels = weight.shape[1]
    blocks = columns // LANES
    quads = LANES // (2 * PATCH)
    tokens = columns // PATCH
    side = [
        pltpu.make_async_copy(weight, small, sems.at[0]),
        pltpu.make_async_copy(veto_weight, veto_rows, sems.at[1]),
        pltpu.make_async_copy(hit_frames, hit_row, sems.at[2]),
    ]
    for c in side:
        c.start()
    size = GROUP * PATCH
    r, c = iota((size, size), 0), iota((size, size), 1)
    swap = (c == (r % GROUP) * PATCH + r // GROUP).astype(F32).astype(BF16)
    batch = math.gcd(frames // GROUP, 6)

    @pl.loop(0, frames // GROUP // batch)
    def _(i):
        for sub in range(batch):
            g = i * batch + sub
            block = images[pl.ds(pl.multiple_of(g * GROUP, GROUP), GROUP)].reshape(size, columns)
            turned = dot(swap, block).astype(BF16)
            for j in range(blocks):
                for p in range(0, PATCH, quads):
                    tiles = [
                        turned[q * GROUP : (q + 1) * GROUP, j * LANES : (j + 1) * LANES] for q in range(p, p + quads)
                    ]
                    for n, tile in enumerate(turn(tiles, 2 * PATCH)):
                        top = pl.multiple_of((n * blocks + j) * frames + g * GROUP, GROUP)
                        rows[pl.ds(top, GROUP), p * 2 * PATCH : p * 2 * PATCH + LANES] = tile

    for c in side:
        c.wait()
    zero = jnp.zeros((PATCH, channels), BF16)
    for p in range(PATCH):
        tile = small[p * PATCH : (p + 1) * PATCH, :]
        for a in range(2):
            top = (p * 2 + a) * PATCH
            for b in range(2):
                wide[top : top + PATCH, b * channels : (b + 1) * channels] = tile if a == b else zero
    pick = (iota((frames, hits), 0) == hit_row[...]).astype(F32).T.astype(BF16)
    sums = jnp.zeros((frames, channels), F32)
    spots = [(n, j) for n in range(quads) for j in range(blocks)]
    parts = [gelu(dot(rows[(n * blocks + j) * frames : (n * blocks + j + 1) * frames, :], wide[...])) for n, j in spots]
    for part in parts:
        sums = sums + part[:, :channels] + part[:, channels:]
    takens = [dot(pick, part.astype(BF16)) for part in parts]
    for (n, j), taken in zip(spots, takens):
        for k in range(2):
            chosen[pl.ds(j * 2 * quads + 2 * n + k, hits, stride=tokens), :] = taken[
                :, k * channels : (k + 1) * channels
            ]
    scale = jnp.broadcast_to(veto_rows[pl.ds(lax.axis_index("mod"), 1), :] / tokens, (VETO_ROWS, channels))
    row = iota((VETO_ROWS, owned), 0)
    for o in range(owners):
        out[o, 0:hit_rows, :] = chosen[o * hit_rows : (o + 1) * hit_rows, :].astype(BF16)
        veto = lax.dot_general(
            scale,
            sums[o * owned : (o + 1) * owned],
            (((1,), (1,)), ((), ())),
            preferred_element_type=F32,
            precision=lax.Precision.HIGHEST,
        )
        high = veto.astype(BF16).astype(F32)
        both = jnp.where(row == 0, high, jnp.where(row == 1, veto - high, 0.0))
        both = jnp.concatenate([both, jnp.zeros((VETO_ROWS, LANES - owned), F32)], axis=1)
        out[o, hit_rows : hit_rows + VETO_ROWS, :] = both.astype(BF16)


def encode_kernel(streams, width, hidden, *refs):
    features, targets, readout, gain, class_weight = refs[:5]
    halves = refs[5 : 5 + 2 * streams]
    veto, latents, scores, table, pools = refs[5 + 2 * streams :]
    owners = features.shape[0]
    channels = features.shape[2]
    hits = latents.shape[0]
    hit_rows = hits * width
    here = lax.axis_index("stream")
    own = lax.axis_index("mod")
    core = own % 2

    @pl.loop(0, hits)
    def _(slot):
        wanted = targets[own * hits + slot] ^ here
        for k in range(streams):

            @pl.when(wanted == k)
            def _():
                table[slot, core] = halves[2 * k][...]
                table[slot, 1 - core] = halves[2 * k + 1][...]

    terms = jnp.sum(features[:, hit_rows : hit_rows + VETO_ROWS, :].astype(F32), axis=0)
    veto[...] = jnp.sum(terms, axis=0, keepdims=True)[:, : veto.shape[1]]
    pools[...] = jnp.zeros_like(pools)

    extra = table.shape[2] - hidden
    blocks = extra // PAD_ROW
    gap = jnp.zeros((PAD_ROW - width, channels), F32)

    def widen(slot, half):
        return jnp.concatenate(
            [table[slot, half, hidden + j * PAD_ROW : hidden + (j + 1) * PAD_ROW, :] for j in range(blocks)], axis=1
        )

    def spread(x):
        normed = rms_norm(x)
        return jnp.concatenate(
            [jnp.concatenate([normed[r], gap], axis=0).astype(BF16) for r in range(owners)], axis=1
        )

    def mix_in(slot, wide):
        token_in = widen(slot, 0).astype(F32).T.astype(BF16)
        return gelu_narrow(dot(token_in, wide))

    def mix_out(slot, x, mixed):
        back = dot(widen(slot, 1), mixed)
        after = jnp.concatenate(
            [x[r] + back[:width, r * channels : (r + 1) * channels] for r in range(owners)], axis=0
        )
        return after.astype(BF16).astype(F32)

    def channel_in(slot, after):
        chan_in = jnp.concatenate(
            [table[slot, 0, j * channels : (j + 1) * channels, :] for j in range(hidden // channels)], axis=1
        )
        return gelu_narrow(dot(rms_norm(after).astype(BF16), chan_in))

    def channel_out(slot, after, inner):
        last = after + dot(inner, table[slot, 1, 0:hidden, :])
        pool = jnp.sum(last.reshape(owners, width, channels), axis=1) * (1.0 / width)
        pools[pl.ds(pl.multiple_of(slot * owners, owners), owners), :] = pool

    group = hits if owners <= 8 else 2

    @pl.loop(0, hits // group)
    def _(i):
        first = i * group
        every = features[:, pl.ds(pl.multiple_of(first * width, 16), group * width), :].astype(F32)
        slots = [first + a for a in range(group)]
        x = [every[:, a * width : (a + 1) * width] for a in range(group)]
        wide = [spread(v) for v in x]
        mixed = [mix_in(n, v) for n, v in zip(slots, wide)]
        after = [mix_out(n, v, m) for n, v, m in zip(slots, x, mixed)]
        inner = [channel_in(n, v) for n, v in zip(slots, after)]
        for n, v, m in zip(slots, after, inner):
            channel_out(n, v, m)

    pooled = jnp.concatenate(
        [pools[pl.ds(r, 8, stride=owners), :].astype(BF16) for r in range(owners)], axis=1
    )
    latent = rms_norm(dot(pooled, readout[...])) * gain[...]
    latents[:, 0, :] = latent[:hits]
    scores[:, 0, :] = lax.dot_general(
        latent,
        class_weight[...],
        (((1,), (1,)), ((), ())),
        preferred_element_type=F32,
        precision=lax.Precision.HIGHEST,
    )[:hits]


def vmem(count):
    return [pl.BlockSpec(memory_space=pltpu.VMEM)] * count


def in_hbm(x):
    return pltpu.with_memory_space_constraint(x, pltpu.HBM)


def local(
    pixels,
    stem_weight,
    veto_weight,
    hit_frames,
    assign,
    token_in,
    token_out,
    chan_in,
    chan_out,
    readout,
    latent_gain,
    class_weight,
):
    owners = lax.axis_size("mod")
    streams = lax.axis_size("stream")
    _, frames, height, columns = pixels.shape
    channels = stem_weight.shape[1]
    mix, width = token_in.shape[1:]
    hidden = chan_in.shape[2]
    hits = hit_frames.shape[1]
    hits_owned = hits // owners
    hit_rows = hits_owned * width
    half_rows = hidden + mix * PAD_ROW // LANES
    anywhere = pl.BlockSpec(memory_space=pl.ANY)

    half = pltpu.VMEM((half_rows, LANES), BF16)
    mine, other, images = pl.pallas_call(
        pack_kernel,
        name="pack",
        out_shape=(half, half, pltpu.VMEM((frames, height, columns), BF16)),
        in_specs=[anywhere] * 5,
        out_specs=vmem(3),
        scratch_shapes=[
            pltpu.VMEM((width, mix), BF16),
            pltpu.VMEM((width, mix), BF16),
            pltpu.SemaphoreType.DMA((4 + hidden // LANES,)),
        ],
        compiler_params=pltpu.CompilerParams(vmem_limit_bytes=PACK_VMEM_BYTES),
    )(in_hbm(token_in[0].T), in_hbm(token_out[0]), in_hbm(chan_in[0]), in_hbm(chan_out[0]), in_hbm(pixels[0]))

    def send(k, rows):
        got = lax.ppermute(rows, "stream", [(i, i ^ k) for i in range(streams)])
        return [got, lax.ppermute(got, "mod", [(i, i ^ 1) for i in range(owners)])]

    halves = {0: [mine, other]} | {k: send(k, mine) for k in range(streams - 1, 0, -1)}
    outgoing = pl.pallas_call(
        stem_kernel,
        name="stem",
        out_shape=jax.ShapeDtypeStruct((owners, hit_rows + VETO_ROWS, channels), BF16),
        in_specs=vmem(1) + [anywhere] * 3,
        out_specs=vmem(1)[0],
        scratch_shapes=[
            pltpu.VMEM((frames * columns // (2 * PATCH), 2 * PATCH * PATCH), BF16),
            pltpu.VMEM(stem_weight.shape, BF16),
            pltpu.VMEM((2 * PATCH * PATCH, 2 * channels), BF16),
            pltpu.VMEM(veto_weight.shape, F32),
            pltpu.VMEM((1, hits), jnp.int32),
            pltpu.VMEM((hits * width, channels), F32),
            pltpu.SemaphoreType.DMA((3,)),
        ],
        compiler_params=pltpu.CompilerParams(vmem_limit_bytes=STEM_VMEM_BYTES),
        cost_estimate=pl.CostEstimate(flops=5_000_000_000, bytes_accessed=3_000_000, transcendentals=0),
    )(images, in_hbm(stem_weight), in_hbm(veto_weight), in_hbm(hit_frames))
    received = lax.all_to_all(outgoing, "mod", split_axis=0, concat_axis=0, tiled=True)
    halves = [ref for k in range(streams) for ref in halves[k]]

    veto, latents, scores = pl.pallas_call(
        functools.partial(encode_kernel, streams, width, hidden),
        name="encode",
        out_shape=(
            jax.ShapeDtypeStruct((1, frames // owners), F32),
            jax.ShapeDtypeStruct((hits_owned, 1, channels), F32),
            jax.ShapeDtypeStruct((hits_owned, 1, class_weight.shape[1]), F32),
        ),
        in_specs=vmem(1)
        + [pl.BlockSpec(memory_space=pltpu.SMEM)]
        + vmem(3 + len(halves)),
        out_specs=tuple(vmem(3)),
        scratch_shapes=[
            pltpu.VMEM((hits_owned, 2, half_rows, LANES), BF16),
            pltpu.VMEM((8 * owners, channels), F32),
        ],
        compiler_params=pltpu.CompilerParams(vmem_limit_bytes=ENCODE_VMEM_BYTES),
    )(received, assign.reshape(hits), readout, latent_gain.reshape(1, channels), class_weight.T, *halves)
    return (veto, jnp.swapaxes(latents, 0, 1), jnp.swapaxes(scores, 0, 1))


def solution(mesh):
    in_specs = (
        P("stream", None, "mod", None),
        P(),
        P(),
        P("stream", None),
        P("stream", None, None),
        P("stream", None, None),
        P("stream", None, None),
        P("stream", None, None),
        P("stream", None, None),
        P(),
        P(),
        P(),
    )
    out_specs = (P("stream", "mod"), P("stream", "mod", None), P("stream", "mod", None))
    return jax.shard_map(local, mesh=mesh, in_specs=in_specs, out_specs=out_specs, check_vma=False)
```

time: 37.8 us -> 29.1 us (0.77)
  Pallas kernels: 19.5 us -> 10.9 us
    pallas_call x1, Pallas kernels: 10.3 us -> 4.87 us  [local(): pl.pallas_call(functools.partial(encode_kernel, streams, width, hidden),...]
    ppermute x6, waiting for transfers between devices: 0.16 us -> 4.05 us  [the longest x3 4.04 us: send(): got = lax.ppermute(rows, 'stream', [(i, i ^ k) for i in range(streams)])]
    all_to_all x1, waiting for transfers between devices: 6.46 us -> 2.57 us  [local(): lax.all_to_all(outgoing, 'mod', split_axis=0, concat_axis=0, tiled=True)]
    pallas_call x1, Pallas kernels: 7.47 us -> 4.11 us  [local(): pl.pallas_call(stem_kernel, name='stem', out_shape=jax.ShapeDtypeStruct((...]
  transfers between devices with their start and end apart: 7 -> 7, of which waited for: 2 -> 2; matrix products, arithmetic and copies ran while one was open for 0% -> 0% of each run, Pallas kernels for 20% -> 14%
where the time goes in v2:
time: 29.1 us; the launch traced here: 28.9 us
  Pallas kernels  10.9 us (37%)
  starting transfers between devices  10.6 us (36%)
  waiting for transfers between devices  6.63 us (23%)
  between operations  0.7 us (2%)
    ppermute x3, starting transfers between devices, send(): got = lax.ppermute(rows, 'stream', [(i, i ^ k) for i in range(streams)])  5.76 us
    pallas_call x1, Pallas kernels, local(): pl.pallas_call(functools.partial(encode_kernel, streams, width, hidden),...  4.87 us
    pallas_call x1, Pallas kernels, local(): pl.pallas_call(stem_kernel, name='stem', out_shape=jax.ShapeDtypeStruct((...  4.11 us
    ppermute x3, waiting for transfers between devices, send(): got = lax.ppermute(rows, 'stream', [(i, i ^ k) for i in range(streams)])  4.04 us
    all_to_all x1, starting transfers between devices, local(): lax.all_to_all(outgoing, 'mod', split_axis=0, concat_axis=0, tiled=True)  3.86 us
    all_to_all x1, waiting for transfers between devices, local(): lax.all_to_all(outgoing, 'mod', split_axis=0, concat_axis=0, tiled=True)  2.57 us
    pallas_call x1, Pallas kernels, local(): pl.pallas_call(pack_kernel, name='pack', out_shape=(half, half, pltpu.VME...  1.93 us
    ppermute x3, starting transfers between devices, send(): return [got, lax.ppermute(got, 'mod', [(i, i ^ 1) for i in range(owners)])]  1.01 us
  transfers between devices with their start and end apart: 7, of which 2 were waited for; matrix products, arithmetic and copies ran while one was open for 0% of the time, Pallas kernels for 14%

profile of v2, /device:TPU:0, one launch (start us, length us, event | category | flops | bytes accessed | tf_op | source)
XLA Modules:
  0.0 28.9 jit_solution(9044931243274409518)
XLA Ops:
  0.6 1.9 %pack.1 = (bf16[608,128]{1,0:T(8,128)(2,1)S(1)}, bf16[608,128]{1,0:T(8,128)(2,1)S(1)}, bf16[192,16,384]{2,1,0:T(8,128)(2,1)S(1)}) custom-call(bf16[24,384]{1,0:T(8,128)(2,1)} %bitcast.18, bf16[24,384]{1,0:T(8,128)(2,1)} %bitcast.19, bf16[128,512]{1,0:T(8,128)(2,1)} %bitcast.16, bf16[512,128]{1,0:T(8,128)(2,1)} %bitcast.17, bf16[192,16,384]{2,1,0:T(8,128)(2,1)} %bitcast.15), custom_call_target="tpu_custom_call" | custom-call | tf_op jit(solution)/shard_map/pack/pallas_call | solution.py:319
  2.6 5.1 %collective-permute-start.4 = (bf16[608,128]{1,0:T(8,128)(2,1)S(1)}, bf16[608,128]{1,0:T(8,128)(2,1)S(1)}, u32[]{:S(2)}, u32[]{:S(2)}) collective-permute-start(bf16[608,128]{1,0:T(8,128)(2,1)S(1)} %get-tuple-element.10.refs_5_), channel_id=1, source_target_pairs={{0,24},{8,16},{16,8},{24,0},{1,25},{9,17},{17,9},{25,1},{2,26},{10... | collective-permute-start | bytes 466952 | tf_op jit(solution)/shard_map/ppermute | solution.py:334
  7.7 0.0 collective-permute-start.2
  7.7 0.6 %collective-permute-start = (bf16[608,128]{1,0:T(8,128)(2,1)S(1)}, bf16[608,128]{1,0:T(8,128)(2,1)S(1)}, u32[]{:S(2)}, u32[]{:S(2)}) collective-permute-start(bf16[608,128]{1,0:T(8,128)(2,1)S(1)} %get-tuple-element.10.refs_5_), channel_id=1, source_target_pairs={{0,8},{8,0},{16,24},{24,16},{1,9},{9,1},{17,25},{25,17},{2,10},{10... | collective-permute-start | bytes 466952 | tf_op jit(solution)/shard_map/ppermute | solution.py:334
  8.3 0.0 copy-start
  8.3 0.0 copy-start.1
  8.3 0.0 copy-start.2
  8.3 0.0 copy-start.3
  8.3 4.1 %stem.1 = bf16[8,160,128]{2,1,0:T(8,128)(2,1)} custom-call(bf16[192,16,384]{2,1,0:T(8,128)(2,1)S(1)} %get-tuple-element.9.images, bf16[256,128]{1,0:T(8,128)(2,1)} %weight.1, f32[8,128]{1,0:T(8,128)} %veto_weight.1, s32[1,48]{1,0:T(1,128)} %hit_frames.1), custom_call_target="tpu_custom_call" | custom-call | flops 5000000000 | bytes 3000000 | tf_op jit(solution)/shard_map/stem/pallas_call | solution.py:338
  12.5 3.9 %all-to-all-start = ((bf16[8,160,128]{2,1,0:T(8,128)(2,1)}), bf16[8,160,128]{2,1,0:T(8,128)(2,1)S(1)}, u32[]{:S(2)}, u32[]{:S(2)}) async-start(bf16[8,160,128]{2,1,0:T(8,128)(2,1)} %stem.1), calls=%async_computation | async-start | bytes 655360 | tf_op jit(solution)/shard_map/all_to_all | solution.py:356
  16.3 0.0 collective-permute-done.4.refs_11_
  16.3 0.5 %collective-permute-start.5 = (bf16[608,128]{1,0:T(8,128)(2,1)S(1)}, bf16[608,128]{1,0:T(8,128)(2,1)S(1)}, u32[]{:S(2)}, u32[]{:S(2)}) collective-permute-start(bf16[608,128]{1,0:T(8,128)(2,1)S(1)} %collective-permute-done.4.refs_11_), channel_id=1, source_target_pairs={{0,1},{1,0},{2,3},{3,2},{4,5},{5,4},{6,7},{7,6},{8,9},{9,8},{10,11... | collective-permute-start | bytes 466952 | tf_op jit(solution)/shard_map/ppermute | solution.py:335
  16.8 4.0 %collective-permute-done.2.refs_9_ = bf16[608,128]{1,0:T(8,128)(2,1)S(1)} collective-permute-done((bf16[608,128]{1,0:T(8,128)(2,1)S(1)}, bf16[608,128]{1,0:T(8,128)(2,1)S(1)}, u32[]{:S(2)}, u32[]{:S(2)}) %collective-permute-start.2) | collective-permute-done | bytes 155680 | tf_op jit(solution)/shard_map/ppermute | solution.py:334
  20.9 0.0 collective-permute-start.3
  20.9 0.0 collective-permute-done.refs_7_
  20.9 0.5 %collective-permute-start.1 = (bf16[608,128]{1,0:T(8,128)(2,1)S(1)}, bf16[608,128]{1,0:T(8,128)(2,1)S(1)}, u32[]{:S(2)}, u32[]{:S(2)}) collective-permute-start(bf16[608,128]{1,0:T(8,128)(2,1)S(1)} %collective-permute-done.refs_7_), channel_id=1, source_target_pairs={{0,1},{1,0},{2,3},{3,2},{4,5},{5,4},{6,7},{7,6},{8,9},{9,8},{10,11... | collective-permute-start | bytes 466952 | tf_op jit(solution)/shard_map/ppermute | solution.py:335
  21.4 2.6 %all-to-all-done.refs_0_ = bf16[8,160,128]{2,1,0:T(8,128)(2,1)S(1)} async-done(((bf16[8,160,128]{2,1,0:T(8,128)(2,1)}), bf16[8,160,128]{2,1,0:T(8,128)(2,1)S(1)}, u32[]{:S(2)}, u32[]{:S(2)}) %all-to-all-start) | async-done | bytes 327712 | tf_op jit(solution)/shard_map/all_to_all | solution.py:356
  24.0 0.0 collective-permute-done.5.refs_12_
  24.0 0.0 collective-permute-done.3.refs_10_
  24.0 0.0 collective-permute-done.1.refs_8_
  24.0 0.0 copy-done
  24.0 0.0 copy-done.1
  24.0 0.0 copy-done.2
  24.0 0.0 copy-done.3
  24.0 4.9 %encode.1 = (f32[1,24]{1,0:T(1,128)}, f32[6,1,128]{2,1,0:T(1,128)}, f32[6,1,8]{2,1,0:T(1,128)}) custom-call(bf16[8,160,128]{2,1,0:T(8,128)(2,1)S(1)} %all-to-all-done.refs_0_, s32[48]{0:T(128)S(1)} %bitcast.13, bf16[1024,128]{1,0:T(8,128)(2,1)S(1)} %copy-done, f32[1,128]{1,0:T(1,128)S(1)} %bitcast.14, f32[8,128]{1,0:T(8,128)S(1)} %bitcast.12, ...), custom_call_target="tpu_custom_call" | custom-call | tf_op jit(solution)/shard_map/encode/pallas_call | solution.py:359
Async XLA Ops:
  2.6 13.7 %collective-permute-start.4 = (bf16[608,128]{1,0:T(8,128)(2,1)S(1)}, bf16[608,128]{1,0:T(8,128)(2,1)S(1)}, u32[]{:S(2)}, u32[]{:S(2)}) collective-permute-start(bf16[608,128]{1,0:T(8,128)(2,1)S(1)} %get-tuple-element.10.refs_5_), channel_id=1, source_target_pairs={{0,24},{8,16},{16,8},{24,0},{1,25},{9,17},{17,9},{25,1},{2,26},{10... | collective-permute-start | bytes 466952 | tf_op jit(solution)/shard_map/ppermute | solution.py:334
  7.7 13.2 %collective-permute-start.2 = (bf16[608,128]{1,0:T(8,128)(2,1)S(1)}, bf16[608,128]{1,0:T(8,128)(2,1)S(1)}, u32[]{:S(2)}, u32[]{:S(2)}) collective-permute-start(bf16[608,128]{1,0:T(8,128)(2,1)S(1)} %get-tuple-element.10.refs_5_), channel_id=1, source_target_pairs={{0,16},{8,24},{16,0},{24,8},{1,17},{9,25},{17,1},{25,9},{2,18},{10... | collective-permute-start | bytes 466952 | tf_op jit(solution)/shard_map/ppermute | solution.py:334
  7.7 13.2 %collective-permute-start = (bf16[608,128]{1,0:T(8,128)(2,1)S(1)}, bf16[608,128]{1,0:T(8,128)(2,1)S(1)}, u32[]{:S(2)}, u32[]{:S(2)}) collective-permute-start(bf16[608,128]{1,0:T(8,128)(2,1)S(1)} %get-tuple-element.10.refs_5_), channel_id=1, source_target_pairs={{0,8},{8,0},{16,24},{24,16},{1,9},{9,1},{17,25},{25,17},{2,10},{10... | collective-permute-start | bytes 466952 | tf_op jit(solution)/shard_map/ppermute | solution.py:334
  8.3 15.6 %copy-start = (bf16[1024,128]{1,0:T(8,128)(2,1)S(1)}, bf16[1024,128]{1,0:T(8,128)(2,1)}, u32[]{:S(2)}) copy-start(bf16[1024,128]{1,0:T(8,128)(2,1)} %refs_2_.1) | copy-start | bytes 786436
  8.3 15.7 %copy-start.1 = (f32[128,8]{0,1:T(8,128)S(1)}, f32[128,8]{0,1:T(8,128)}, u32[]{:S(2)}) copy-start(f32[128,8]{0,1:T(8,128)} %param.23) | copy-start | bytes 12292
  8.3 15.7 %copy-start.2 = (s32[1,48,1]{1,2,0:T(1,128)S(1)}, s32[1,48,1]{1,2,0:T(1,128)}, u32[]{:S(2)}) copy-start(s32[1,48,1]{1,2,0:T(1,128)} %param.16) | copy-start | bytes 580
  8.3 15.7 %copy-start.3 = (f32[128]{0:T(128)S(1)}, f32[128]{0:T(128)}, u32[]{:S(2)}) copy-start(f32[128]{0:T(128)} %param.22) | copy-start | bytes 1540
  12.5 11.5 %all-to-all-start = ((bf16[8,160,128]{2,1,0:T(8,128)(2,1)}), bf16[8,160,128]{2,1,0:T(8,128)(2,1)S(1)}, u32[]{:S(2)}, u32[]{:S(2)}) async-start(bf16[8,160,128]{2,1,0:T(8,128)(2,1)} %stem.1), calls=%async_computation | async-start | bytes 655360 | tf_op jit(solution)/shard_map/all_to_all | solution.py:356
  16.3 7.6 %collective-permute-start.5 = (bf16[608,128]{1,0:T(8,128)(2,1)S(1)}, bf16[608,128]{1,0:T(8,128)(2,1)S(1)}, u32[]{:S(2)}, u32[]{:S(2)}) collective-permute-start(bf16[608,128]{1,0:T(8,128)(2,1)S(1)} %collective-permute-done.4.refs_11_), channel_id=1, source_target_pairs={{0,1},{1,0},{2,3},{3,2},{4,5},{5,4},{6,7},{7,6},{8,9},{9,8},{10,11... | collective-permute-start | bytes 466952 | tf_op jit(solution)/shard_map/ppermute | solution.py:335
  20.9 3.1 %collective-permute-start.3 = (bf16[608,128]{1,0:T(8,128)(2,1)S(1)}, bf16[608,128]{1,0:T(8,128)(2,1)S(1)}, u32[]{:S(2)}, u32[]{:S(2)}) collective-permute-start(bf16[608,128]{1,0:T(8,128)(2,1)S(1)} %collective-permute-done.2.refs_9_), channel_id=1, source_target_pairs={{0,1},{1,0},{2,3},{3,2},{4,5},{5,4},{6,7},{7,6},{8,9},{9,8},{10,11... | collective-permute-start | bytes 466952 | tf_op jit(solution)/shard_map/ppermute | solution.py:335
  20.9 3.1 %collective-permute-start.1 = (bf16[608,128]{1,0:T(8,128)(2,1)S(1)}, bf16[608,128]{1,0:T(8,128)(2,1)S(1)}, u32[]{:S(2)}, u32[]{:S(2)}) collective-permute-start(bf16[608,128]{1,0:T(8,128)(2,1)S(1)} %collective-permute-done.refs_7_), channel_id=1, source_target_pairs={{0,1},{1,0},{2,3},{3,2},{4,5},{5,4},{6,7},{7,6},{8,9},{9,8},{10,11... | collective-permute-start | bytes 466952 | tf_op jit(solution)/shard_map/ppermute | solution.py:335

commit v3 on v2

--- a/solution.py
+++ b/solution.py
@@ -46,7 +46,7 @@
 
 
 def pack_kernel(
-    token_in, token_out, chan_in, chan_out, pixels, mine, other, images, token_in_rows, token_out_rows, sems
+    token_in, token_out, chan_in, chan_out, mine, other, token_in_rows, token_out_rows, sems
 ):
     core = lax.axis_index("mod") % 2
     channels, hidden = chan_in.shape
@@ -57,7 +57,6 @@
     )
     for c in small:
         c.start()
-    whole = pltpu.make_async_copy(pixels, images, sems.at[3 + hidden // LANES])
 
     def pack(first, second):
         large = [pltpu.make_async_copy(chan_out, second.at[pl.ds(0, hidden)], sems.at[2])]
@@ -69,7 +68,6 @@
             )
         for c in large:
             c.start()
-        whole.start()
         for c in small:
             c.wait()
         for source, ref in ((token_in_rows, first), (token_out_rows, second)):
@@ -87,8 +85,6 @@
     @pl.when(core == 1)
     def _():
         pack(other, mine)
-
-    whole.wait()
 
 
 def turn(tiles, span):
@@ -163,9 +159,9 @@
     pick = (iota((frames, hits), 0) == hit_row[...]).astype(F32).T.astype(BF16)
     sums = jnp.zeros((frames, channels), F32)
     spots = [(n, j) for n in range(quads) for j in range(blocks)]
-    parts = [gelu(dot(rows[(n * blocks + j) * frames : (n * blocks + j + 1) * frames, :], wide[...])) for n, j in spots]
+    parts = [gelu_narrow(dot(rows[(n * blocks + j) * frames : (n * blocks + j + 1) * frames, :], wide[...])) for n, j in spots]
     for part in parts:
-        sums = sums + part[:, :channels] + part[:, channels:]
+        sums = sums + part[:, :channels].astype(F32) + part[:, channels:].astype(F32)
     takens = [dot(pick, part.astype(BF16)) for part in parts]
     for (n, j), taken in zip(spots, takens):
         for k in range(2):
@@ -283,6 +279,10 @@
 
 def vmem(count):
     return [pl.BlockSpec(memory_space=pltpu.VMEM)] * count
+
+
+def in_vmem(x):
+    return pltpu.with_memory_space_constraint(x, pltpu.VMEM)
 
 
 def in_hbm(x):
@@ -316,19 +316,20 @@
     anywhere = pl.BlockSpec(memory_space=pl.ANY)
 
     half = pltpu.VMEM((half_rows, LANES), BF16)
-    mine, other, images = pl.pallas_call(
+    mine, other = pl.pallas_call(
         pack_kernel,
         name="pack",
-        out_shape=(half, half, pltpu.VMEM((frames, height, columns), BF16)),
-        in_specs=[anywhere] * 5,
-        out_specs=vmem(3),
+        out_shape=(half, half),
+        in_specs=[anywhere] * 4,
+        out_specs=vmem(2),
         scratch_shapes=[
             pltpu.VMEM((width, mix), BF16),
             pltpu.VMEM((width, mix), BF16),
             pltpu.SemaphoreType.DMA((4 + hidden // LANES,)),
         ],
         compiler_params=pltpu.CompilerParams(vmem_limit_bytes=PACK_VMEM_BYTES),
-    )(in_hbm(token_in[0].T), in_hbm(token_out[0]), in_hbm(chan_in[0]), in_hbm(chan_out[0]), in_hbm(pixels[0]))
+        cost_estimate=pl.CostEstimate(flops=5000000000, bytes_accessed=3000000, transcendentals=0),
+    )(in_hbm(token_in[0].T), in_hbm(token_out[0]), in_hbm(chan_in[0]), in_hbm(chan_out[0]))
 
     def send(k, rows):
         got = lax.ppermute(rows, "stream", [(i, i ^ k) for i in range(streams)])
@@ -352,7 +353,7 @@
         ],
         compiler_params=pltpu.CompilerParams(vmem_limit_bytes=STEM_VMEM_BYTES),
         cost_estimate=pl.CostEstimate(flops=5_000_000_000, bytes_accessed=3_000_000, transcendentals=0),
-    )(images, in_hbm(stem_weight), in_hbm(veto_weight), in_hbm(hit_frames))
+    )(in_vmem(pixels[0]), in_hbm(stem_weight), in_hbm(veto_weight), in_hbm(hit_frames))
     received = lax.all_to_all(outgoing, "mod", split_axis=0, concat_axis=0, tiled=True)
     halves = [ref for k in range(streams) for ref in halves[k]]
 

time: 29.1 us -> 28.2 us (0.969)
  Pallas kernels: 10.9 us -> 9.93 us
    pallas_call x1, Pallas kernels: 1.93 us -> 1.16 us  [local(): pl.pallas_call(pack_kernel, name='pack', out_shape=(half, half), in_specs...]
    ppermute x3, waiting for transfers between devices: 4.04 us -> 3.54 us  [send(): got = lax.ppermute(rows, 'stream', [(i, i ^ k) for i in range(streams)])]
    all_to_all x1, waiting for transfers between devices: 2.57 us -> 3.07 us  [local(): lax.all_to_all(outgoing, 'mod', split_axis=0, concat_axis=0, tiled=True)]
where the time goes in v3:
time: 28.2 us; the launch traced here: 27.9 us
  starting transfers between devices  10.6 us (38%)
  Pallas kernels  9.93 us (35%)
  waiting for transfers between devices  6.63 us (24%)
  between operations  0.72 us (3%)
    ppermute x3, starting transfers between devices, send(): got = lax.ppermute(rows, 'stream', [(i, i ^ k) for i in range(streams)])  5.68 us
    pallas_call x1, Pallas kernels, local(): pl.pallas_call(functools.partial(encode_kernel, streams, width, hidden),...  4.88 us
    all_to_all x1, starting transfers between devices, local(): lax.all_to_all(outgoing, 'mod', split_axis=0, concat_axis=0, tiled=True)  3.94 us
    pallas_call x1, Pallas kernels, local(): pl.pallas_call(stem_kernel, name='stem', out_shape=jax.ShapeDtypeStruct((...  3.89 us
    ppermute x3, waiting for transfers between devices, send(): got = lax.ppermute(rows, 'stream', [(i, i ^ k) for i in range(streams)])  3.54 us
    all_to_all x1, waiting for transfers between devices, local(): lax.all_to_all(outgoing, 'mod', split_axis=0, concat_axis=0, tiled=True)  3.07 us
    pallas_call x1, Pallas kernels, local(): pl.pallas_call(pack_kernel, name='pack', out_shape=(half, half), in_specs...  1.16 us
    ppermute x3, starting transfers between devices, send(): return [got, lax.ppermute(got, 'mod', [(i, i ^ 1) for i in range(owners)])]  1.01 us
  transfers between devices with their start and end apart: 7, of which 2 were waited for; matrix products, arithmetic and copies ran while one was open for 0% of the time, Pallas kernels for 14%

profile of v3, /device:TPU:0, one launch (start us, length us, event | category | flops | bytes accessed | tf_op | source)
XLA Modules:
  0.0 27.9 jit_solution(12844504978859998387)
XLA Ops:
  0.6 0.0 copy-start.4
  0.6 1.2 %pack.1 = (bf16[608,128]{1,0:T(8,128)(2,1)S(1)}, bf16[608,128]{1,0:T(8,128)(2,1)S(1)}) custom-call(bf16[24,384]{1,0:T(8,128)(2,1)} %bitcast.18, bf16[24,384]{1,0:T(8,128)(2,1)} %bitcast.19, bf16[128,512]{1,0:T(8,128)(2,1)} %bitcast.16, bf16[512,128]{1,0:T(8,128)(2,1)} %bitcast.17), custom_call_target="tpu_custom_call" | custom-call | flops 5000000000 | bytes 3000000 | tf_op jit(solution)/shard_map/pack/pallas_call | solution.py:319
  1.8 3.1 %collective-permute-start = (bf16[608,128]{1,0:T(8,128)(2,1)S(1)}, bf16[608,128]{1,0:T(8,128)(2,1)S(1)}, u32[]{:S(2)}, u32[]{:S(2)}) collective-permute-start(bf16[608,128]{1,0:T(8,128)(2,1)S(1)} %get-tuple-element.8.refs_5_), channel_id=1, source_target_pairs={{0,8},{8,0},{16,24},{24,16},{1,9},{9,1},{17,25},{25,17},{2,10},{10... | collective-permute-start | bytes 466952 | tf_op jit(solution)/shard_map/ppermute | solution.py:335
  4.9 2.6 %collective-permute-start.2 = (bf16[608,128]{1,0:T(8,128)(2,1)S(1)}, bf16[608,128]{1,0:T(8,128)(2,1)S(1)}, u32[]{:S(2)}, u32[]{:S(2)}) collective-permute-start(bf16[608,128]{1,0:T(8,128)(2,1)S(1)} %get-tuple-element.8.refs_5_), channel_id=1, source_target_pairs={{0,16},{8,24},{16,0},{24,8},{1,17},{9,25},{17,1},{25,9},{2,18},{10... | collective-permute-start | bytes 466952 | tf_op jit(solution)/shard_map/ppermute | solution.py:335
  7.5 0.0 collective-permute-start.4
  7.5 0.0 copy-done.4
  7.5 0.0 copy-start
  7.5 0.0 copy-start.1
  7.5 0.0 copy-start.2
  7.5 0.0 copy-start.3
  7.5 3.9 %stem.1 = bf16[8,160,128]{2,1,0:T(8,128)(2,1)} custom-call(bf16[192,16,384]{2,1,0:T(8,128)(2,1)S(1)} %bitcast.15, bf16[256,128]{1,0:T(8,128)(2,1)} %weight.1, f32[8,128]{1,0:T(8,128)} %veto_weight.1, s32[1,48]{1,0:T(1,128)} %hit_frames.1), custom_call_target="tpu_custom_call" | custom-call | flops 5000000000 | bytes 3000000 | tf_op jit(solution)/shard_map/stem/pallas_call | solution.py:339
  11.4 3.9 %all-to-all-start = ((bf16[8,160,128]{2,1,0:T(8,128)(2,1)}), bf16[8,160,128]{2,1,0:T(8,128)(2,1)S(1)}, u32[]{:S(2)}, u32[]{:S(2)}) async-start(bf16[8,160,128]{2,1,0:T(8,128)(2,1)} %stem.1), calls=%async_computation | async-start | bytes 655360 | tf_op jit(solution)/shard_map/all_to_all | solution.py:357
  15.4 0.0 collective-permute-done.refs_7_
  15.4 0.5 %collective-permute-start.1 = (bf16[608,128]{1,0:T(8,128)(2,1)S(1)}, bf16[608,128]{1,0:T(8,128)(2,1)S(1)}, u32[]{:S(2)}, u32[]{:S(2)}) collective-permute-start(bf16[608,128]{1,0:T(8,128)(2,1)S(1)} %collective-permute-done.refs_7_), channel_id=1, source_target_pairs={{0,1},{1,0},{2,3},{3,2},{4,5},{5,4},{6,7},{7,6},{8,9},{9,8},{10,11... | collective-permute-start | bytes 466952 | tf_op jit(solution)/shard_map/ppermute | solution.py:336
  15.9 3.5 %collective-permute-done.2.refs_9_ = bf16[608,128]{1,0:T(8,128)(2,1)S(1)} collective-permute-done((bf16[608,128]{1,0:T(8,128)(2,1)S(1)}, bf16[608,128]{1,0:T(8,128)(2,1)S(1)}, u32[]{:S(2)}, u32[]{:S(2)}) %collective-permute-start.2) | collective-permute-done | bytes 155680 | tf_op jit(solution)/shard_map/ppermute | solution.py:335
  19.4 0.0 collective-permute-start.3
  19.4 0.0 collective-permute-done.4.refs_11_
  19.4 0.5 %collective-permute-start.5 = (bf16[608,128]{1,0:T(8,128)(2,1)S(1)}, bf16[608,128]{1,0:T(8,128)(2,1)S(1)}, u32[]{:S(2)}, u32[]{:S(2)}) collective-permute-start(bf16[608,128]{1,0:T(8,128)(2,1)S(1)} %collective-permute-done.4.refs_11_), channel_id=1, source_target_pairs={{0,1},{1,0},{2,3},{3,2},{4,5},{5,4},{6,7},{7,6},{8,9},{9,8},{10,11... | collective-permute-start | bytes 466952 | tf_op jit(solution)/shard_map/ppermute | solution.py:336
  19.9 3.1 %all-to-all-done.refs_0_ = bf16[8,160,128]{2,1,0:T(8,128)(2,1)S(1)} async-done(((bf16[8,160,128]{2,1,0:T(8,128)(2,1)}), bf16[8,160,128]{2,1,0:T(8,128)(2,1)S(1)}, u32[]{:S(2)}, u32[]{:S(2)}) %all-to-all-start) | async-done | bytes 327712 | tf_op jit(solution)/shard_map/all_to_all | solution.py:357
  23.0 0.0 collective-permute-done.1.refs_8_
  23.0 0.0 collective-permute-done.3.refs_10_
  23.0 0.0 collective-permute-done.5.refs_12_
  23.0 0.0 copy-done
  23.0 0.0 copy-done.1
  23.0 0.0 copy-done.2
  23.1 0.0 copy-done.3
  23.1 4.9 %encode.1 = (f32[1,24]{1,0:T(1,128)}, f32[6,1,128]{2,1,0:T(1,128)}, f32[6,1,8]{2,1,0:T(1,128)}) custom-call(bf16[8,160,128]{2,1,0:T(8,128)(2,1)S(1)} %all-to-all-done.refs_0_, s32[48]{0:T(128)S(1)} %bitcast.13, bf16[1024,128]{1,0:T(8,128)(2,1)S(1)} %copy-done, f32[1,128]{1,0:T(1,128)S(1)} %bitcast.14, f32[8,128]{1,0:T(8,128)S(1)} %bitcast.12, ...), custom_call_target="tpu_custom_call" | custom-call | tf_op jit(solution)/shard_map/encode/pallas_call | solution.py:360
Async XLA Ops:
  0.6 6.9 %copy-start.4 = (bf16[1,192,16,384]{3,2,1,0:T(8,128)(2,1)S(1)}, bf16[1,192,16,384]{3,2,1,0:T(8,128)(2,1)}, u32[]{:S(2)}) copy-start(bf16[1,192,16,384]{3,2,1,0:T(8,128)(2,1)} %param.12) | copy-start | bytes 7077892
  1.8 13.6 %collective-permute-start = (bf16[608,128]{1,0:T(8,128)(2,1)S(1)}, bf16[608,128]{1,0:T(8,128)(2,1)S(1)}, u32[]{:S(2)}, u32[]{:S(2)}) collective-permute-start(bf16[608,128]{1,0:T(8,128)(2,1)S(1)} %get-tuple-element.8.refs_5_), channel_id=1, source_target_pairs={{0,8},{8,0},{16,24},{24,16},{1,9},{9,1},{17,25},{25,17},{2,10},{10... | collective-permute-start | bytes 466952 | tf_op jit(solution)/shard_map/ppermute | solution.py:335
  4.9 14.5 %collective-permute-start.2 = (bf16[608,128]{1,0:T(8,128)(2,1)S(1)}, bf16[608,128]{1,0:T(8,128)(2,1)S(1)}, u32[]{:S(2)}, u32[]{:S(2)}) collective-permute-start(bf16[608,128]{1,0:T(8,128)(2,1)S(1)} %get-tuple-element.8.refs_5_), channel_id=1, source_target_pairs={{0,16},{8,24},{16,0},{24,8},{1,17},{9,25},{17,1},{25,9},{2,18},{10... | collective-permute-start | bytes 466952 | tf_op jit(solution)/shard_map/ppermute | solution.py:335
  7.5 11.9 %collective-permute-start.4 = (bf16[608,128]{1,0:T(8,128)(2,1)S(1)}, bf16[608,128]{1,0:T(8,128)(2,1)S(1)}, u32[]{:S(2)}, u32[]{:S(2)}) collective-permute-start(bf16[608,128]{1,0:T(8,128)(2,1)S(1)} %get-tuple-element.8.refs_5_), channel_id=1, source_target_pairs={{0,24},{8,16},{16,8},{24,0},{1,25},{9,17},{17,9},{25,1},{2,26},{10... | collective-permute-start | bytes 466952 | tf_op jit(solution)/shard_map/ppermute | solution.py:335
  7.5 15.5 %copy-start = (bf16[1024,128]{1,0:T(8,128)(2,1)S(1)}, bf16[1024,128]{1,0:T(8,128)(2,1)}, u32[]{:S(2)}) copy-start(bf16[1024,128]{1,0:T(8,128)(2,1)} %refs_2_.1) | copy-start | bytes 786436
  7.5 15.5 %copy-start.1 = (f32[128,8]{0,1:T(8,128)S(1)}, f32[128,8]{0,1:T(8,128)}, u32[]{:S(2)}) copy-start(f32[128,8]{0,1:T(8,128)} %param.23) | copy-start | bytes 12292
  7.5 15.5 %copy-start.2 = (s32[1,48,1]{1,2,0:T(1,128)S(1)}, s32[1,48,1]{1,2,0:T(1,128)}, u32[]{:S(2)}) copy-start(s32[1,48,1]{1,2,0:T(1,128)} %param.16) | copy-start | bytes 580
  7.5 15.5 %copy-start.3 = (f32[128]{0:T(128)S(1)}, f32[128]{0:T(128)}, u32[]{:S(2)}) copy-start(f32[128]{0:T(128)} %param.22) | copy-start | bytes 1540
  11.4 11.6 %all-to-all-start = ((bf16[8,160,128]{2,1,0:T(8,128)(2,1)}), bf16[8,160,128]{2,1,0:T(8,128)(2,1)S(1)}, u32[]{:S(2)}, u32[]{:S(2)}) async-start(bf16[8,160,128]{2,1,0:T(8,128)(2,1)} %stem.1), calls=%async_computation | async-start | bytes 655360 | tf_op jit(solution)/shard_map/all_to_all | solution.py:357
  15.4 7.6 %collective-permute-start.1 = (bf16[608,128]{1,0:T(8,128)(2,1)S(1)}, bf16[608,128]{1,0:T(8,128)(2,1)S(1)}, u32[]{:S(2)}, u32[]{:S(2)}) collective-permute-start(bf16[608,128]{1,0:T(8,128)(2,1)S(1)} %collective-permute-done.refs_7_), channel_id=1, source_target_pairs={{0,1},{1,0},{2,3},{3,2},{4,5},{5,4},{6,7},{7,6},{8,9},{9,8},{10,11... | collective-permute-start | bytes 466952 | tf_op jit(solution)/shard_map/ppermute | solution.py:336
  19.4 3.6 %collective-permute-start.3 = (bf16[608,128]{1,0:T(8,128)(2,1)S(1)}, bf16[608,128]{1,0:T(8,128)(2,1)S(1)}, u32[]{:S(2)}, u32[]{:S(2)}) collective-permute-start(bf16[608,128]{1,0:T(8,128)(2,1)S(1)} %collective-permute-done.2.refs_9_), channel_id=1, source_target_pairs={{0,1},{1,0},{2,3},{3,2},{4,5},{5,4},{6,7},{7,6},{8,9},{9,8},{10,11... | collective-permute-start | bytes 466952 | tf_op jit(solution)/shard_map/ppermute | solution.py:336
  19.4 3.6 %collective-permute-start.5 = (bf16[608,128]{1,0:T(8,128)(2,1)S(1)}, bf16[608,128]{1,0:T(8,128)(2,1)S(1)}, u32[]{:S(2)}, u32[]{:S(2)}) collective-permute-start(bf16[608,128]{1,0:T(8,128)(2,1)S(1)} %collective-permute-done.4.refs_11_), channel_id=1, source_target_pairs={{0,1},{1,0},{2,3},{3,2},{4,5},{5,4},{6,7},{7,6},{8,9},{9,8},{10,11... | collective-permute-start | bytes 466952 | tf_op jit(solution)/shard_map/ppermute | solution.py:336

commit v4 on v3

--- a/solution.py
+++ b/solution.py
@@ -87,6 +87,14 @@
         pack(other, mine)
 
 
+def bundle_kernel(chips, *refs):
+    features, out = refs[:chips], refs[-1]
+    other = 1 - lax.axis_index("mod") % 2
+    size = features[0].shape[1]
+    for n, ref in enumerate(features):
+        out[n * size : (n + 1) * size, :] = ref[other]
+
+
 def turn(tiles, span):
     count = len(tiles)
     lane = iota(tiles[0].shape, 1)
@@ -109,13 +117,14 @@
 
 
 def stem_kernel(
-    images, weight, veto_weight, hit_frames, out, rows, small, wide, veto_rows, hit_row, chosen, sems
+    images, weight, veto_weight, hit_frames, *refs
 ):
+    out, (rows, small, wide, veto_rows, hit_row, chosen, totals, sems) = refs[:-8], refs[-8:]
     frames, _, columns = images.shape
-    owners = out.shape[0]
+    owners = 2 * len(out)
     hits = hit_frames.shape[1]
     owned = frames // owners
-    hit_rows = out.shape[1] - VETO_ROWS
+    hit_rows = out[0].shape[1] - VETO_ROWS
     channels = weight.shape[1]
     blocks = columns // LANES
     quads = LANES // (2 * PATCH)
@@ -170,29 +179,35 @@
             ]
     scale = jnp.broadcast_to(veto_rows[pl.ds(lax.axis_index("mod"), 1), :] / tokens, (VETO_ROWS, channels))
     row = iota((VETO_ROWS, owned), 0)
-    for o in range(owners):
-        out[o, 0:hit_rows, :] = chosen[o * hit_rows : (o + 1) * hit_rows, :].astype(BF16)
-        veto = lax.dot_general(
-            scale,
-            sums[o * owned : (o + 1) * owned],
-            (((1,), (1,)), ((), ())),
-            preferred_element_type=F32,
-            precision=lax.Precision.HIGHEST,
-        )
-        high = veto.astype(BF16).astype(F32)
-        both = jnp.where(row == 0, high, jnp.where(row == 1, veto - high, 0.0))
-        both = jnp.concatenate([both, jnp.zeros((VETO_ROWS, LANES - owned), F32)], axis=1)
-        out[o, hit_rows : hit_rows + VETO_ROWS, :] = both.astype(BF16)
-
-
-def encode_kernel(streams, width, hidden, *refs):
-    features, targets, readout, gain, class_weight = refs[:5]
-    halves = refs[5 : 5 + 2 * streams]
-    veto, latents, scores, table, pools = refs[5 + 2 * streams :]
-    owners = features.shape[0]
-    channels = features.shape[2]
+    totals[...] = sums
+    for k in range(owners // 2):
+        for core in range(2):
+            o = ((lax.axis_index("mod") // 2) ^ k) * 2 + core
+            taken = chosen[pl.ds(pl.multiple_of(o * hit_rows, 8), hit_rows), :]
+            out[k][core, 0:hit_rows, :] = taken.astype(BF16)
+            veto = lax.dot_general(
+                scale,
+                totals[pl.ds(pl.multiple_of(o * owned, 8), owned), :],
+                (((1,), (1,)), ((), ())),
+                preferred_element_type=F32,
+                precision=lax.Precision.HIGHEST,
+            )
+            high = veto.astype(BF16).astype(F32)
+            both = jnp.where(row == 0, high, jnp.where(row == 1, veto - high, 0.0))
+            both = jnp.concatenate([both, jnp.zeros((VETO_ROWS, LANES - owned), F32)], axis=1)
+            out[k][core, hit_rows : hit_rows + VETO_ROWS, :] = both.astype(BF16)
+
+
+def encode_kernel(owners, streams, width, hidden, *refs):
+    chips = owners // 2
+    received, bundle, refs = refs[:chips], refs[chips], refs[chips + 1 :]
+    targets, readout, gain, class_weight = refs[:4]
+    halves = refs[4 : 4 + 2 * streams]
+    veto, latents, scores, table, pools = refs[4 + 2 * streams :]
+    channels = received[0].shape[2]
     hits = latents.shape[0]
     hit_rows = hits * width
+    block = hit_rows + VETO_ROWS
     here = lax.axis_index("stream")
     own = lax.axis_index("mod")
     core = own % 2
@@ -207,7 +222,9 @@
                 table[slot, core] = halves[2 * k][...]
                 table[slot, 1 - core] = halves[2 * k + 1][...]
 
-    terms = jnp.sum(features[:, hit_rows : hit_rows + VETO_ROWS, :].astype(F32), axis=0)
+    tails = [ref[core, hit_rows:block, :] for ref in received]
+    tails += [bundle[n * block + hit_rows : (n + 1) * block, :] for n in range(chips)]
+    terms = sum(tail.astype(F32) for tail in tails)
     veto[...] = jnp.sum(terms, axis=0, keepdims=True)[:, : veto.shape[1]]
     pools[...] = jnp.zeros_like(pools)
 
@@ -253,7 +270,12 @@
     @pl.loop(0, hits // group)
     def _(i):
         first = i * group
-        every = features[:, pl.ds(pl.multiple_of(first * width, 16), group * width), :].astype(F32)
+        start = pl.multiple_of(first * width, 16)
+        every = []
+        for n, ref in enumerate(received):
+            every.append(ref[core, pl.ds(start, group * width), :].astype(F32))
+            every.append(bundle[pl.ds(n * block + start, group * width), :].astype(F32))
+        every = jnp.stack(every)
         slots = [first + a for a in range(group)]
         x = [every[:, a * width : (a + 1) * width] for a in range(group)]
         wide = [spread(v) for v in x]
@@ -266,7 +288,9 @@
     pooled = jnp.concatenate(
         [pools[pl.ds(r, 8, stride=owners), :].astype(BF16) for r in range(owners)], axis=1
     )
-    latent = rms_norm(dot(pooled, readout[...])) * gain[...]
+    modules = [((own // 2) ^ (r // 2)) * 2 + (core if r % 2 == 0 else 1 - core) for r in range(owners)]
+    weights = [readout[pl.ds(pl.multiple_of(m * channels, channels), channels), :] for m in modules]
+    latent = rms_norm(dot(pooled, jnp.concatenate(weights, axis=0))) * gain[...]
     latents[:, 0, :] = latent[:hits]
     scores[:, 0, :] = lax.dot_general(
         latent,
@@ -331,17 +355,21 @@
         cost_estimate=pl.CostEstimate(flops=5000000000, bytes_accessed=3000000, transcendentals=0),
     )(in_hbm(token_in[0].T), in_hbm(token_out[0]), in_hbm(chan_in[0]), in_hbm(chan_out[0]))
 
-    def send(k, rows):
-        got = lax.ppermute(rows, "stream", [(i, i ^ k) for i in range(streams)])
-        return [got, lax.ppermute(got, "mod", [(i, i ^ 1) for i in range(owners)])]
-
-    halves = {0: [mine, other]} | {k: send(k, mine) for k in range(streams - 1, 0, -1)}
+    def cross(x, distance):
+        return lax.ppermute(x, "mod", [(i, i ^ distance) for i in range(owners)])
+
+    got = {0: mine}
+    for k in sorted(range(1, streams), key=lambda k: k != streams // 2):
+        low = k & -k
+        pairs = [(i, i ^ low) for i in range(streams)]
+        got[k] = lax.ppermute(got[k ^ low], "stream", pairs)
+    chips = owners // 2
     outgoing = pl.pallas_call(
         stem_kernel,
         name="stem",
-        out_shape=jax.ShapeDtypeStruct((owners, hit_rows + VETO_ROWS, channels), BF16),
+        out_shape=(pltpu.VMEM((2, hit_rows + VETO_ROWS, channels), BF16),) * chips,
         in_specs=vmem(1) + [anywhere] * 3,
-        out_specs=vmem(1)[0],
+        out_specs=vmem(chips),
         scratch_shapes=[
             pltpu.VMEM((frames * columns // (2 * PATCH), 2 * PATCH * PATCH), BF16),
             pltpu.VMEM(stem_weight.shape, BF16),
@@ -349,23 +377,36 @@
             pltpu.VMEM(veto_weight.shape, F32),
             pltpu.VMEM((1, hits), jnp.int32),
             pltpu.VMEM((hits * width, channels), F32),
+            pltpu.VMEM((frames, channels), F32),
             pltpu.SemaphoreType.DMA((3,)),
         ],
         compiler_params=pltpu.CompilerParams(vmem_limit_bytes=STEM_VMEM_BYTES),
         cost_estimate=pl.CostEstimate(flops=5_000_000_000, bytes_accessed=3_000_000, transcendentals=0),
     )(in_vmem(pixels[0]), in_hbm(stem_weight), in_hbm(veto_weight), in_hbm(hit_frames))
-    received = lax.all_to_all(outgoing, "mod", split_axis=0, concat_axis=0, tiled=True)
-    halves = [ref for k in range(streams) for ref in halves[k]]
+    received = [outgoing[0]] + [cross(outgoing[k], 2 * k) for k in range(1, chips)]
+    bundle = pl.pallas_call(
+        functools.partial(bundle_kernel, chips),
+        name="bundle",
+        out_shape=pltpu.VMEM((chips * (hit_rows + VETO_ROWS), LANES), BF16),
+        in_specs=vmem(chips + 1),
+        out_specs=vmem(1)[0],
+        compiler_params=pltpu.CompilerParams(vmem_limit_bytes=PACK_VMEM_BYTES),
+        cost_estimate=pl.CostEstimate(flops=1_000_000_000, bytes_accessed=1_000_000, transcendentals=0),
+    )(*[in_vmem(x) for x in received], in_vmem(got[1]))
+    bundle = cross(bundle, 1)
+    halves = [mine, other]
+    for k in range(1, streams):
+        halves += [got[k], cross(got[k], 1)]
 
     veto, latents, scores = pl.pallas_call(
-        functools.partial(encode_kernel, streams, width, hidden),
+        functools.partial(encode_kernel, owners, streams, width, hidden),
         name="encode",
         out_shape=(
             jax.ShapeDtypeStruct((1, frames // owners), F32),
             jax.ShapeDtypeStruct((hits_owned, 1, channels), F32),
             jax.ShapeDtypeStruct((hits_owned, 1, class_weight.shape[1]), F32),
         ),
-        in_specs=vmem(1)
+        in_specs=vmem(chips + 1)
         + [pl.BlockSpec(memory_space=pltpu.SMEM)]
         + vmem(3 + len(halves)),
         out_specs=tuple(vmem(3)),
@@ -374,7 +415,7 @@
             pltpu.VMEM((8 * owners, channels), F32),
         ],
         compiler_params=pltpu.CompilerParams(vmem_limit_bytes=ENCODE_VMEM_BYTES),
-    )(received, assign.reshape(hits), readout, latent_gain.reshape(1, channels), class_weight.T, *halves)
+    )(*received, bundle, assign.reshape(hits), readout, latent_gain.reshape(1, channels), class_weight.T, *halves)
     return (veto, jnp.swapaxes(latents, 0, 1), jnp.swapaxes(scores, 0, 1))
 
 

time: 28.2 us -> 26.4 us (0.936)
  waiting for transfers between devices: 6.63 us -> 5.59 us
  Pallas kernels: 9.93 us -> 9.2 us
    ppermute x6 -> x10, starting transfers between devices: 6.69 us -> 10.7 us  [the longest x3 6.13 us: local(): got[k] = lax.ppermute(got[k ^ low], 'stream', pairs)]
    all_to_all x1 -> x0, starting transfers between devices: 3.94 us -> none  [local(): lax.all_to_all(outgoing, 'mod', split_axis=0, concat_axis=0, tiled=True)]
    all_to_all x1 -> x0, waiting for transfers between devices: 3.07 us -> none  [local(): lax.all_to_all(outgoing, 'mod', split_axis=0, concat_axis=0, tiled=True)]
    ppermute x6 -> x10, waiting for transfers between devices: 3.55 us -> 5.59 us  [the longest x7 5.1 us: cross(): return lax.ppermute(x, 'mod', [(i, i ^ distance) for i in range(owners)])]
    pallas_call x2 -> x3, Pallas kernels: 8.77 us -> 8.04 us  [the longest x1 4.86 us: local(): pl.pallas_call(functools.partial(encode_kernel, owners, streams, width, h...]
  transfers between devices with their start and end apart: 7 -> 10, of which waited for: 2 -> 8; matrix products, arithmetic and copies ran while one was open for 0% -> 0% of each run, Pallas kernels for 14% -> 12%
where the time goes in v4:
time: 26.4 us; the launch traced here: 26.2 us
  starting transfers between devices  10.7 us (41%)
  Pallas kernels  9.2 us (35%)
  waiting for transfers between devices  5.59 us (21%)
  between operations  0.72 us (3%)
    ppermute x3, starting transfers between devices, local(): got[k] = lax.ppermute(got[k ^ low], 'stream', pairs)  6.13 us
    ppermute x7, waiting for transfers between devices, cross(): return lax.ppermute(x, 'mod', [(i, i ^ distance) for i in range(owners)])  5.1 us
    pallas_call x1, Pallas kernels, local(): pl.pallas_call(functools.partial(encode_kernel, owners, streams, width, h...  4.86 us
    ppermute x7, starting transfers between devices, cross(): return lax.ppermute(x, 'mod', [(i, i ^ distance) for i in range(owners)])  4.54 us
    pallas_call x1, Pallas kernels, local(): pl.pallas_call(stem_kernel, name='stem', out_shape=(pltpu.VMEM((2, hit_ro...  3.17 us
    pallas_call x1, Pallas kernels, local(): pl.pallas_call(pack_kernel, name='pack', out_shape=(half, half), in_specs...  1.16 us
  transfers between devices with their start and end apart: 10, of which 8 were waited for; matrix products, arithmetic and copies ran while one was open for 0% of the time, Pallas kernels for 12%

profile of v4, /device:TPU:0, one launch (start us, length us, event | category | flops | bytes accessed | tf_op | source)
XLA Modules:
  0.0 26.2 jit_solution(16793381953762108082)
XLA Ops:
  0.6 0.0 copy-start.4
  0.6 1.2 %pack.1 = (bf16[608,128]{1,0:T(8,128)(2,1)S(1)}, bf16[608,128]{1,0:T(8,128)(2,1)S(1)}) custom-call(bf16[24,384]{1,0:T(8,128)(2,1)} %bitcast.18, bf16[24,384]{1,0:T(8,128)(2,1)} %bitcast.19, bf16[128,512]{1,0:T(8,128)(2,1)} %bitcast.16, bf16[512,128]{1,0:T(8,128)(2,1)} %bitcast.17), custom_call_target="tpu_custom_call" | custom-call | flops 5000000000 | bytes 3000000 | tf_op jit(solution)/shard_map/pack/pallas_call | solution.py:343
  1.8 3.1 %collective-permute-start.3 = (bf16[608,128]{1,0:T(8,128)(2,1)S(1)}, bf16[608,128]{1,0:T(8,128)(2,1)S(1)}, u32[]{:S(2)}, u32[]{:S(2)}) collective-permute-start(bf16[608,128]{1,0:T(8,128)(2,1)S(1)} %get-tuple-element.16.refs_9_), channel_id=1, source_target_pairs={{0,8},{8,0},{16,24},{24,16},{1,9},{9,1},{17,25},{25,17},{2,10},{10... | collective-permute-start | bytes 466952 | tf_op jit(solution)/shard_map/ppermute | solution.py:365
  4.9 2.6 %collective-permute-start.6 = (bf16[608,128]{1,0:T(8,128)(2,1)S(1)}, bf16[608,128]{1,0:T(8,128)(2,1)S(1)}, u32[]{:S(2)}, u32[]{:S(2)}) collective-permute-start(bf16[608,128]{1,0:T(8,128)(2,1)S(1)} %get-tuple-element.16.refs_9_), channel_id=1, source_target_pairs={{0,16},{8,24},{16,0},{24,8},{1,17},{9,25},{17,1},{25,9},{2,18},{10... | collective-permute-start | bytes 466952 | tf_op jit(solution)/shard_map/ppermute | solution.py:365
  7.5 0.0 copy-done.4
  7.5 3.2 %stem.1 = (bf16[2,160,128]{2,1,0:T(8,128)(2,1)S(1)}, bf16[2,160,128]{2,1,0:T(8,128)(2,1)S(1)}, bf16[2,160,128]{2,1,0:T(8,128)(2,1)S(1)}, bf16[2,160,128]{2,1,0:T(8,128)(2,1)S(1)}) custom-call(bf16[192,16,384]{2,1,0:T(8,128)(2,1)S(1)} %bitcast.15, bf16[256,128]{1,0:T(8,128)(2,1)} %weight.1, f32[8,128]{1,0:T(8,128)} %veto_weight.1, s32[1,48]{1,0:T(1,128)} %hit_frames.1), custom_call_target="tpu_custom_call" | custom-call | flops 5000000000 | bytes 3000000 | tf_op jit(solution)/shard_map/stem/pallas_call | solution.py:367
  10.7 0.0 copy-start
  10.7 0.0 copy-start.1
  10.7 0.0 copy-start.2
  10.7 0.0 copy-start.3
  10.7 1.5 %collective-permute-start = (bf16[2,160,128]{2,1,0:T(8,128)(2,1)S(1)}, bf16[2,160,128]{2,1,0:T(8,128)(2,1)S(1)}, u32[]{:S(2)}, u32[]{:S(2)}) collective-permute-start(bf16[2,160,128]{2,1,0:T(8,128)(2,1)S(1)} %get-tuple-element.13), channel_id=1, source_target_pairs={{0,2},{1,3},{2,0},{3,1},{4,6},{5,7},{6,4},{7,5},{8,10},{9,11},{10,... | collective-permute-start | bytes 245768 | tf_op jit(solution)/shard_map/ppermute | solution.py:359
  12.3 1.5 %collective-permute-start.1 = (bf16[2,160,128]{2,1,0:T(8,128)(2,1)S(1)}, bf16[2,160,128]{2,1,0:T(8,128)(2,1)S(1)}, u32[]{:S(2)}, u32[]{:S(2)}) collective-permute-start(bf16[2,160,128]{2,1,0:T(8,128)(2,1)S(1)} %get-tuple-element.14), channel_id=1, source_target_pairs={{0,4},{1,5},{2,6},{3,7},{4,0},{5,1},{6,2},{7,3},{8,12},{9,13},{10,... | collective-permute-start | bytes 245768 | tf_op jit(solution)/shard_map/ppermute | solution.py:359
  13.8 0.5 %collective-permute-start.2 = (bf16[2,160,128]{2,1,0:T(8,128)(2,1)S(1)}, bf16[2,160,128]{2,1,0:T(8,128)(2,1)S(1)}, u32[]{:S(2)}, u32[]{:S(2)}) collective-permute-start(bf16[2,160,128]{2,1,0:T(8,128)(2,1)S(1)} %get-tuple-element.15), channel_id=1, source_target_pairs={{0,6},{1,7},{2,4},{3,5},{4,2},{5,3},{6,0},{7,1},{8,14},{9,15},{10,... | collective-permute-start | bytes 245768 | tf_op jit(solution)/shard_map/ppermute | solution.py:359
  14.3 0.4 %collective-permute-done.6.refs_13_ = bf16[608,128]{1,0:T(8,128)(2,1)S(1)} collective-permute-done((bf16[608,128]{1,0:T(8,128)(2,1)S(1)}, bf16[608,128]{1,0:T(8,128)(2,1)S(1)}, u32[]{:S(2)}, u32[]{:S(2)}) %collective-permute-start.6) | collective-permute-done | bytes 155680 | tf_op jit(solution)/shard_map/ppermute | solution.py:365
  14.7 0.4 %collective-permute-start.8 = (bf16[608,128]{1,0:T(8,128)(2,1)S(1)}, bf16[608,128]{1,0:T(8,128)(2,1)S(1)}, u32[]{:S(2)}, u32[]{:S(2)}) collective-permute-start(bf16[608,128]{1,0:T(8,128)(2,1)S(1)} %collective-permute-done.6.refs_13_), channel_id=1, source_target_pairs={{0,8},{8,0},{16,24},{24,16},{1,9},{9,1},{17,25},{25,17},{2,10},{10... | collective-permute-start | bytes 466952 | tf_op jit(solution)/shard_map/ppermute | solution.py:365
  15.1 0.3 %collective-permute-done.refs_1_ = bf16[2,160,128]{2,1,0:T(8,128)(2,1)S(1)} collective-permute-done((bf16[2,160,128]{2,1,0:T(8,128)(2,1)S(1)}, bf16[2,160,128]{2,1,0:T(8,128)(2,1)S(1)}, u32[]{:S(2)}, u32[]{:S(2)}) %collective-permute-start) | collective-permute-done | bytes 81952 | tf_op jit(solution)/shard_map/ppermute | solution.py:359
  15.4 2.1 %collective-permute-done.1.refs_2_ = bf16[2,160,128]{2,1,0:T(8,128)(2,1)S(1)} collective-permute-done((bf16[2,160,128]{2,1,0:T(8,128)(2,1)S(1)}, bf16[2,160,128]{2,1,0:T(8,128)(2,1)S(1)}, u32[]{:S(2)}, u32[]{:S(2)}) %collective-permute-start.1) | collective-permute-done | bytes 81952 | tf_op jit(solution)/shard_map/ppermute | solution.py:359
  17.6 1.6 %collective-permute-done.2.refs_3_ = bf16[2,160,128]{2,1,0:T(8,128)(2,1)S(1)} collective-permute-done((bf16[2,160,128]{2,1,0:T(8,128)(2,1)S(1)}, bf16[2,160,128]{2,1,0:T(8,128)(2,1)S(1)}, u32[]{:S(2)}, u32[]{:S(2)}) %collective-permute-start.2) | collective-permute-done | bytes 81952 | tf_op jit(solution)/shard_map/ppermute | solution.py:359
  19.1 0.0 collective-permute-done.3.refs_4_.refs_11_
  19.2 0.1 collective-permute-start.4
  19.2 0.5 %collective-permute-start.5 = (bf16[608,128]{1,0:T(8,128)(2,1)S(1)}, bf16[608,128]{1,0:T(8,128)(2,1)S(1)}, u32[]{:S(2)}, u32[]{:S(2)}) collective-permute-start(bf16[608,128]{1,0:T(8,128)(2,1)S(1)} %collective-permute-done.3.refs_4_.refs_11_), channel_id=1, source_target_pairs={{0,1},{1,0},{2,3},{3,2},{4,5},{5,4},{6,7},{7,6},{8,9},{9,8},{10,11... | collective-permute-start | bytes 466952 | tf_op jit(solution)/shard_map/ppermute | solution.py:359
  19.7 0.1 collective-permute-start.7
  19.8 0.1 collective-permute-done.8.refs_15_
  19.9 0.3 %collective-permute-start.9 = (bf16[608,128]{1,0:T(8,128)(2,1)S(1)}, bf16[608,128]{1,0:T(8,128)(2,1)S(1)}, u32[]{:S(2)}, u32[]{:S(2)}) collective-permute-start(bf16[608,128]{1,0:T(8,128)(2,1)S(1)} %collective-permute-done.8.refs_15_), channel_id=1, source_target_pairs={{0,1},{1,0},{2,3},{3,2},{4,5},{5,4},{6,7},{7,6},{8,9},{9,8},{10,11... | collective-permute-start | bytes 466952 | tf_op jit(solution)/shard_map/ppermute | solution.py:359
  20.2 0.6 %collective-permute-done.5.refs_12_ = bf16[608,128]{1,0:T(8,128)(2,1)S(1)} collective-permute-done((bf16[608,128]{1,0:T(8,128)(2,1)S(1)}, bf16[608,128]{1,0:T(8,128)(2,1)S(1)}, u32[]{:S(2)}, u32[]{:S(2)}) %collective-permute-start.5) | collective-permute-done | bytes 155680 | tf_op jit(solution)/shard_map/ppermute | solution.py:359
  20.8 0.3 %collective-permute-done.7.refs_14_ = bf16[608,128]{1,0:T(8,128)(2,1)S(1)} collective-permute-done((bf16[608,128]{1,0:T(8,128)(2,1)S(1)}, bf16[608,128]{1,0:T(8,128)(2,1)S(1)}, u32[]{:S(2)}, u32[]{:S(2)}) %collective-permute-start.7) | collective-permute-done | bytes 155680 | tf_op jit(solution)/shard_map/ppermute | solution.py:359
  21.1 0.0 collective-permute-done.4.refs_4_
  21.1 0.2 collective-permute-done.9.refs_16_
  21.3 0.0 copy-done
  21.3 0.0 copy-done.1
  21.3 0.0 copy-done.2
  21.4 4.9 %encode.1 = (f32[1,24]{1,0:T(1,128)}, f32[6,1,128]{2,1,0:T(1,128)}, f32[6,1,8]{2,1,0:T(1,128)}) custom-call(bf16[2,160,128]{2,1,0:T(8,128)(2,1)S(1)} %get-tuple-element.12.refs_0_, bf16[2,160,128]{2,1,0:T(8,128)(2,1)S(1)} %collective-permute-done.refs_1_, bf16[2,160,128]{2,1,0:T(8,128)(2,1)S(1)} %collective-permute-done.1.refs_2_, ...), custom_call_target="tpu_custom_call" | custom-call | tf_op jit(solution)/shard_map/encode/pallas_call | solution.py:401
  (2 shorter events, 0.0 us)
Async XLA Ops:
  0.6 6.9 %copy-start.4 = (bf16[1,192,16,384]{3,2,1,0:T(8,128)(2,1)S(1)}, bf16[1,192,16,384]{3,2,1,0:T(8,128)(2,1)}, u32[]{:S(2)}) copy-start(bf16[1,192,16,384]{3,2,1,0:T(8,128)(2,1)} %param.12) | copy-start | bytes 7077892
  1.8 17.3 %collective-permute-start.3 = (bf16[608,128]{1,0:T(8,128)(2,1)S(1)}, bf16[608,128]{1,0:T(8,128)(2,1)S(1)}, u32[]{:S(2)}, u32[]{:S(2)}) collective-permute-start(bf16[608,128]{1,0:T(8,128)(2,1)S(1)} %get-tuple-element.16.refs_9_), channel_id=1, source_target_pairs={{0,8},{8,0},{16,24},{24,16},{1,9},{9,1},{17,25},{25,17},{2,10},{10... | collective-permute-start | bytes 466952 | tf_op jit(solution)/shard_map/ppermute | solution.py:365
  4.9 9.8 %collective-permute-start.6 = (bf16[608,128]{1,0:T(8,128)(2,1)S(1)}, bf16[608,128]{1,0:T(8,128)(2,1)S(1)}, u32[]{:S(2)}, u32[]{:S(2)}) collective-permute-start(bf16[608,128]{1,0:T(8,128)(2,1)S(1)} %get-tuple-element.16.refs_9_), channel_id=1, source_target_pairs={{0,16},{8,24},{16,0},{24,8},{1,17},{9,25},{17,1},{25,9},{2,18},{10... | collective-permute-start | bytes 466952 | tf_op jit(solution)/shard_map/ppermute | solution.py:365
  10.7 10.7 %copy-start = (bf16[1024,128]{1,0:T(8,128)(2,1)S(1)}, bf16[1024,128]{1,0:T(8,128)(2,1)}, u32[]{:S(2)}) copy-start(bf16[1024,128]{1,0:T(8,128)(2,1)} %refs_6_.1) | copy-start | bytes 786436
  10.7 10.7 %copy-start.1 = (f32[128,8]{0,1:T(8,128)S(1)}, f32[128,8]{0,1:T(8,128)}, u32[]{:S(2)}) copy-start(f32[128,8]{0,1:T(8,128)} %param.23) | copy-start | bytes 12292
  10.7 10.6 %copy-start.2 = (s32[1,48,1]{1,2,0:T(1,128)S(1)}, s32[1,48,1]{1,2,0:T(1,128)}, u32[]{:S(2)}) copy-start(s32[1,48,1]{1,2,0:T(1,128)} %param.16) | copy-start | bytes 580
  10.7 10.6 %copy-start.3 = (f32[128]{0:T(128)S(1)}, f32[128]{0:T(128)}, u32[]{:S(2)}) copy-start(f32[128]{0:T(128)} %param.22) | copy-start | bytes 1540
  10.7 4.7 %collective-permute-start = (bf16[2,160,128]{2,1,0:T(8,128)(2,1)S(1)}, bf16[2,160,128]{2,1,0:T(8,128)(2,1)S(1)}, u32[]{:S(2)}, u32[]{:S(2)}) collective-permute-start(bf16[2,160,128]{2,1,0:T(8,128)(2,1)S(1)} %get-tuple-element.13), channel_id=1, source_target_pairs={{0,2},{1,3},{2,0},{3,1},{4,6},{5,7},{6,4},{7,5},{8,10},{9,11},{10,... | collective-permute-start | bytes 245768 | tf_op jit(solution)/shard_map/ppermute | solution.py:359
  12.3 5.3 %collective-permute-start.1 = (bf16[2,160,128]{2,1,0:T(8,128)(2,1)S(1)}, bf16[2,160,128]{2,1,0:T(8,128)(2,1)S(1)}, u32[]{:S(2)}, u32[]{:S(2)}) collective-permute-start(bf16[2,160,128]{2,1,0:T(8,128)(2,1)S(1)} %get-tuple-element.14), channel_id=1, source_target_pairs={{0,4},{1,5},{2,6},{3,7},{4,0},{5,1},{6,2},{7,3},{8,12},{9,13},{10,... | collective-permute-start | bytes 245768 | tf_op jit(solution)/shard_map/ppermute | solution.py:359
  13.8 5.3 %collective-permute-start.2 = (bf16[2,160,128]{2,1,0:T(8,128)(2,1)S(1)}, bf16[2,160,128]{2,1,0:T(8,128)(2,1)S(1)}, u32[]{:S(2)}, u32[]{:S(2)}) collective-permute-start(bf16[2,160,128]{2,1,0:T(8,128)(2,1)S(1)} %get-tuple-element.15), channel_id=1, source_target_pairs={{0,6},{1,7},{2,4},{3,5},{4,2},{5,3},{6,0},{7,1},{8,14},{9,15},{10,... | collective-permute-start | bytes 245768 | tf_op jit(solution)/shard_map/ppermute | solution.py:359
  14.7 5.2 %collective-permute-start.8 = (bf16[608,128]{1,0:T(8,128)(2,1)S(1)}, bf16[608,128]{1,0:T(8,128)(2,1)S(1)}, u32[]{:S(2)}, u32[]{:S(2)}) collective-permute-start(bf16[608,128]{1,0:T(8,128)(2,1)S(1)} %collective-permute-done.6.refs_13_), channel_id=1, source_target_pairs={{0,8},{8,0},{16,24},{24,16},{1,9},{9,1},{17,25},{25,17},{2,10},{10... | collective-permute-start | bytes 466952 | tf_op jit(solution)/shard_map/ppermute | solution.py:365
  19.2 2.0 %collective-permute-start.4 = (bf16[640,128]{1,0:T(8,128)(2,1)S(1)}, bf16[640,128]{1,0:T(8,128)(2,1)S(1)}, u32[]{:S(2)}, u32[]{:S(2)}) collective-permute-start(bf16[640,128]{1,0:T(8,128)(2,1)S(1)} %bundle.1), channel_id=1, source_target_pairs={{0,1},{1,0},{2,3},{3,2},{4,5},{5,4},{6,7},{7,6},{8,9},{9,8},{10,11... | collective-permute-start | bytes 491528 | tf_op jit(solution)/shard_map/ppermute | solution.py:359
  19.2 1.6 %collective-permute-start.5 = (bf16[608,128]{1,0:T(8,128)(2,1)S(1)}, bf16[608,128]{1,0:T(8,128)(2,1)S(1)}, u32[]{:S(2)}, u32[]{:S(2)}) collective-permute-start(bf16[608,128]{1,0:T(8,128)(2,1)S(1)} %collective-permute-done.3.refs_4_.refs_11_), channel_id=1, source_target_pairs={{0,1},{1,0},{2,3},{3,2},{4,5},{5,4},{6,7},{7,6},{8,9},{9,8},{10,11... | collective-permute-start | bytes 466952 | tf_op jit(solution)/shard_map/ppermute | solution.py:359
  19.7 1.4 %collective-permute-start.7 = (bf16[608,128]{1,0:T(8,128)(2,1)S(1)}, bf16[608,128]{1,0:T(8,128)(2,1)S(1)}, u32[]{:S(2)}, u32[]{:S(2)}) collective-permute-start(bf16[608,128]{1,0:T(8,128)(2,1)S(1)} %collective-permute-done.6.refs_13_), channel_id=1, source_target_pairs={{0,1},{1,0},{2,3},{3,2},{4,5},{5,4},{6,7},{7,6},{8,9},{9,8},{10,11... | collective-permute-start | bytes 466952 | tf_op jit(solution)/shard_map/ppermute | solution.py:359
  19.9 1.4 %collective-permute-start.9 = (bf16[608,128]{1,0:T(8,128)(2,1)S(1)}, bf16[608,128]{1,0:T(8,128)(2,1)S(1)}, u32[]{:S(2)}, u32[]{:S(2)}) collective-permute-start(bf16[608,128]{1,0:T(8,128)(2,1)S(1)} %collective-permute-done.8.refs_15_), channel_id=1, source_target_pairs={{0,1},{1,0},{2,3},{3,2},{4,5},{5,4},{6,7},{7,6},{8,9},{9,8},{10,11... | collective-permute-start | bytes 466952 | tf_op jit(solution)/shard_map/ppermute | solution.py:359

commit v5 on v4

--- a/solution.py
+++ b/solution.py
@@ -27,10 +27,9 @@
     return half + half * jnp.tanh(x * (GELU_A + GELU_B * (x * x)))
 
 
-def gelu_narrow(x):
+def double_gelu(x):
     x = x.astype(BF16)
-    half = x * BF16(0.5)
-    return half + half * jnp.tanh(x * (BF16(GELU_A) + BF16(GELU_B) * (x * x)))
+    return x + x * jnp.tanh(x * (BF16(GELU_A) + BF16(GELU_B) * (x * x)))
 
 
 def rms_norm(values):
@@ -91,7 +90,8 @@
     features, out = refs[:chips], refs[-1]
     other = 1 - lax.axis_index("mod") % 2
     size = features[0].shape[1]
-    for n, ref in enumerate(features):
+    for place, ref in enumerate(features):
+        n = chips - 1 - place
         out[n * size : (n + 1) * size, :] = ref[other]
 
 
@@ -168,7 +168,7 @@
     pick = (iota((frames, hits), 0) == hit_row[...]).astype(F32).T.astype(BF16)
     sums = jnp.zeros((frames, channels), F32)
     spots = [(n, j) for n in range(quads) for j in range(blocks)]
-    parts = [gelu_narrow(dot(rows[(n * blocks + j) * frames : (n * blocks + j + 1) * frames, :], wide[...])) for n, j in spots]
+    parts = [double_gelu(dot(rows[(n * blocks + j) * frames : (n * blocks + j + 1) * frames, :], wide[...])) for n, j in spots]
     for part in parts:
         sums = sums + part[:, :channels].astype(F32) + part[:, channels:].astype(F32)
     takens = [dot(pick, part.astype(BF16)) for part in parts]
@@ -177,13 +177,13 @@
             chosen[pl.ds(j * 2 * quads + 2 * n + k, hits, stride=tokens), :] = taken[
                 :, k * channels : (k + 1) * channels
             ]
-    scale = jnp.broadcast_to(veto_rows[pl.ds(lax.axis_index("mod"), 1), :] / tokens, (VETO_ROWS, channels))
+    scale = jnp.broadcast_to(veto_rows[pl.ds(lax.axis_index("mod"), 1), :] / (2 * tokens), (VETO_ROWS, channels))
     row = iota((VETO_ROWS, owned), 0)
     totals[...] = sums
     for k in range(owners // 2):
         for core in range(2):
             o = ((lax.axis_index("mod") // 2) ^ k) * 2 + core
-            taken = chosen[pl.ds(pl.multiple_of(o * hit_rows, 8), hit_rows), :]
+            taken = 0.5 * chosen[pl.ds(pl.multiple_of(o * hit_rows, 8), hit_rows), :]
             out[k][core, 0:hit_rows, :] = taken.astype(BF16)
             veto = lax.dot_general(
                 scale,
@@ -200,7 +200,7 @@
 
 def encode_kernel(owners, streams, width, hidden, *refs):
     chips = owners // 2
-    received, bundle, refs = refs[:chips], refs[chips], refs[chips + 1 :]
+    received, bundle, refs = refs[:chips][::-1], refs[chips], refs[chips + 1 :]
     targets, readout, gain, class_weight = refs[:4]
     halves = refs[4 : 4 + 2 * streams]
     veto, latents, scores, table, pools = refs[4 + 2 * streams :]
@@ -245,10 +245,10 @@
 
     def mix_in(slot, wide):
         token_in = widen(slot, 0).astype(F32).T.astype(BF16)
-        return gelu_narrow(dot(token_in, wide))
+        return double_gelu(dot(token_in, wide))
 
     def mix_out(slot, x, mixed):
-        back = dot(widen(slot, 1), mixed)
+        back = 0.5 * dot(widen(slot, 1), mixed)
         after = jnp.concatenate(
             [x[r] + back[:width, r * channels : (r + 1) * channels] for r in range(owners)], axis=0
         )
@@ -258,10 +258,10 @@
         chan_in = jnp.concatenate(
             [table[slot, 0, j * channels : (j + 1) * channels, :] for j in range(hidden // channels)], axis=1
         )
-        return gelu_narrow(dot(rms_norm(after).astype(BF16), chan_in))
+        return double_gelu(dot(rms_norm(after).astype(BF16), chan_in))
 
     def channel_out(slot, after, inner):
-        last = after + dot(inner, table[slot, 1, 0:hidden, :])
+        last = after + 0.5 * dot(inner, table[slot, 1, 0:hidden, :])
         pool = jnp.sum(last.reshape(owners, width, channels), axis=1) * (1.0 / width)
         pools[pl.ds(pl.multiple_of(slot * owners, owners), owners), :] = pool
 
@@ -392,7 +392,7 @@
         out_specs=vmem(1)[0],
         compiler_params=pltpu.CompilerParams(vmem_limit_bytes=PACK_VMEM_BYTES),
         cost_estimate=pl.CostEstimate(flops=1_000_000_000, bytes_accessed=1_000_000, transcendentals=0),
-    )(*[in_vmem(x) for x in received], in_vmem(got[1]))
+    )(*[in_vmem(x) for x in received[::-1]], in_vmem(got[1]))
     bundle = cross(bundle, 1)
     halves = [mine, other]
     for k in range(1, streams):
@@ -415,7 +415,7 @@
             pltpu.VMEM((8 * owners, channels), F32),
         ],
         compiler_params=pltpu.CompilerParams(vmem_limit_bytes=ENCODE_VMEM_BYTES),
-    )(*received, bundle, assign.reshape(hits), readout, latent_gain.reshape(1, channels), class_weight.T, *halves)
+    )(*received[::-1], bundle, assign.reshape(hits), readout, latent_gain.reshape(1, channels), class_weight.T, *halves)
     return (veto, jnp.swapaxes(latents, 0, 1), jnp.swapaxes(scores, 0, 1))
 
 

time: 26.4 us -> 26.1 us (0.989)
  starting transfers between devices: 10.7 us -> 10.3 us
  waiting for transfers between devices: 5.59 us -> 5.9 us
    ppermute x3, waiting for transfers between devices: 0.49 us -> 1.5 us  [local(): got[k] = lax.ppermute(got[k ^ low], 'stream', pairs)]
    ppermute x7, waiting for transfers between devices: 5.1 us -> 4.4 us  [cross(): return lax.ppermute(x, 'mod', [(i, i ^ distance) for i in range(owners)])]
    ppermute x7, starting transfers between devices: 4.54 us -> 4.2 us  [cross(): return lax.ppermute(x, 'mod', [(i, i ^ distance) for i in range(owners)])]
  transfers between devices with their start and end apart: 10 -> 10, of which waited for: 8 -> 7; matrix products, arithmetic and copies ran while one was open for 0% -> 0% of each run, Pallas kernels for 12% -> 12%
where the time goes in v5:
time: 26.1 us; the launch traced here: 26 us
  starting transfers between devices  10.3 us (39%)
  Pallas kernels  9.02 us (35%)
  waiting for transfers between devices  5.9 us (23%)
  between operations  0.72 us (3%)
    ppermute x3, starting transfers between devices, local(): got[k] = lax.ppermute(got[k ^ low], 'stream', pairs)  6.13 us
    pallas_call x1, Pallas kernels, local(): pl.pallas_call(functools.partial(encode_kernel, owners, streams, width, h...  4.69 us
    ppermute x7, waiting for transfers between devices, cross(): return lax.ppermute(x, 'mod', [(i, i ^ distance) for i in range(owners)])  4.4 us
    ppermute x7, starting transfers between devices, cross(): return lax.ppermute(x, 'mod', [(i, i ^ distance) for i in range(owners)])  4.2 us
    pallas_call x1, Pallas kernels, local(): pl.pallas_call(stem_kernel, name='stem', out_shape=(pltpu.VMEM((2, hit_ro...  3.15 us
    ppermute x3, waiting for transfers between devices, local(): got[k] = lax.ppermute(got[k ^ low], 'stream', pairs)  1.5 us
    pallas_call x1, Pallas kernels, local(): pl.pallas_call(pack_kernel, name='pack', out_shape=(half, half), in_specs...  1.16 us
  transfers between devices with their start and end apart: 10, of which 7 were waited for; matrix products, arithmetic and copies ran while one was open for 0% of the time, Pallas kernels for 12%

profile of v5, /device:TPU:0, one launch (start us, length us, event | category | flops | bytes accessed | tf_op | source)
XLA Modules:
  0.0 26.0 jit_solution(4683188105582394874)
XLA Ops:
  0.6 0.0 copy-start.4
  0.6 1.2 %pack.1 = (bf16[608,128]{1,0:T(8,128)(2,1)S(1)}, bf16[608,128]{1,0:T(8,128)(2,1)S(1)}) custom-call(bf16[24,384]{1,0:T(8,128)(2,1)} %bitcast.18, bf16[24,384]{1,0:T(8,128)(2,1)} %bitcast.19, bf16[128,512]{1,0:T(8,128)(2,1)} %bitcast.16, bf16[512,128]{1,0:T(8,128)(2,1)} %bitcast.17), custom_call_target="tpu_custom_call" | custom-call | flops 5000000000 | bytes 3000000 | tf_op jit(solution)/shard_map/pack/pallas_call | solution.py:343
  1.8 3.1 %collective-permute-start.3 = (bf16[608,128]{1,0:T(8,128)(2,1)S(1)}, bf16[608,128]{1,0:T(8,128)(2,1)S(1)}, u32[]{:S(2)}, u32[]{:S(2)}) collective-permute-start(bf16[608,128]{1,0:T(8,128)(2,1)S(1)} %get-tuple-element.16.refs_9_), channel_id=1, source_target_pairs={{0,8},{8,0},{16,24},{24,16},{1,9},{9,1},{17,25},{25,17},{2,10},{10... | collective-permute-start | bytes 466952 | tf_op jit(solution)/shard_map/ppermute | solution.py:365
  4.9 2.6 %collective-permute-start.6 = (bf16[608,128]{1,0:T(8,128)(2,1)S(1)}, bf16[608,128]{1,0:T(8,128)(2,1)S(1)}, u32[]{:S(2)}, u32[]{:S(2)}) collective-permute-start(bf16[608,128]{1,0:T(8,128)(2,1)S(1)} %get-tuple-element.16.refs_9_), channel_id=1, source_target_pairs={{0,16},{8,24},{16,0},{24,8},{1,17},{9,25},{17,1},{25,9},{2,18},{10... | collective-permute-start | bytes 466952 | tf_op jit(solution)/shard_map/ppermute | solution.py:365
  7.5 0.0 copy-done.4
  7.5 3.2 %stem.1 = (bf16[2,160,128]{2,1,0:T(8,128)(2,1)S(1)}, bf16[2,160,128]{2,1,0:T(8,128)(2,1)S(1)}, bf16[2,160,128]{2,1,0:T(8,128)(2,1)S(1)}, bf16[2,160,128]{2,1,0:T(8,128)(2,1)S(1)}) custom-call(bf16[192,16,384]{2,1,0:T(8,128)(2,1)S(1)} %bitcast.15, bf16[256,128]{1,0:T(8,128)(2,1)} %weight.1, f32[8,128]{1,0:T(8,128)} %veto_weight.1, s32[1,48]{1,0:T(1,128)} %hit_frames.1), custom_call_target="tpu_custom_call" | custom-call | flops 5000000000 | bytes 3000000 | tf_op jit(solution)/shard_map/stem/pallas_call | solution.py:367
  10.7 0.0 copy-start
  10.7 0.0 copy-start.1
  10.7 0.0 copy-start.2
  10.7 0.0 copy-start.3
  10.7 2.5 %collective-permute-start = (bf16[2,160,128]{2,1,0:T(8,128)(2,1)S(1)}, bf16[2,160,128]{2,1,0:T(8,128)(2,1)S(1)}, u32[]{:S(2)}, u32[]{:S(2)}) collective-permute-start(bf16[2,160,128]{2,1,0:T(8,128)(2,1)S(1)} %get-tuple-element.12), channel_id=1, source_target_pairs={{0,6},{1,7},{2,4},{3,5},{4,2},{5,3},{6,0},{7,1},{8,14},{9,15},{10,... | collective-permute-start | bytes 245768 | tf_op jit(solution)/shard_map/ppermute | solution.py:359
  13.2 0.5 %collective-permute-start.1 = (bf16[2,160,128]{2,1,0:T(8,128)(2,1)S(1)}, bf16[2,160,128]{2,1,0:T(8,128)(2,1)S(1)}, u32[]{:S(2)}, u32[]{:S(2)}) collective-permute-start(bf16[2,160,128]{2,1,0:T(8,128)(2,1)S(1)} %get-tuple-element.13), channel_id=1, source_target_pairs={{0,4},{1,5},{2,6},{3,7},{4,0},{5,1},{6,2},{7,3},{8,12},{9,13},{10,... | collective-permute-start | bytes 245768 | tf_op jit(solution)/shard_map/ppermute | solution.py:359
  13.7 0.6 %collective-permute-start.2 = (bf16[2,160,128]{2,1,0:T(8,128)(2,1)S(1)}, bf16[2,160,128]{2,1,0:T(8,128)(2,1)S(1)}, u32[]{:S(2)}, u32[]{:S(2)}) collective-permute-start(bf16[2,160,128]{2,1,0:T(8,128)(2,1)S(1)} %get-tuple-element.14), channel_id=1, source_target_pairs={{0,2},{1,3},{2,0},{3,1},{4,6},{5,7},{6,4},{7,5},{8,10},{9,11},{10,... | collective-permute-start | bytes 245768 | tf_op jit(solution)/shard_map/ppermute | solution.py:359
  14.3 0.4 %collective-permute-done.6.refs_13_ = bf16[608,128]{1,0:T(8,128)(2,1)S(1)} collective-permute-done((bf16[608,128]{1,0:T(8,128)(2,1)S(1)}, bf16[608,128]{1,0:T(8,128)(2,1)S(1)}, u32[]{:S(2)}, u32[]{:S(2)}) %collective-permute-start.6) | collective-permute-done | bytes 155680 | tf_op jit(solution)/shard_map/ppermute | solution.py:365
  14.7 0.4 %collective-permute-start.8 = (bf16[608,128]{1,0:T(8,128)(2,1)S(1)}, bf16[608,128]{1,0:T(8,128)(2,1)S(1)}, u32[]{:S(2)}, u32[]{:S(2)}) collective-permute-start(bf16[608,128]{1,0:T(8,128)(2,1)S(1)} %collective-permute-done.6.refs_13_), channel_id=1, source_target_pairs={{0,8},{8,0},{16,24},{24,16},{1,9},{9,1},{17,25},{25,17},{2,10},{10... | collective-permute-start | bytes 466952 | tf_op jit(solution)/shard_map/ppermute | solution.py:365
  15.1 1.2 %collective-permute-done.refs_0_ = bf16[2,160,128]{2,1,0:T(8,128)(2,1)S(1)} collective-permute-done((bf16[2,160,128]{2,1,0:T(8,128)(2,1)S(1)}, bf16[2,160,128]{2,1,0:T(8,128)(2,1)S(1)}, u32[]{:S(2)}, u32[]{:S(2)}) %collective-permute-start) | collective-permute-done | bytes 81952 | tf_op jit(solution)/shard_map/ppermute | solution.py:359
  16.3 1.4 %collective-permute-done.1.refs_1_ = bf16[2,160,128]{2,1,0:T(8,128)(2,1)S(1)} collective-permute-done((bf16[2,160,128]{2,1,0:T(8,128)(2,1)S(1)}, bf16[2,160,128]{2,1,0:T(8,128)(2,1)S(1)}, u32[]{:S(2)}, u32[]{:S(2)}) %collective-permute-start.1) | collective-permute-done | bytes 81952 | tf_op jit(solution)/shard_map/ppermute | solution.py:359
  17.7 0.5 %collective-permute-done.2.refs_2_ = bf16[2,160,128]{2,1,0:T(8,128)(2,1)S(1)} collective-permute-done((bf16[2,160,128]{2,1,0:T(8,128)(2,1)S(1)}, bf16[2,160,128]{2,1,0:T(8,128)(2,1)S(1)}, u32[]{:S(2)}, u32[]{:S(2)}) %collective-permute-start.2) | collective-permute-done | bytes 81952 | tf_op jit(solution)/shard_map/ppermute | solution.py:359
  18.1 0.0 collective-permute-done.3.refs_4_.refs_11_
  18.2 0.1 collective-permute-start.4
  18.2 0.5 %collective-permute-start.5 = (bf16[608,128]{1,0:T(8,128)(2,1)S(1)}, bf16[608,128]{1,0:T(8,128)(2,1)S(1)}, u32[]{:S(2)}, u32[]{:S(2)}) collective-permute-start(bf16[608,128]{1,0:T(8,128)(2,1)S(1)} %collective-permute-done.3.refs_4_.refs_11_), channel_id=1, source_target_pairs={{0,1},{1,0},{2,3},{3,2},{4,5},{5,4},{6,7},{7,6},{8,9},{9,8},{10,11... | collective-permute-start | bytes 466952 | tf_op jit(solution)/shard_map/ppermute | solution.py:359
  18.7 0.1 collective-permute-start.7
  18.8 1.1 %collective-permute-done.8.refs_15_ = bf16[608,128]{1,0:T(8,128)(2,1)S(1)} collective-permute-done((bf16[608,128]{1,0:T(8,128)(2,1)S(1)}, bf16[608,128]{1,0:T(8,128)(2,1)S(1)}, u32[]{:S(2)}, u32[]{:S(2)}) %collective-permute-start.8) | collective-permute-done | bytes 155680 | tf_op jit(solution)/shard_map/ppermute | solution.py:365
  19.9 0.0 collective-permute-start.9
  19.9 0.0 collective-permute-done.5.refs_12_
  19.9 0.2 collective-permute-done.7.refs_14_
  20.1 0.0 collective-permute-done.4.refs_4_
  20.1 1.2 %collective-permute-done.9.refs_16_ = bf16[608,128]{1,0:T(8,128)(2,1)S(1)} collective-permute-done((bf16[608,128]{1,0:T(8,128)(2,1)S(1)}, bf16[608,128]{1,0:T(8,128)(2,1)S(1)}, u32[]{:S(2)}, u32[]{:S(2)}) %collective-permute-start.9) | collective-permute-done | bytes 155680 | tf_op jit(solution)/shard_map/ppermute | solution.py:359
  21.3 0.0 copy-done
  21.3 0.0 copy-done.1
  21.3 0.0 copy-done.2
  21.3 4.7 %encode.1 = (f32[1,24]{1,0:T(1,128)}, f32[6,1,128]{2,1,0:T(1,128)}, f32[6,1,8]{2,1,0:T(1,128)}) custom-call(bf16[2,160,128]{2,1,0:T(8,128)(2,1)S(1)} %collective-permute-done.refs_0_, bf16[2,160,128]{2,1,0:T(8,128)(2,1)S(1)} %collective-permute-done.1.refs_1_, bf16[2,160,128]{2,1,0:T(8,128)(2,1)S(1)} %collective-permute-done.2.refs_2_, ...), custom_call_target="tpu_custom_call" | custom-call | tf_op jit(solution)/shard_map/encode/pallas_call | solution.py:401
  (2 shorter events, 0.0 us)
Async XLA Ops:
  0.6 6.9 %copy-start.4 = (bf16[1,192,16,384]{3,2,1,0:T(8,128)(2,1)S(1)}, bf16[1,192,16,384]{3,2,1,0:T(8,128)(2,1)}, u32[]{:S(2)}) copy-start(bf16[1,192,16,384]{3,2,1,0:T(8,128)(2,1)} %param.12) | copy-start | bytes 7077892
  1.8 16.3 %collective-permute-start.3 = (bf16[608,128]{1,0:T(8,128)(2,1)S(1)}, bf16[608,128]{1,0:T(8,128)(2,1)S(1)}, u32[]{:S(2)}, u32[]{:S(2)}) collective-permute-start(bf16[608,128]{1,0:T(8,128)(2,1)S(1)} %get-tuple-element.16.refs_9_), channel_id=1, source_target_pairs={{0,8},{8,0},{16,24},{24,16},{1,9},{9,1},{17,25},{25,17},{2,10},{10... | collective-permute-start | bytes 466952 | tf_op jit(solution)/shard_map/ppermute | solution.py:365
  4.9 9.8 %collective-permute-start.6 = (bf16[608,128]{1,0:T(8,128)(2,1)S(1)}, bf16[608,128]{1,0:T(8,128)(2,1)S(1)}, u32[]{:S(2)}, u32[]{:S(2)}) collective-permute-start(bf16[608,128]{1,0:T(8,128)(2,1)S(1)} %get-tuple-element.16.refs_9_), channel_id=1, source_target_pairs={{0,16},{8,24},{16,0},{24,8},{1,17},{9,25},{17,1},{25,9},{2,18},{10... | collective-permute-start | bytes 466952 | tf_op jit(solution)/shard_map/ppermute | solution.py:365
  10.7 10.6 %copy-start = (bf16[1024,128]{1,0:T(8,128)(2,1)S(1)}, bf16[1024,128]{1,0:T(8,128)(2,1)}, u32[]{:S(2)}) copy-start(bf16[1024,128]{1,0:T(8,128)(2,1)} %refs_6_.1) | copy-start | bytes 786436
  10.7 10.6 %copy-start.1 = (f32[128,8]{0,1:T(8,128)S(1)}, f32[128,8]{0,1:T(8,128)}, u32[]{:S(2)}) copy-start(f32[128,8]{0,1:T(8,128)} %param.23) | copy-start | bytes 12292
  10.7 10.6 %copy-start.2 = (s32[1,48,1]{1,2,0:T(1,128)S(1)}, s32[1,48,1]{1,2,0:T(1,128)}, u32[]{:S(2)}) copy-start(s32[1,48,1]{1,2,0:T(1,128)} %param.16) | copy-start | bytes 580
  10.7 10.6 %copy-start.3 = (f32[128]{0:T(128)S(1)}, f32[128]{0:T(128)}, u32[]{:S(2)}) copy-start(f32[128]{0:T(128)} %param.22) | copy-start | bytes 1540
  10.7 5.6 %collective-permute-start = (bf16[2,160,128]{2,1,0:T(8,128)(2,1)S(1)}, bf16[2,160,128]{2,1,0:T(8,128)(2,1)S(1)}, u32[]{:S(2)}, u32[]{:S(2)}) collective-permute-start(bf16[2,160,128]{2,1,0:T(8,128)(2,1)S(1)} %get-tuple-element.12), channel_id=1, source_target_pairs={{0,6},{1,7},{2,4},{3,5},{4,2},{5,3},{6,0},{7,1},{8,14},{9,15},{10,... | collective-permute-start | bytes 245768 | tf_op jit(solution)/shard_map/ppermute | solution.py:359
  13.2 4.4 %collective-permute-start.1 = (bf16[2,160,128]{2,1,0:T(8,128)(2,1)S(1)}, bf16[2,160,128]{2,1,0:T(8,128)(2,1)S(1)}, u32[]{:S(2)}, u32[]{:S(2)}) collective-permute-start(bf16[2,160,128]{2,1,0:T(8,128)(2,1)S(1)} %get-tuple-element.13), channel_id=1, source_target_pairs={{0,4},{1,5},{2,6},{3,7},{4,0},{5,1},{6,2},{7,3},{8,12},{9,13},{10,... | collective-permute-start | bytes 245768 | tf_op jit(solution)/shard_map/ppermute | solution.py:359
  13.7 4.4 %collective-permute-start.2 = (bf16[2,160,128]{2,1,0:T(8,128)(2,1)S(1)}, bf16[2,160,128]{2,1,0:T(8,128)(2,1)S(1)}, u32[]{:S(2)}, u32[]{:S(2)}) collective-permute-start(bf16[2,160,128]{2,1,0:T(8,128)(2,1)S(1)} %get-tuple-element.14), channel_id=1, source_target_pairs={{0,2},{1,3},{2,0},{3,1},{4,6},{5,7},{6,4},{7,5},{8,10},{9,11},{10,... | collective-permute-start | bytes 245768 | tf_op jit(solution)/shard_map/ppermute | solution.py:359
  14.7 5.2 %collective-permute-start.8 = (bf16[608,128]{1,0:T(8,128)(2,1)S(1)}, bf16[608,128]{1,0:T(8,128)(2,1)S(1)}, u32[]{:S(2)}, u32[]{:S(2)}) collective-permute-start(bf16[608,128]{1,0:T(8,128)(2,1)S(1)} %collective-permute-done.6.refs_13_), channel_id=1, source_target_pairs={{0,8},{8,0},{16,24},{24,16},{1,9},{9,1},{17,25},{25,17},{2,10},{10... | collective-permute-start | bytes 466952 | tf_op jit(solution)/shard_map/ppermute | solution.py:365
  18.2 2.0 %collective-permute-start.4 = (bf16[640,128]{1,0:T(8,128)(2,1)S(1)}, bf16[640,128]{1,0:T(8,128)(2,1)S(1)}, u32[]{:S(2)}, u32[]{:S(2)}) collective-permute-start(bf16[640,128]{1,0:T(8,128)(2,1)S(1)} %bundle.1), channel_id=1, source_target_pairs={{0,1},{1,0},{2,3},{3,2},{4,5},{5,4},{6,7},{7,6},{8,9},{9,8},{10,11... | collective-permute-start | bytes 491528 | tf_op jit(solution)/shard_map/ppermute | solution.py:359
  18.2 1.7 %collective-permute-start.5 = (bf16[608,128]{1,0:T(8,128)(2,1)S(1)}, bf16[608,128]{1,0:T(8,128)(2,1)S(1)}, u32[]{:S(2)}, u32[]{:S(2)}) collective-permute-start(bf16[608,128]{1,0:T(8,128)(2,1)S(1)} %collective-permute-done.3.refs_4_.refs_11_), channel_id=1, source_target_pairs={{0,1},{1,0},{2,3},{3,2},{4,5},{5,4},{6,7},{7,6},{8,9},{9,8},{10,11... | collective-permute-start | bytes 466952 | tf_op jit(solution)/shard_map/ppermute | solution.py:359
  18.7 1.4 %collective-permute-start.7 = (bf16[608,128]{1,0:T(8,128)(2,1)S(1)}, bf16[608,128]{1,0:T(8,128)(2,1)S(1)}, u32[]{:S(2)}, u32[]{:S(2)}) collective-permute-start(bf16[608,128]{1,0:T(8,128)(2,1)S(1)} %collective-permute-done.6.refs_13_), channel_id=1, source_target_pairs={{0,1},{1,0},{2,3},{3,2},{4,5},{5,4},{6,7},{7,6},{8,9},{9,8},{10,11... | collective-permute-start | bytes 466952 | tf_op jit(solution)/shard_map/ppermute | solution.py:359
  19.9 1.4 %collective-permute-start.9 = (bf16[608,128]{1,0:T(8,128)(2,1)S(1)}, bf16[608,128]{1,0:T(8,128)(2,1)S(1)}, u32[]{:S(2)}, u32[]{:S(2)}) collective-permute-start(bf16[608,128]{1,0:T(8,128)(2,1)S(1)} %collective-permute-done.8.refs_15_), channel_id=1, source_target_pairs={{0,1},{1,0},{2,3},{3,2},{4,5},{5,4},{6,7},{7,6},{8,9},{9,8},{10,11... | collective-permute-start | bytes 466952 | tf_op jit(solution)/shard_map/ppermute | solution.py:359

commit v6 on v5

--- a/solution.py
+++ b/solution.py
@@ -198,12 +198,33 @@
             out[k][core, hit_rows : hit_rows + VETO_ROWS, :] = both.astype(BF16)
 
 
+def prepare_kernel(width, *refs):
+    chips = len(refs) - 3
+    received, bundle, wides, veto = refs[:chips][::-1], refs[chips], refs[chips + 1], refs[chips + 2]
+    core = lax.axis_index("mod") % 2
+    hits = wides.shape[0]
+    channels = received[0].shape[2]
+    hit_rows = hits * width
+    block = hit_rows + VETO_ROWS
+    gap = jnp.zeros((hits, PAD_ROW - width, channels), F32)
+    for n, ref in enumerate(received):
+        parts = (ref[core, 0:hit_rows, :], bundle[n * block : n * block + hit_rows, :])
+        for c, part in enumerate(parts):
+            normed = rms_norm(part.astype(F32).reshape(hits, width, channels))
+            r = 2 * n + c
+            wides[:, :, r * channels : (r + 1) * channels] = jnp.concatenate([normed, gap], axis=1).astype(BF16)
+    tails = [ref[core, hit_rows:block, :] for ref in received]
+    tails += [bundle[n * block + hit_rows : (n + 1) * block, :] for n in range(chips)]
+    terms = sum(tail.astype(F32) for tail in tails)
+    veto[...] = jnp.sum(terms, axis=0, keepdims=True)[:, : veto.shape[1]]
+
+
 def encode_kernel(owners, streams, width, hidden, *refs):
     chips = owners // 2
-    received, bundle, refs = refs[:chips][::-1], refs[chips], refs[chips + 1 :]
+    received, bundle, wides, refs = refs[:chips][::-1], refs[chips], refs[chips + 1], refs[chips + 2 :]
     targets, readout, gain, class_weight = refs[:4]
     halves = refs[4 : 4 + 2 * streams]
-    veto, latents, scores, table, pools = refs[4 + 2 * streams :]
+    latents, scores, table, pools = refs[4 + 2 * streams :]
     channels = received[0].shape[2]
     hits = latents.shape[0]
     hit_rows = hits * width
@@ -222,30 +243,19 @@
                 table[slot, core] = halves[2 * k][...]
                 table[slot, 1 - core] = halves[2 * k + 1][...]
 
-    tails = [ref[core, hit_rows:block, :] for ref in received]
-    tails += [bundle[n * block + hit_rows : (n + 1) * block, :] for n in range(chips)]
-    terms = sum(tail.astype(F32) for tail in tails)
-    veto[...] = jnp.sum(terms, axis=0, keepdims=True)[:, : veto.shape[1]]
     pools[...] = jnp.zeros_like(pools)
 
     extra = table.shape[2] - hidden
     blocks = extra // PAD_ROW
-    gap = jnp.zeros((PAD_ROW - width, channels), F32)
 
     def widen(slot, half):
         return jnp.concatenate(
             [table[slot, half, hidden + j * PAD_ROW : hidden + (j + 1) * PAD_ROW, :] for j in range(blocks)], axis=1
         )
 
-    def spread(x):
-        normed = rms_norm(x)
-        return jnp.concatenate(
-            [jnp.concatenate([normed[r], gap], axis=0).astype(BF16) for r in range(owners)], axis=1
-        )
-
-    def mix_in(slot, wide):
+    def mix_in(slot):
         token_in = widen(slot, 0).astype(F32).T.astype(BF16)
-        return double_gelu(dot(token_in, wide))
+        return double_gelu(dot(token_in, wides[slot]))
 
     def mix_out(slot, x, mixed):
         back = 0.5 * dot(widen(slot, 1), mixed)
@@ -278,8 +288,7 @@
         every = jnp.stack(every)
         slots = [first + a for a in range(group)]
         x = [every[:, a * width : (a + 1) * width] for a in range(group)]
-        wide = [spread(v) for v in x]
-        mixed = [mix_in(n, v) for n, v in zip(slots, wide)]
+        mixed = [mix_in(n) for n in slots]
         after = [mix_out(n, v, m) for n, v, m in zip(slots, x, mixed)]
         inner = [channel_in(n, v) for n, v in zip(slots, after)]
         for n, v, m in zip(slots, after, inner):
@@ -398,24 +407,34 @@
     for k in range(1, streams):
         halves += [got[k], cross(got[k], 1)]
 
-    veto, latents, scores = pl.pallas_call(
+    wides, veto = pl.pallas_call(
+        functools.partial(prepare_kernel, width),
+        name="prepare",
+        out_shape=(
+            pltpu.VMEM((hits_owned, PAD_ROW, owners * channels), BF16),
+            jax.ShapeDtypeStruct((1, frames // owners), F32),
+        ),
+        in_specs=vmem(chips + 1),
+        out_specs=tuple(vmem(2)),
+        compiler_params=pltpu.CompilerParams(vmem_limit_bytes=PACK_VMEM_BYTES),
+    )(*received[::-1], bundle)
+    latents, scores = pl.pallas_call(
         functools.partial(encode_kernel, owners, streams, width, hidden),
         name="encode",
         out_shape=(
-            jax.ShapeDtypeStruct((1, frames // owners), F32),
             jax.ShapeDtypeStruct((hits_owned, 1, channels), F32),
             jax.ShapeDtypeStruct((hits_owned, 1, class_weight.shape[1]), F32),
         ),
-        in_specs=vmem(chips + 1)
+        in_specs=vmem(chips + 2)
         + [pl.BlockSpec(memory_space=pltpu.SMEM)]
         + vmem(3 + len(halves)),
-        out_specs=tuple(vmem(3)),
+        out_specs=tuple(vmem(2)),
         scratch_shapes=[
             pltpu.VMEM((hits_owned, 2, half_rows, LANES), BF16),
             pltpu.VMEM((8 * owners, channels), F32),
         ],
         compiler_params=pltpu.CompilerParams(vmem_limit_bytes=ENCODE_VMEM_BYTES),
-    )(*received[::-1], bundle, assign.reshape(hits), readout, latent_gain.reshape(1, channels), class_weight.T, *halves)
+    )(*received[::-1], bundle, wides, assign.reshape(hits), readout, latent_gain.reshape(1, channels), class_weight.T, *halves)
     return (veto, jnp.swapaxes(latents, 0, 1), jnp.swapaxes(scores, 0, 1))
 
 

time: 26.1 us -> 25.6 us (0.981)
  waiting for transfers between devices: 5.9 us -> 4.81 us
  Pallas kernels: 9.02 us -> 9.61 us
    ppermute x3, waiting for transfers between devices: 1.5 us -> 0.68 us  [local(): got[k] = lax.ppermute(got[k ^ low], 'stream', pairs)]
    pallas_call x0 -> x1, Pallas kernels: none -> 0.7 us  [local(): pl.pallas_call(functools.partial(prepare_kernel, width), name='prepare',...]
    ppermute x7, waiting for transfers between devices: 4.4 us -> 4.13 us  [cross(): return lax.ppermute(x, 'mod', [(i, i ^ distance) for i in range(owners)])]
  transfers between devices with their start and end apart: 10 -> 10, of which waited for: 7 -> 6; matrix products, arithmetic and copies ran while one was open for 0% -> 0% of each run, Pallas kernels for 12% -> 15%
where the time goes in v6:
time: 25.6 us; the launch traced here: 25.5 us
  starting transfers between devices  10.3 us (40%)
  Pallas kernels  9.61 us (38%)
  waiting for transfers between devices  4.81 us (19%)
  between operations  0.72 us (3%)
    ppermute x3, starting transfers between devices, local(): got[k] = lax.ppermute(got[k ^ low], 'stream', pairs)  6.11 us
    pallas_call x1, Pallas kernels, local(): pl.pallas_call(functools.partial(encode_kernel, owners, streams, width, h...  4.59 us
    ppermute x7, starting transfers between devices, cross(): return lax.ppermute(x, 'mod', [(i, i ^ distance) for i in range(owners)])  4.2 us
    ppermute x7, waiting for transfers between devices, cross(): return lax.ppermute(x, 'mod', [(i, i ^ distance) for i in range(owners)])  4.13 us
    pallas_call x1, Pallas kernels, local(): pl.pallas_call(stem_kernel, name='stem', out_shape=(pltpu.VMEM((2, hit_ro...  3.15 us
    pallas_call x1, Pallas kernels, local(): pl.pallas_call(pack_kernel, name='pack', out_shape=(half, half), in_specs...  1.16 us
    pallas_call x1, Pallas kernels, local(): pl.pallas_call(functools.partial(prepare_kernel, width), name='prepare',...  0.7 us
    ppermute x3, waiting for transfers between devices, local(): got[k] = lax.ppermute(got[k ^ low], 'stream', pairs)  0.68 us
  transfers between devices with their start and end apart: 10, of which 6 were waited for; matrix products, arithmetic and copies ran while one was open for 0% of the time, Pallas kernels for 15%

profile of v6, /device:TPU:0, one launch (start us, length us, event | category | flops | bytes accessed | tf_op | source)
XLA Modules:
  0.0 25.5 jit_solution(5459508356012305595)
XLA Ops:
  0.6 0.0 copy-start.4
  0.6 1.2 %pack.1 = (bf16[608,128]{1,0:T(8,128)(2,1)S(1)}, bf16[608,128]{1,0:T(8,128)(2,1)S(1)}) custom-call(bf16[24,384]{1,0:T(8,128)(2,1)} %bitcast.18, bf16[24,384]{1,0:T(8,128)(2,1)} %bitcast.19, bf16[128,512]{1,0:T(8,128)(2,1)} %bitcast.16, bf16[512,128]{1,0:T(8,128)(2,1)} %bitcast.17), custom_call_target="tpu_custom_call" | custom-call | flops 5000000000 | bytes 3000000 | tf_op jit(solution)/shard_map/pack/pallas_call | solution.py:352
  1.8 4.1 %collective-permute-start.6 = (bf16[608,128]{1,0:T(8,128)(2,1)S(1)}, bf16[608,128]{1,0:T(8,128)(2,1)S(1)}, u32[]{:S(2)}, u32[]{:S(2)}) collective-permute-start(bf16[608,128]{1,0:T(8,128)(2,1)S(1)} %get-tuple-element.17.refs_10_), channel_id=1, source_target_pairs={{0,16},{8,24},{16,0},{24,8},{1,17},{9,25},{17,1},{25,9},{2,18},{10... | collective-permute-start | bytes 466952 | tf_op jit(solution)/shard_map/ppermute | solution.py:374
  5.9 1.6 %collective-permute-start.3 = (bf16[608,128]{1,0:T(8,128)(2,1)S(1)}, bf16[608,128]{1,0:T(8,128)(2,1)S(1)}, u32[]{:S(2)}, u32[]{:S(2)}) collective-permute-start(bf16[608,128]{1,0:T(8,128)(2,1)S(1)} %get-tuple-element.17.refs_10_), channel_id=1, source_target_pairs={{0,8},{8,0},{16,24},{24,16},{1,9},{9,1},{17,25},{25,17},{2,10},{10... | collective-permute-start | bytes 466952 | tf_op jit(solution)/shard_map/ppermute | solution.py:374
  7.5 0.0 copy-done.4
  7.5 3.2 %stem.1 = (bf16[2,160,128]{2,1,0:T(8,128)(2,1)S(1)}, bf16[2,160,128]{2,1,0:T(8,128)(2,1)S(1)}, bf16[2,160,128]{2,1,0:T(8,128)(2,1)S(1)}, bf16[2,160,128]{2,1,0:T(8,128)(2,1)S(1)}) custom-call(bf16[192,16,384]{2,1,0:T(8,128)(2,1)S(1)} %bitcast.15, bf16[256,128]{1,0:T(8,128)(2,1)} %weight.1, f32[8,128]{1,0:T(8,128)} %veto_weight.1, s32[1,48]{1,0:T(1,128)} %hit_frames.1), custom_call_target="tpu_custom_call" | custom-call | flops 5000000000 | bytes 3000000 | tf_op jit(solution)/shard_map/stem/pallas_call | solution.py:376
  10.7 0.0 copy-start
  10.7 0.0 copy-start.1
  10.7 0.0 copy-start.2
  10.7 0.0 copy-start.3
  10.7 2.5 %collective-permute-start = (bf16[2,160,128]{2,1,0:T(8,128)(2,1)S(1)}, bf16[2,160,128]{2,1,0:T(8,128)(2,1)S(1)}, u32[]{:S(2)}, u32[]{:S(2)}) collective-permute-start(bf16[2,160,128]{2,1,0:T(8,128)(2,1)S(1)} %get-tuple-element.13), channel_id=1, source_target_pairs={{0,6},{1,7},{2,4},{3,5},{4,2},{5,3},{6,0},{7,1},{8,14},{9,15},{10,... | collective-permute-start | bytes 245768 | tf_op jit(solution)/shard_map/ppermute | solution.py:368
  13.2 0.5 %collective-permute-start.1 = (bf16[2,160,128]{2,1,0:T(8,128)(2,1)S(1)}, bf16[2,160,128]{2,1,0:T(8,128)(2,1)S(1)}, u32[]{:S(2)}, u32[]{:S(2)}) collective-permute-start(bf16[2,160,128]{2,1,0:T(8,128)(2,1)S(1)} %get-tuple-element.14), channel_id=1, source_target_pairs={{0,4},{1,5},{2,6},{3,7},{4,0},{5,1},{6,2},{7,3},{8,12},{9,13},{10,... | collective-permute-start | bytes 245768 | tf_op jit(solution)/shard_map/ppermute | solution.py:368
  13.7 0.6 %collective-permute-start.2 = (bf16[2,160,128]{2,1,0:T(8,128)(2,1)S(1)}, bf16[2,160,128]{2,1,0:T(8,128)(2,1)S(1)}, u32[]{:S(2)}, u32[]{:S(2)}) collective-permute-start(bf16[2,160,128]{2,1,0:T(8,128)(2,1)S(1)} %get-tuple-element.15), channel_id=1, source_target_pairs={{0,2},{1,3},{2,0},{3,1},{4,6},{5,7},{6,4},{7,5},{8,10},{9,11},{10,... | collective-permute-start | bytes 245768 | tf_op jit(solution)/shard_map/ppermute | solution.py:368
  14.3 0.0 collective-permute-done.6.refs_14_
  14.3 0.4 %collective-permute-start.8 = (bf16[608,128]{1,0:T(8,128)(2,1)S(1)}, bf16[608,128]{1,0:T(8,128)(2,1)S(1)}, u32[]{:S(2)}, u32[]{:S(2)}) collective-permute-start(bf16[608,128]{1,0:T(8,128)(2,1)S(1)} %collective-permute-done.6.refs_14_), channel_id=1, source_target_pairs={{0,8},{8,0},{16,24},{24,16},{1,9},{9,1},{17,25},{25,17},{2,10},{10... | collective-permute-start | bytes 466952 | tf_op jit(solution)/shard_map/ppermute | solution.py:374
  14.7 1.6 %collective-permute-done.refs_0_ = bf16[2,160,128]{2,1,0:T(8,128)(2,1)S(1)} collective-permute-done((bf16[2,160,128]{2,1,0:T(8,128)(2,1)S(1)}, bf16[2,160,128]{2,1,0:T(8,128)(2,1)S(1)}, u32[]{:S(2)}, u32[]{:S(2)}) %collective-permute-start) | collective-permute-done | bytes 81952 | tf_op jit(solution)/shard_map/ppermute | solution.py:368
  16.3 1.4 %collective-permute-done.1.refs_1_ = bf16[2,160,128]{2,1,0:T(8,128)(2,1)S(1)} collective-permute-done((bf16[2,160,128]{2,1,0:T(8,128)(2,1)S(1)}, bf16[2,160,128]{2,1,0:T(8,128)(2,1)S(1)}, u32[]{:S(2)}, u32[]{:S(2)}) %collective-permute-start.1) | collective-permute-done | bytes 81952 | tf_op jit(solution)/shard_map/ppermute | solution.py:368
  17.7 0.5 %collective-permute-done.2.refs_2_ = bf16[2,160,128]{2,1,0:T(8,128)(2,1)S(1)} collective-permute-done((bf16[2,160,128]{2,1,0:T(8,128)(2,1)S(1)}, bf16[2,160,128]{2,1,0:T(8,128)(2,1)S(1)}, u32[]{:S(2)}, u32[]{:S(2)}) %collective-permute-start.2) | collective-permute-done | bytes 81952 | tf_op jit(solution)/shard_map/ppermute | solution.py:368
  18.1 0.0 collective-permute-done.3.refs_4_.refs_12_
  18.2 0.1 collective-permute-start.4
  18.2 0.5 %collective-permute-start.7 = (bf16[608,128]{1,0:T(8,128)(2,1)S(1)}, bf16[608,128]{1,0:T(8,128)(2,1)S(1)}, u32[]{:S(2)}, u32[]{:S(2)}) collective-permute-start(bf16[608,128]{1,0:T(8,128)(2,1)S(1)} %collective-permute-done.6.refs_14_), channel_id=1, source_target_pairs={{0,1},{1,0},{2,3},{3,2},{4,5},{5,4},{6,7},{7,6},{8,9},{9,8},{10,11... | collective-permute-start | bytes 466952 | tf_op jit(solution)/shard_map/ppermute | solution.py:368
  18.7 0.1 collective-permute-start.5
  18.8 0.7 %collective-permute-done.8.refs_16_ = bf16[608,128]{1,0:T(8,128)(2,1)S(1)} collective-permute-done((bf16[608,128]{1,0:T(8,128)(2,1)S(1)}, bf16[608,128]{1,0:T(8,128)(2,1)S(1)}, u32[]{:S(2)}, u32[]{:S(2)}) %collective-permute-start.8) | collective-permute-done | bytes 155680 | tf_op jit(solution)/shard_map/ppermute | solution.py:374
  19.5 0.0 collective-permute-start.9
  19.5 0.1 collective-permute-done.4.refs_4_
  19.6 0.7 %prepare.1 = (bf16[6,32,1024]{2,1,0:T(8,128)(2,1)S(1)}, f32[1,24]{1,0:T(1,128)}) custom-call(bf16[2,160,128]{2,1,0:T(8,128)(2,1)S(1)} %collective-permute-done.refs_0_, bf16[2,160,128]{2,1,0:T(8,128)(2,1)S(1)} %collective-permute-done.1.refs_1_, bf16[2,160,128]{2,1,0:T(8,128)(2,1)S(1)} %collective-permute-done.2.refs_2_, ...), custom_call_target="tpu_custom_call" | custom-call | tf_op jit(solution)/shard_map/prepare/pallas_call | solution.py:410
  20.3 0.0 collective-permute-done.7.refs_15_
  20.3 0.0 collective-permute-done.5.refs_13_
  20.3 0.5 %collective-permute-done.9.refs_17_ = bf16[608,128]{1,0:T(8,128)(2,1)S(1)} collective-permute-done((bf16[608,128]{1,0:T(8,128)(2,1)S(1)}, bf16[608,128]{1,0:T(8,128)(2,1)S(1)}, u32[]{:S(2)}, u32[]{:S(2)}) %collective-permute-start.9) | collective-permute-done | bytes 155680 | tf_op jit(solution)/shard_map/ppermute | solution.py:368
  20.9 0.0 copy-done
  20.9 0.0 copy-done.1
  20.9 4.6 %encode.1 = (f32[6,1,128]{2,1,0:T(1,128)}, f32[6,1,8]{2,1,0:T(1,128)}) custom-call(bf16[2,160,128]{2,1,0:T(8,128)(2,1)S(1)} %collective-permute-done.refs_0_, bf16[2,160,128]{2,1,0:T(8,128)(2,1)S(1)} %collective-permute-done.1.refs_1_, bf16[2,160,128]{2,1,0:T(8,128)(2,1)S(1)} %collective-permute-done.2.refs_2_, ...), custom_call_target="tpu_custom_call" | custom-call | tf_op jit(solution)/shard_map/encode/pallas_call | solution.py:421
  (3 shorter events, 0.0 us)
Async XLA Ops:
  0.6 6.9 %copy-start.4 = (bf16[1,192,16,384]{3,2,1,0:T(8,128)(2,1)S(1)}, bf16[1,192,16,384]{3,2,1,0:T(8,128)(2,1)}, u32[]{:S(2)}) copy-start(bf16[1,192,16,384]{3,2,1,0:T(8,128)(2,1)} %param.12) | copy-start | bytes 7077892
  1.8 12.4 %collective-permute-start.6 = (bf16[608,128]{1,0:T(8,128)(2,1)S(1)}, bf16[608,128]{1,0:T(8,128)(2,1)S(1)}, u32[]{:S(2)}, u32[]{:S(2)}) collective-permute-start(bf16[608,128]{1,0:T(8,128)(2,1)S(1)} %get-tuple-element.17.refs_10_), channel_id=1, source_target_pairs={{0,16},{8,24},{16,0},{24,8},{1,17},{9,25},{17,1},{25,9},{2,18},{10... | collective-permute-start | bytes 466952 | tf_op jit(solution)/shard_map/ppermute | solution.py:374
  5.9 12.2 %collective-permute-start.3 = (bf16[608,128]{1,0:T(8,128)(2,1)S(1)}, bf16[608,128]{1,0:T(8,128)(2,1)S(1)}, u32[]{:S(2)}, u32[]{:S(2)}) collective-permute-start(bf16[608,128]{1,0:T(8,128)(2,1)S(1)} %get-tuple-element.17.refs_10_), channel_id=1, source_target_pairs={{0,8},{8,0},{16,24},{24,16},{1,9},{9,1},{17,25},{25,17},{2,10},{10... | collective-permute-start | bytes 466952 | tf_op jit(solution)/shard_map/ppermute | solution.py:374
  10.7 10.2 %copy-start = (bf16[1024,128]{1,0:T(8,128)(2,1)S(1)}, bf16[1024,128]{1,0:T(8,128)(2,1)}, u32[]{:S(2)}) copy-start(bf16[1024,128]{1,0:T(8,128)(2,1)} %refs_7_.1) | copy-start | bytes 786436
  10.7 10.2 %copy-start.1 = (f32[128,8]{0,1:T(8,128)S(1)}, f32[128,8]{0,1:T(8,128)}, u32[]{:S(2)}) copy-start(f32[128,8]{0,1:T(8,128)} %param.23) | copy-start | bytes 12292
  10.7 10.2 %copy-start.2 = (s32[1,48,1]{1,2,0:T(1,128)S(1)}, s32[1,48,1]{1,2,0:T(1,128)}, u32[]{:S(2)}) copy-start(s32[1,48,1]{1,2,0:T(1,128)} %param.16) | copy-start | bytes 580
  10.7 10.2 %copy-start.3 = (f32[128]{0:T(128)S(1)}, f32[128]{0:T(128)}, u32[]{:S(2)}) copy-start(f32[128]{0:T(128)} %param.22) | copy-start | bytes 1540
  10.7 5.6 %collective-permute-start = (bf16[2,160,128]{2,1,0:T(8,128)(2,1)S(1)}, bf16[2,160,128]{2,1,0:T(8,128)(2,1)S(1)}, u32[]{:S(2)}, u32[]{:S(2)}) collective-permute-start(bf16[2,160,128]{2,1,0:T(8,128)(2,1)S(1)} %get-tuple-element.13), channel_id=1, source_target_pairs={{0,6},{1,7},{2,4},{3,5},{4,2},{5,3},{6,0},{7,1},{8,14},{9,15},{10,... | collective-permute-start | bytes 245768 | tf_op jit(solution)/shard_map/ppermute | solution.py:368
  13.2 4.4 %collective-permute-start.1 = (bf16[2,160,128]{2,1,0:T(8,128)(2,1)S(1)}, bf16[2,160,128]{2,1,0:T(8,128)(2,1)S(1)}, u32[]{:S(2)}, u32[]{:S(2)}) collective-permute-start(bf16[2,160,128]{2,1,0:T(8,128)(2,1)S(1)} %get-tuple-element.14), channel_id=1, source_target_pairs={{0,4},{1,5},{2,6},{3,7},{4,0},{5,1},{6,2},{7,3},{8,12},{9,13},{10,... | collective-permute-start | bytes 245768 | tf_op jit(solution)/shard_map/ppermute | solution.py:368
  13.7 4.4 %collective-permute-start.2 = (bf16[2,160,128]{2,1,0:T(8,128)(2,1)S(1)}, bf16[2,160,128]{2,1,0:T(8,128)(2,1)S(1)}, u32[]{:S(2)}, u32[]{:S(2)}) collective-permute-start(bf16[2,160,128]{2,1,0:T(8,128)(2,1)S(1)} %get-tuple-element.15), channel_id=1, source_target_pairs={{0,2},{1,3},{2,0},{3,1},{4,6},{5,7},{6,4},{7,5},{8,10},{9,11},{10,... | collective-permute-start | bytes 245768 | tf_op jit(solution)/shard_map/ppermute | solution.py:368
  14.3 5.2 %collective-permute-start.8 = (bf16[608,128]{1,0:T(8,128)(2,1)S(1)}, bf16[608,128]{1,0:T(8,128)(2,1)S(1)}, u32[]{:S(2)}, u32[]{:S(2)}) collective-permute-start(bf16[608,128]{1,0:T(8,128)(2,1)S(1)} %collective-permute-done.6.refs_14_), channel_id=1, source_target_pairs={{0,8},{8,0},{16,24},{24,16},{1,9},{9,1},{17,25},{25,17},{2,10},{10... | collective-permute-start | bytes 466952 | tf_op jit(solution)/shard_map/ppermute | solution.py:374
  18.2 1.5 %collective-permute-start.4 = (bf16[640,128]{1,0:T(8,128)(2,1)S(1)}, bf16[640,128]{1,0:T(8,128)(2,1)S(1)}, u32[]{:S(2)}, u32[]{:S(2)}) collective-permute-start(bf16[640,128]{1,0:T(8,128)(2,1)S(1)} %bundle.1), channel_id=1, source_target_pairs={{0,1},{1,0},{2,3},{3,2},{4,5},{5,4},{6,7},{7,6},{8,9},{9,8},{10,11... | collective-permute-start | bytes 491528 | tf_op jit(solution)/shard_map/ppermute | solution.py:368
  18.2 2.1 %collective-permute-start.7 = (bf16[608,128]{1,0:T(8,128)(2,1)S(1)}, bf16[608,128]{1,0:T(8,128)(2,1)S(1)}, u32[]{:S(2)}, u32[]{:S(2)}) collective-permute-start(bf16[608,128]{1,0:T(8,128)(2,1)S(1)} %collective-permute-done.6.refs_14_), channel_id=1, source_target_pairs={{0,1},{1,0},{2,3},{3,2},{4,5},{5,4},{6,7},{7,6},{8,9},{9,8},{10,11... | collective-permute-start | bytes 466952 | tf_op jit(solution)/shard_map/ppermute | solution.py:368
  18.7 1.6 %collective-permute-start.5 = (bf16[608,128]{1,0:T(8,128)(2,1)S(1)}, bf16[608,128]{1,0:T(8,128)(2,1)S(1)}, u32[]{:S(2)}, u32[]{:S(2)}) collective-permute-start(bf16[608,128]{1,0:T(8,128)(2,1)S(1)} %collective-permute-done.3.refs_4_.refs_12_), channel_id=1, source_target_pairs={{0,1},{1,0},{2,3},{3,2},{4,5},{5,4},{6,7},{7,6},{8,9},{9,8},{10,11... | collective-permute-start | bytes 466952 | tf_op jit(solution)/shard_map/ppermute | solution.py:368
  19.5 1.4 %collective-permute-start.9 = (bf16[608,128]{1,0:T(8,128)(2,1)S(1)}, bf16[608,128]{1,0:T(8,128)(2,1)S(1)}, u32[]{:S(2)}, u32[]{:S(2)}) collective-permute-start(bf16[608,128]{1,0:T(8,128)(2,1)S(1)} %collective-permute-done.8.refs_16_), channel_id=1, source_target_pairs={{0,1},{1,0},{2,3},{3,2},{4,5},{5,4},{6,7},{7,6},{8,9},{9,8},{10,11... | collective-permute-start | bytes 466952 | tf_op jit(solution)/shard_map/ppermute | solution.py:368

commit v7 on v6

--- a/solution.py
+++ b/solution.py
@@ -38,6 +38,15 @@
 
 def dot(a, b):
     return jnp.dot(a, b, preferred_element_type=F32)
+
+
+def dot_rows(a, b):
+    return lax.dot_general(a, b, (((1,), (1,)), ((), ())), preferred_element_type=F32)
+
+
+def split(x):
+    top = x.astype(BF16)
+    return top, (x - top.astype(F32)).astype(BF16)
 
 
 def iota(shape, axis):
@@ -180,18 +189,14 @@
     scale = jnp.broadcast_to(veto_rows[pl.ds(lax.axis_index("mod"), 1), :] / (2 * tokens), (VETO_ROWS, channels))
     row = iota((VETO_ROWS, owned), 0)
     totals[...] = sums
+    scale_top, scale_low = split(scale)
     for k in range(owners // 2):
         for core in range(2):
             o = ((lax.axis_index("mod") // 2) ^ k) * 2 + core
             taken = 0.5 * chosen[pl.ds(pl.multiple_of(o * hit_rows, 8), hit_rows), :]
             out[k][core, 0:hit_rows, :] = taken.astype(BF16)
-            veto = lax.dot_general(
-                scale,
-                totals[pl.ds(pl.multiple_of(o * owned, 8), owned), :],
-                (((1,), (1,)), ((), ())),
-                preferred_element_type=F32,
-                precision=lax.Precision.HIGHEST,
-            )
+            top, low = split(totals[pl.ds(pl.multiple_of(o * owned, 8), owned), :])
+            veto = dot_rows(scale_top, top) + (dot_rows(scale_top, low) + dot_rows(scale_low, top))
             high = veto.astype(BF16).astype(F32)
             both = jnp.where(row == 0, high, jnp.where(row == 1, veto - high, 0.0))
             both = jnp.concatenate([both, jnp.zeros((VETO_ROWS, LANES - owned), F32)], axis=1)
@@ -233,8 +238,7 @@
     own = lax.axis_index("mod")
     core = own % 2
 
-    @pl.loop(0, hits)
-    def _(slot):
+    for slot in range(hits):
         wanted = targets[own * hits + slot] ^ here
         for k in range(streams):
 

time: 25.6 us -> 25.5 us (level)
  no operation moved by 1% of the time
where the time goes in v7:
time: 25.5 us; the launch traced here: 25.4 us
  starting transfers between devices  10.3 us (40%)
  Pallas kernels  9.48 us (37%)
  waiting for transfers between devices  4.78 us (19%)
  between operations  0.72 us (3%)
    ppermute x3, starting transfers between devices, local(): got[k] = lax.ppermute(got[k ^ low], 'stream', pairs)  6.13 us
    pallas_call x1, Pallas kernels, local(): pl.pallas_call(functools.partial(encode_kernel, owners, streams, width, h...  4.54 us
    ppermute x7, starting transfers between devices, cross(): return lax.ppermute(x, 'mod', [(i, i ^ distance) for i in range(owners)])  4.2 us
    ppermute x7, waiting for transfers between devices, cross(): return lax.ppermute(x, 'mod', [(i, i ^ distance) for i in range(owners)])  4.13 us
    pallas_call x1, Pallas kernels, local(): pl.pallas_call(stem_kernel, name='stem', out_shape=(pltpu.VMEM((2, hit_ro...  3.07 us
    pallas_call x1, Pallas kernels, local(): pl.pallas_call(pack_kernel, name='pack', out_shape=(half, half), in_specs...  1.16 us
    pallas_call x1, Pallas kernels, local(): pl.pallas_call(functools.partial(prepare_kernel, width), name='prepare',...  0.7 us
    ppermute x3, waiting for transfers between devices, local(): got[k] = lax.ppermute(got[k ^ low], 'stream', pairs)  0.65 us
  transfers between devices with their start and end apart: 10, of which 6 were waited for; matrix products, arithmetic and copies ran while one was open for 0% of the time, Pallas kernels for 15%

profile of v7, /device:TPU:0, one launch (start us, length us, event | category | flops | bytes accessed | tf_op | source)
XLA Modules:
  0.0 25.4 jit_solution(7868883071973810040)
XLA Ops:
  0.6 0.0 copy-start.4
  0.6 1.2 %pack.1 = (bf16[608,128]{1,0:T(8,128)(2,1)S(1)}, bf16[608,128]{1,0:T(8,128)(2,1)S(1)}) custom-call(bf16[24,384]{1,0:T(8,128)(2,1)} %bitcast.18, bf16[24,384]{1,0:T(8,128)(2,1)} %bitcast.19, bf16[128,512]{1,0:T(8,128)(2,1)} %bitcast.16, bf16[512,128]{1,0:T(8,128)(2,1)} %bitcast.17), custom_call_target="tpu_custom_call" | custom-call | flops 5000000000 | bytes 3000000 | tf_op jit(solution)/shard_map/pack/pallas_call | solution.py:356
  1.8 4.1 %collective-permute-start.6 = (bf16[608,128]{1,0:T(8,128)(2,1)S(1)}, bf16[608,128]{1,0:T(8,128)(2,1)S(1)}, u32[]{:S(2)}, u32[]{:S(2)}) collective-permute-start(bf16[608,128]{1,0:T(8,128)(2,1)S(1)} %get-tuple-element.17.refs_10_), channel_id=1, source_target_pairs={{0,16},{8,24},{16,0},{24,8},{1,17},{9,25},{17,1},{25,9},{2,18},{10... | collective-permute-start | bytes 466952 | tf_op jit(solution)/shard_map/ppermute | solution.py:378
  5.9 1.6 %collective-permute-start.3 = (bf16[608,128]{1,0:T(8,128)(2,1)S(1)}, bf16[608,128]{1,0:T(8,128)(2,1)S(1)}, u32[]{:S(2)}, u32[]{:S(2)}) collective-permute-start(bf16[608,128]{1,0:T(8,128)(2,1)S(1)} %get-tuple-element.17.refs_10_), channel_id=1, source_target_pairs={{0,8},{8,0},{16,24},{24,16},{1,9},{9,1},{17,25},{25,17},{2,10},{10... | collective-permute-start | bytes 466952 | tf_op jit(solution)/shard_map/ppermute | solution.py:378
  7.5 0.0 copy-done.4
  7.5 3.1 %stem.1 = (bf16[2,160,128]{2,1,0:T(8,128)(2,1)S(1)}, bf16[2,160,128]{2,1,0:T(8,128)(2,1)S(1)}, bf16[2,160,128]{2,1,0:T(8,128)(2,1)S(1)}, bf16[2,160,128]{2,1,0:T(8,128)(2,1)S(1)}) custom-call(bf16[192,16,384]{2,1,0:T(8,128)(2,1)S(1)} %bitcast.15, bf16[256,128]{1,0:T(8,128)(2,1)} %weight.1, f32[8,128]{1,0:T(8,128)} %veto_weight.1, s32[1,48]{1,0:T(1,128)} %hit_frames.1), custom_call_target="tpu_custom_call" | custom-call | flops 5000000000 | bytes 3000000 | tf_op jit(solution)/shard_map/stem/pallas_call | solution.py:380
  10.6 0.0 copy-start
  10.6 0.0 copy-start.1
  10.6 0.0 copy-start.2
  10.6 0.0 copy-start.3
  10.6 2.5 %collective-permute-start = (bf16[2,160,128]{2,1,0:T(8,128)(2,1)S(1)}, bf16[2,160,128]{2,1,0:T(8,128)(2,1)S(1)}, u32[]{:S(2)}, u32[]{:S(2)}) collective-permute-start(bf16[2,160,128]{2,1,0:T(8,128)(2,1)S(1)} %get-tuple-element.13), channel_id=1, source_target_pairs={{0,6},{1,7},{2,4},{3,5},{4,2},{5,3},{6,0},{7,1},{8,14},{9,15},{10,... | collective-permute-start | bytes 245768 | tf_op jit(solution)/shard_map/ppermute | solution.py:372
  13.1 0.5 %collective-permute-start.1 = (bf16[2,160,128]{2,1,0:T(8,128)(2,1)S(1)}, bf16[2,160,128]{2,1,0:T(8,128)(2,1)S(1)}, u32[]{:S(2)}, u32[]{:S(2)}) collective-permute-start(bf16[2,160,128]{2,1,0:T(8,128)(2,1)S(1)} %get-tuple-element.14), channel_id=1, source_target_pairs={{0,4},{1,5},{2,6},{3,7},{4,0},{5,1},{6,2},{7,3},{8,12},{9,13},{10,... | collective-permute-start | bytes 245768 | tf_op jit(solution)/shard_map/ppermute | solution.py:372
  13.6 0.5 %collective-permute-start.2 = (bf16[2,160,128]{2,1,0:T(8,128)(2,1)S(1)}, bf16[2,160,128]{2,1,0:T(8,128)(2,1)S(1)}, u32[]{:S(2)}, u32[]{:S(2)}) collective-permute-start(bf16[2,160,128]{2,1,0:T(8,128)(2,1)S(1)} %get-tuple-element.15), channel_id=1, source_target_pairs={{0,2},{1,3},{2,0},{3,1},{4,6},{5,7},{6,4},{7,5},{8,10},{9,11},{10,... | collective-permute-start | bytes 245768 | tf_op jit(solution)/shard_map/ppermute | solution.py:372
  14.2 0.0 collective-permute-done.6.refs_14_
  14.2 0.5 %collective-permute-start.8 = (bf16[608,128]{1,0:T(8,128)(2,1)S(1)}, bf16[608,128]{1,0:T(8,128)(2,1)S(1)}, u32[]{:S(2)}, u32[]{:S(2)}) collective-permute-start(bf16[608,128]{1,0:T(8,128)(2,1)S(1)} %collective-permute-done.6.refs_14_), channel_id=1, source_target_pairs={{0,8},{8,0},{16,24},{24,16},{1,9},{9,1},{17,25},{25,17},{2,10},{10... | collective-permute-start | bytes 466952 | tf_op jit(solution)/shard_map/ppermute | solution.py:378
  14.6 1.5 %collective-permute-done.refs_0_ = bf16[2,160,128]{2,1,0:T(8,128)(2,1)S(1)} collective-permute-done((bf16[2,160,128]{2,1,0:T(8,128)(2,1)S(1)}, bf16[2,160,128]{2,1,0:T(8,128)(2,1)S(1)}, u32[]{:S(2)}, u32[]{:S(2)}) %collective-permute-start) | collective-permute-done | bytes 81952 | tf_op jit(solution)/shard_map/ppermute | solution.py:372
  16.2 1.4 %collective-permute-done.1.refs_1_ = bf16[2,160,128]{2,1,0:T(8,128)(2,1)S(1)} collective-permute-done((bf16[2,160,128]{2,1,0:T(8,128)(2,1)S(1)}, bf16[2,160,128]{2,1,0:T(8,128)(2,1)S(1)}, u32[]{:S(2)}, u32[]{:S(2)}) %collective-permute-start.1) | collective-permute-done | bytes 81952 | tf_op jit(solution)/shard_map/ppermute | solution.py:372
  17.6 0.5 %collective-permute-done.2.refs_2_ = bf16[2,160,128]{2,1,0:T(8,128)(2,1)S(1)} collective-permute-done((bf16[2,160,128]{2,1,0:T(8,128)(2,1)S(1)}, bf16[2,160,128]{2,1,0:T(8,128)(2,1)S(1)}, u32[]{:S(2)}, u32[]{:S(2)}) %collective-permute-start.2) | collective-permute-done | bytes 81952 | tf_op jit(solution)/shard_map/ppermute | solution.py:372
  18.1 0.0 collective-permute-done.3.refs_4_.refs_12_
  18.1 0.1 collective-permute-start.4
  18.2 0.5 %collective-permute-start.7 = (bf16[608,128]{1,0:T(8,128)(2,1)S(1)}, bf16[608,128]{1,0:T(8,128)(2,1)S(1)}, u32[]{:S(2)}, u32[]{:S(2)}) collective-permute-start(bf16[608,128]{1,0:T(8,128)(2,1)S(1)} %collective-permute-done.6.refs_14_), channel_id=1, source_target_pairs={{0,1},{1,0},{2,3},{3,2},{4,5},{5,4},{6,7},{7,6},{8,9},{9,8},{10,11... | collective-permute-start | bytes 466952 | tf_op jit(solution)/shard_map/ppermute | solution.py:372
  18.7 0.1 collective-permute-start.5
  18.8 0.6 %collective-permute-done.8.refs_16_ = bf16[608,128]{1,0:T(8,128)(2,1)S(1)} collective-permute-done((bf16[608,128]{1,0:T(8,128)(2,1)S(1)}, bf16[608,128]{1,0:T(8,128)(2,1)S(1)}, u32[]{:S(2)}, u32[]{:S(2)}) %collective-permute-start.8) | collective-permute-done | bytes 155680 | tf_op jit(solution)/shard_map/ppermute | solution.py:378
  19.4 0.0 collective-permute-start.9
  19.4 0.2 collective-permute-done.4.refs_4_
  19.6 0.7 %prepare.1 = (bf16[6,32,1024]{2,1,0:T(8,128)(2,1)S(1)}, f32[1,24]{1,0:T(1,128)}) custom-call(bf16[2,160,128]{2,1,0:T(8,128)(2,1)S(1)} %collective-permute-done.refs_0_, bf16[2,160,128]{2,1,0:T(8,128)(2,1)S(1)} %collective-permute-done.1.refs_1_, bf16[2,160,128]{2,1,0:T(8,128)(2,1)S(1)} %collective-permute-done.2.refs_2_, ...), custom_call_target="tpu_custom_call" | custom-call | tf_op jit(solution)/shard_map/prepare/pallas_call | solution.py:414
  20.3 0.0 collective-permute-done.7.refs_15_
  20.3 0.0 collective-permute-done.5.refs_13_
  20.3 0.5 %collective-permute-done.9.refs_17_ = bf16[608,128]{1,0:T(8,128)(2,1)S(1)} collective-permute-done((bf16[608,128]{1,0:T(8,128)(2,1)S(1)}, bf16[608,128]{1,0:T(8,128)(2,1)S(1)}, u32[]{:S(2)}, u32[]{:S(2)}) %collective-permute-start.9) | collective-permute-done | bytes 155680 | tf_op jit(solution)/shard_map/ppermute | solution.py:372
  20.8 0.0 copy-done
  20.8 0.0 copy-done.1
  20.8 4.5 %encode.1 = (f32[6,1,128]{2,1,0:T(1,128)}, f32[6,1,8]{2,1,0:T(1,128)}) custom-call(bf16[2,160,128]{2,1,0:T(8,128)(2,1)S(1)} %collective-permute-done.refs_0_, bf16[2,160,128]{2,1,0:T(8,128)(2,1)S(1)} %collective-permute-done.1.refs_1_, bf16[2,160,128]{2,1,0:T(8,128)(2,1)S(1)} %collective-permute-done.2.refs_2_, ...), custom_call_target="tpu_custom_call" | custom-call | tf_op jit(solution)/shard_map/encode/pallas_call | solution.py:425
  (3 shorter events, 0.0 us)
Async XLA Ops:
  0.6 6.9 %copy-start.4 = (bf16[1,192,16,384]{3,2,1,0:T(8,128)(2,1)S(1)}, bf16[1,192,16,384]{3,2,1,0:T(8,128)(2,1)}, u32[]{:S(2)}) copy-start(bf16[1,192,16,384]{3,2,1,0:T(8,128)(2,1)} %param.12) | copy-start | bytes 7077892
  1.8 12.4 %collective-permute-start.6 = (bf16[608,128]{1,0:T(8,128)(2,1)S(1)}, bf16[608,128]{1,0:T(8,128)(2,1)S(1)}, u32[]{:S(2)}, u32[]{:S(2)}) collective-permute-start(bf16[608,128]{1,0:T(8,128)(2,1)S(1)} %get-tuple-element.17.refs_10_), channel_id=1, source_target_pairs={{0,16},{8,24},{16,0},{24,8},{1,17},{9,25},{17,1},{25,9},{2,18},{10... | collective-permute-start | bytes 466952 | tf_op jit(solution)/shard_map/ppermute | solution.py:378
  5.9 12.2 %collective-permute-start.3 = (bf16[608,128]{1,0:T(8,128)(2,1)S(1)}, bf16[608,128]{1,0:T(8,128)(2,1)S(1)}, u32[]{:S(2)}, u32[]{:S(2)}) collective-permute-start(bf16[608,128]{1,0:T(8,128)(2,1)S(1)} %get-tuple-element.17.refs_10_), channel_id=1, source_target_pairs={{0,8},{8,0},{16,24},{24,16},{1,9},{9,1},{17,25},{25,17},{2,10},{10... | collective-permute-start | bytes 466952 | tf_op jit(solution)/shard_map/ppermute | solution.py:378
  10.6 10.2 %copy-start = (bf16[1024,128]{1,0:T(8,128)(2,1)S(1)}, bf16[1024,128]{1,0:T(8,128)(2,1)}, u32[]{:S(2)}) copy-start(bf16[1024,128]{1,0:T(8,128)(2,1)} %refs_7_.1) | copy-start | bytes 786436
  10.6 10.2 %copy-start.1 = (f32[128,8]{0,1:T(8,128)S(1)}, f32[128,8]{0,1:T(8,128)}, u32[]{:S(2)}) copy-start(f32[128,8]{0,1:T(8,128)} %param.23) | copy-start | bytes 12292
  10.6 10.2 %copy-start.2 = (s32[1,48,1]{1,2,0:T(1,128)S(1)}, s32[1,48,1]{1,2,0:T(1,128)}, u32[]{:S(2)}) copy-start(s32[1,48,1]{1,2,0:T(1,128)} %param.16) | copy-start | bytes 580
  10.6 10.2 %copy-start.3 = (f32[128]{0:T(128)S(1)}, f32[128]{0:T(128)}, u32[]{:S(2)}) copy-start(f32[128]{0:T(128)} %param.22) | copy-start | bytes 1540
  10.6 5.6 %collective-permute-start = (bf16[2,160,128]{2,1,0:T(8,128)(2,1)S(1)}, bf16[2,160,128]{2,1,0:T(8,128)(2,1)S(1)}, u32[]{:S(2)}, u32[]{:S(2)}) collective-permute-start(bf16[2,160,128]{2,1,0:T(8,128)(2,1)S(1)} %get-tuple-element.13), channel_id=1, source_target_pairs={{0,6},{1,7},{2,4},{3,5},{4,2},{5,3},{6,0},{7,1},{8,14},{9,15},{10,... | collective-permute-start | bytes 245768 | tf_op jit(solution)/shard_map/ppermute | solution.py:372
  13.1 4.4 %collective-permute-start.1 = (bf16[2,160,128]{2,1,0:T(8,128)(2,1)S(1)}, bf16[2,160,128]{2,1,0:T(8,128)(2,1)S(1)}, u32[]{:S(2)}, u32[]{:S(2)}) collective-permute-start(bf16[2,160,128]{2,1,0:T(8,128)(2,1)S(1)} %get-tuple-element.14), channel_id=1, source_target_pairs={{0,4},{1,5},{2,6},{3,7},{4,0},{5,1},{6,2},{7,3},{8,12},{9,13},{10,... | collective-permute-start | bytes 245768 | tf_op jit(solution)/shard_map/ppermute | solution.py:372
  13.6 4.4 %collective-permute-start.2 = (bf16[2,160,128]{2,1,0:T(8,128)(2,1)S(1)}, bf16[2,160,128]{2,1,0:T(8,128)(2,1)S(1)}, u32[]{:S(2)}, u32[]{:S(2)}) collective-permute-start(bf16[2,160,128]{2,1,0:T(8,128)(2,1)S(1)} %get-tuple-element.15), channel_id=1, source_target_pairs={{0,2},{1,3},{2,0},{3,1},{4,6},{5,7},{6,4},{7,5},{8,10},{9,11},{10,... | collective-permute-start | bytes 245768 | tf_op jit(solution)/shard_map/ppermute | solution.py:372
  14.2 5.2 %collective-permute-start.8 = (bf16[608,128]{1,0:T(8,128)(2,1)S(1)}, bf16[608,128]{1,0:T(8,128)(2,1)S(1)}, u32[]{:S(2)}, u32[]{:S(2)}) collective-permute-start(bf16[608,128]{1,0:T(8,128)(2,1)S(1)} %collective-permute-done.6.refs_14_), channel_id=1, source_target_pairs={{0,8},{8,0},{16,24},{24,16},{1,9},{9,1},{17,25},{25,17},{2,10},{10... | collective-permute-start | bytes 466952 | tf_op jit(solution)/shard_map/ppermute | solution.py:378
  18.1 1.5 %collective-permute-start.4 = (bf16[640,128]{1,0:T(8,128)(2,1)S(1)}, bf16[640,128]{1,0:T(8,128)(2,1)S(1)}, u32[]{:S(2)}, u32[]{:S(2)}) collective-permute-start(bf16[640,128]{1,0:T(8,128)(2,1)S(1)} %bundle.1), channel_id=1, source_target_pairs={{0,1},{1,0},{2,3},{3,2},{4,5},{5,4},{6,7},{7,6},{8,9},{9,8},{10,11... | collective-permute-start | bytes 491528 | tf_op jit(solution)/shard_map/ppermute | solution.py:372
  18.2 2.1 %collective-permute-start.7 = (bf16[608,128]{1,0:T(8,128)(2,1)S(1)}, bf16[608,128]{1,0:T(8,128)(2,1)S(1)}, u32[]{:S(2)}, u32[]{:S(2)}) collective-permute-start(bf16[608,128]{1,0:T(8,128)(2,1)S(1)} %collective-permute-done.6.refs_14_), channel_id=1, source_target_pairs={{0,1},{1,0},{2,3},{3,2},{4,5},{5,4},{6,7},{7,6},{8,9},{9,8},{10,11... | collective-permute-start | bytes 466952 | tf_op jit(solution)/shard_map/ppermute | solution.py:372
  18.7 1.6 %collective-permute-start.5 = (bf16[608,128]{1,0:T(8,128)(2,1)S(1)}, bf16[608,128]{1,0:T(8,128)(2,1)S(1)}, u32[]{:S(2)}, u32[]{:S(2)}) collective-permute-start(bf16[608,128]{1,0:T(8,128)(2,1)S(1)} %collective-permute-done.3.refs_4_.refs_12_), channel_id=1, source_target_pairs={{0,1},{1,0},{2,3},{3,2},{4,5},{5,4},{6,7},{7,6},{8,9},{9,8},{10,11... | collective-permute-start | bytes 466952 | tf_op jit(solution)/shard_map/ppermute | solution.py:372
  19.4 1.4 %collective-permute-start.9 = (bf16[608,128]{1,0:T(8,128)(2,1)S(1)}, bf16[608,128]{1,0:T(8,128)(2,1)S(1)}, u32[]{:S(2)}, u32[]{:S(2)}) collective-permute-start(bf16[608,128]{1,0:T(8,128)(2,1)S(1)} %collective-permute-done.8.refs_16_), channel_id=1, source_target_pairs={{0,1},{1,0},{2,3},{3,2},{4,5},{5,4},{6,7},{7,6},{8,9},{9,8},{10,11... | collective-permute-start | bytes 466952 | tf_op jit(solution)/shard_map/ppermute | solution.py:372
